TPU v7x, 32 devices: a whole 2x2x4 slice. The times are simulated.
32 devices in a mesh: section: 8 (over z, y), dp: 4 (over x, core).
Axes of the slice: x: 2, y: 2, z: 4, core: 2. Of those that a mesh axis runs over, the one named last changes fastest.
Arguments:
- enc_state: bfloat16 [8, 128, 4096], P('section', 'dp'), may hold values from -1000 to 1000
- final_gain: float32 [4096], replicated, may hold values from 0.5 to 1.5
- queries: bfloat16 [8, 512, 4096], P('section', 'dp'), may hold values from -60 to 60
- w_key: bfloat16 [8, 4096, 4096], P('section', None, 'dp'), may hold values from -0.09375 to 0.09375
- w_value: bfloat16 [8, 4096, 4096], P('section', None, 'dp'), may hold values from -0.09375 to 0.09375
- ctx_grad: bfloat16 [8, 512, 4096], P('section', 'dp'), may hold values from -6 to 6
- mem_len: int32 [4], P('dp'), may hold values from 8 to 32, as said below
Outputs:
- query_grad: bfloat16 [8, 512, 4096], P('section', 'dp')
- key_weight_grad: bfloat16 [8, 4096, 4096], P('section', None, 'dp')
- value_weight_grad: bfloat16 [8, 4096, 4096], P('section', None, 'dp')
- state_grad: bfloat16 [8, 128, 4096], P('section', 'dp')
- gain_grad: float32 [4096], replicated
Inputs may be any that keep to these rules, and one draw needn't show every extreme that they name: Sequence b's memory holds mem_len[b] valid tokens from position 0; in every draw some sequence has all 32.
All inputs are finite; a program needn't handle non-finite values.
Results may differ from a plain program's by a relative error of at most 0.028.
The roundings to bfloat16 on the way count: a program that leaves them out, or rounds other values in their place, can miss the bound.
Values may be sent and summed in bfloat16 or wider, within the bound.
No kernel may reach another device: no remote copies, remote signals or barrier semaphores. Data moves between devices by JAX's collectives and lax.ppermute only.
A program may use at most 128 MiB of HBM per device.

v0:
```python
import jax
import jax.numpy as jnp
from jax import lax
from jax.sharding import PartitionSpec as P

HEAD_DIM = 256


epsilon = 1e-06


def broadcast(block, axis, holder):
    block = jnp.where(lax.axis_index(axis) == holder, block, jnp.zeros_like(block))
    return lax.psum(block, axis)


def on_device(enc_state, final_gain, queries, w_key, w_value, ctx_grad, mem_len):
    sections = lax.axis_size("section")
    replicas = lax.axis_size("dp")
    section_index = lax.axis_index("section")
    last_encoder = sections // 2 - 1
    is_decoder = (section_index > last_encoder).astype(jnp.float32)
    is_last = (section_index == last_encoder).astype(jnp.float32)
    src_len = enc_state.shape[1]
    tgt_len = queries.shape[1]
    local_width = w_key.shape[2]
    heads_here = local_width // HEAD_DIM
    score_scale = HEAD_DIM ** (-0.5)
    enc_rows = enc_state[0].astype(jnp.float32)
    inverse = lax.rsqrt(jnp.mean(enc_rows * enc_rows, axis=1, keepdims=True) + epsilon)
    normed = enc_rows * inverse
    memory = (normed * final_gain).astype(jnp.bfloat16)
    sent = broadcast(memory, "section", last_encoder)
    all_memory, all_len = (
        lax.all_gather(sent, "dp", axis=0, tiled=True),
        lax.all_gather(mem_len, "dp", axis=0, tiled=True),
    )
    w_both = jnp.concatenate([w_key[0], w_value[0]], axis=1)
    projected = jnp.dot(all_memory, w_both, preferred_element_type=jnp.float32).astype(jnp.bfloat16)
    key_rows = projected[:, :local_width].reshape(replicas, src_len, heads_here, HEAD_DIM)
    value_rows = projected[:, local_width:].reshape(replicas, src_len, heads_here, HEAD_DIM)
    query_heads, grad_heads = (
        lax.all_to_all(queries[0], "dp", split_axis=1, concat_axis=0, tiled=True),
        lax.all_to_all(ctx_grad[0], "dp", split_axis=1, concat_axis=0, tiled=True),
    )
    query_rows = query_heads.reshape(replicas, tgt_len, heads_here, HEAD_DIM)
    grad_rows = grad_heads.reshape(replicas, tgt_len, heads_here, HEAD_DIM)
    key_valid = jnp.arange(src_len, dtype=jnp.int32)[None, :] < all_len[:, None]
    scores = (
        jnp.einsum("btha,buha->bhut", query_rows, key_rows, preferred_element_type=jnp.float32)
        * score_scale
    )
    scores = jnp.where(key_valid[:, None, :, None], scores, -1e30)
    row_max = jnp.max(scores, axis=2, keepdims=True)
    exponent = jnp.exp(scores - row_max)
    probs = exponent / jnp.sum(exponent, axis=2, keepdims=True)
    probs_low = probs.astype(jnp.bfloat16)
    grad_probs = jnp.einsum(
        "btha,buha->bhut", grad_rows, value_rows, preferred_element_type=jnp.float32
    )
    row_delta = jnp.sum(probs * grad_probs, axis=2, keepdims=True)
    grad_scores = (probs * (grad_probs - row_delta) * score_scale).astype(jnp.bfloat16)
    query_grad_heads = (
        jnp.einsum("bhut,buha->btha", grad_scores, key_rows, preferred_element_type=jnp.float32)
        .astype(jnp.bfloat16)
        .reshape(replicas * tgt_len, local_width)
    )
    key_grad = (
        jnp.einsum("bhut,btha->buha", grad_scores, query_rows, preferred_element_type=jnp.float32)
        .astype(jnp.bfloat16)
        .reshape(replicas * src_len, local_width)
    )
    value_grad = (
        jnp.einsum("bhut,btha->buha", probs_low, grad_rows, preferred_element_type=jnp.float32)
        .astype(jnp.bfloat16)
        .reshape(replicas * src_len, local_width)
    )
    both_grads = jnp.concatenate([key_grad, value_grad], axis=1)
    weight_grads = (
        lax.dot_general(
            all_memory, both_grads, (((0,), (0,)), ((), ())), preferred_element_type=jnp.float32
        )
        * is_decoder
    ).astype(jnp.bfloat16)
    query_back = lax.all_to_all(query_grad_heads, "dp", split_axis=0, concat_axis=1, tiled=True)
    query_grad = (query_back.astype(jnp.float32) * is_decoder).astype(jnp.bfloat16)[None]
    section_part = lax.psum_scatter(
        (
            lax.dot_general(
                both_grads, w_both, (((1,), (1,)), ((), ())), preferred_element_type=jnp.float32
            )
            * is_decoder
        ).astype(jnp.bfloat16),
        "dp",
        scatter_dimension=0,
        tiled=True,
    )
    memory_grad = lax.psum(section_part, "section").astype(jnp.float32)
    scaled_grad = memory_grad * final_gain
    last_grad = inverse * (
        scaled_grad - normed * jnp.mean(scaled_grad * normed, axis=1, keepdims=True)
    )
    state_grad = (last_grad * is_last).astype(jnp.bfloat16)[None]
    gain_grad = lax.psum(jnp.sum(memory_grad * normed, axis=0) * is_last, ("section", "dp"))
    key_weight_grad = weight_grads[:, :local_width][None]
    value_weight_grad = weight_grads[:, local_width:][None]
    return (query_grad, key_weight_grad, value_weight_grad, state_grad, gain_grad)


def solution(mesh):
    placed = (
        P("section", "dp", None),
        P(),
        P("section", "dp", None),
        P("section", None, "dp"),
        P("section", None, "dp"),
        P("section", "dp", None),
        P("dp"),
    )
    return jax.shard_map(
        on_device,
        mesh=mesh,
        in_specs=placed,
        out_specs=(
            P("section", "dp", None),
            P("section", None, "dp"),
            P("section", None, "dp"),
            P("section", "dp", None),
            P(),
        ),
        check_vma=False,
    )
```

profile of v0, /device:TPU:12, one launch (start us, length us, event | category | flops | bytes accessed | tf_op | source)
XLA Modules:
  0.0 290.2 jit_solution(4116352237587877278)
XLA Ops:
  7.2 1.1 fusion.27
  8.3 1.8 fusion.32
  10.2 72.9 %all-reduce.4.cloned.1.call-done = bf16[32,4096]{1,0:T(8,128)(2,1)} async-done(((bf16[32,4096]{1,0:T(8,128)(2,1)}), bf16[32,4096]{1,0:T(8,128)(2,1)}) %all-reduce.4.cloned.1.call-update) | async-done | bytes 262160 | tf_op jit(solution)/shard_map/psum | solution.py:14
  83.1 2.3 copy.16
  85.4 3.5 %all-to-all-start = ((bf16[128,4,1024]{0,2,1:T(8,128)(2,1)}), bf16[128,4,1024]{0,2,1:T(8,128)(2,1)S(1)}, u32[]{:S(2)}, u32[]{:S(2)}) async-start(bf16[128,4,1024]{0,2,1:T(8,128)(2,1)} %bitcast.5), calls=%async_computation | async-start | bytes 2097152 | tf_op jit(solution)/shard_map/all_to_all | solution.py:43
  89.5 1.2 dynamic-slice
  90.8 0.8 dynamic-update-slice
  91.5 17.5 %all-reduce = s32[4]{0:T(128)S(1)} all-reduce(s32[4]{0:T(128)S(1)} %dynamic-update-slice), channel_id=1, replica_groups=mesh['section'=8,'dp'=4] {'dp'}, use_global_device_ids=true, to_apply=%add | all-reduce | flops 4 | bytes 32
  109.0 2.3 copy.19
  111.4 3.5 %all-to-all-start.1 = ((bf16[128,4,1024]{0,2,1:T(8,128)(2,1)}), bf16[128,4,1024]{0,2,1:T(8,128)(2,1)S(1)}, u32[]{:S(2)}, u32[]{:S(2)}) async-start(bf16[128,4,1024]{0,2,1:T(8,128)(2,1)} %bitcast.8), calls=%async_computation.1 | async-start | bytes 2097152 | tf_op jit(solution)/shard_map/all_to_all | solution.py:44
  115.0 7.5 %fusion.6 = bf16[128,2048]{1,0:T(8,128)(2,1)S(1)} fusion(bf16[128,4096]{1,0:T(8,128)(2,1)} %all-gather.2.cloned.1.call-done, bf16[4096,1024]{1,0:T(8,128)(2,1)} %bitcast.60, bf16[4096,1024]{1,0:T(8,128)(2,1)} %bitcast.62), kind=kOutput, calls=%fused_computation.10 | convolution fusion | flops 2181300224 | bytes 18350080 | tf_op jit(solution)/shard_map/dot_general | solution.py:39
  123.2 0.7 fusion.48
  123.9 5.4 %all-to-all-done.1 = bf16[128,4,1024]{0,2,1:T(8,128)(2,1)S(1)} async-done(((bf16[128,4,1024]{0,2,1:T(8,128)(2,1)}), bf16[128,4,1024]{0,2,1:T(8,128)(2,1)S(1)}, u32[]{:S(2)}, u32[]{:S(2)}) %all-to-all-start.1) | async-done | bytes 1048608 | tf_op jit(solution)/shard_map/all_to_all | solution.py:44
  130.5 1.5 convolution_convert_fusion
  132.6 10.1 %fusion.5 = bf16[128,4096]{1,0:T(8,128)(2,1)} fusion(bf16[128,2048]{1,0:T(8,128)(2,1)S(1)} %constant_dynamic-update-slice_fusion, bf16[4096,1024]{1,0:T(8,128)(2,1)} %bitcast.61, bf16[4096,1024]{1,0:T(8,128)(2,1)} %bitcast.63, f32[]{:T(128)S(6)} %convert_element_type.90), kind=kOutput, calls=%fused_computation.9 | convolution fusion | flops 2182086656 | bytes 18350084 | tf_op jit(solution)/shard_map/dot_general | solution.py:89
  142.7 3.5 %all-to-all-start.2 = ((bf16[4,128,1024]{1,2,0:T(8,128)(2,1)}), bf16[4,128,1024]{1,2,0:T(8,128)(2,1)S(1)}, u32[]{:S(2)}, u32[]{:S(2)}) async-start(bf16[4,128,1024]{1,2,0:T(8,128)(2,1)} %bitcast.55), calls=%async_computation.2 | async-start | bytes 2097152 | tf_op jit(solution)/shard_map/all_to_all | solution.py:85
  146.3 8.1 %multiply_convert_fusion = bf16[4096,2048]{1,0:T(8,128)(2,1)} fusion(f32[]{:T(128)S(6)} %convert_element_type.90, bf16[128,4096]{1,0:T(8,128)(2,1)S(1)} %copy-done.1, bf16[128,2048]{1,0:T(8,128)(2,1)S(1)} %constant_dynamic-update-slice_fusion), kind=kOutput, calls=%fused_computation.2 | convolution fusion | flops 2164260864 | bytes 18350084 | tf_op jit(solution)/shard_map/dot_general | solution.py:80
  154.5 11.8 %slice_bitcast_fusion = (bf16[1,4096,1024]{2,1,0:T(8,128)(2,1)}, bf16[1,4096,1024]{2,1,0:T(8,128)(2,1)}) fusion(bf16[4096,2048]{1,0:T(8,128)(2,1)} %multiply_convert_fusion), kind=kLoop, calls=%fused_computation.6 | loop fusion | bytes 33554432 | tf_op jit(solution)/shard_map/broadcast_in_dim | solution.py:106
  166.3 1.0 reduce-scatter.2.cloned.1.call-done
  167.5 1.3 copy.32
  168.9 71.1 %all-reduce.6.cloned.1.call-done = bf16[32,4096]{1,0:T(8,128)(2,1)} async-done(((bf16[32,4096]{1,0:T(8,128)(2,1)}), bf16[32,4096]{1,0:T(8,128)(2,1)}) %all-reduce.6.cloned.1.call-update) | async-done | bytes 262160 | tf_op jit(solution)/shard_map/psum | solution.py:98
  240.0 1.3 fusion.26
  241.3 40.6 %psum.23 = f32[4096]{0:T(1024)} all-reduce(f32[4096]{0:T(1024)S(1)} %broadcast_multiply_fusion), channel_id=1, replica_groups=mesh['section'=8,'dp'=4] {'section','dp'}, use_global_device_ids=true, to_apply=%region_9.10 | all-reduce | flops 4096 | bytes 32768 | tf_op jit(solution)/shard_map/psum | solution.py:104
  281.8 1.8 fusion.33
  (36 shorter events, 3.0 us)
Async XLA Ops:
  7.2 75.9 %all-reduce.4.cloned.1.call-start = ((), (), s32[]{:S(2)}) async-start(), calls=%async_computation.4 | async-start | bytes 524288 | tf_op jit(solution)/shard_map/psum | solution.py:14
  10.2 104.8 %all-gather.2.cloned.1.call-start = ((), (), s32[]{:S(2)}) async-start(), calls=%async_computation.5 | async-start | bytes 1310720 | tf_op jit(solution)/shard_map/all_gather | solution.py:35
  85.4 26.0 %all-to-all-start = ((bf16[128,4,1024]{0,2,1:T(8,128)(2,1)}), bf16[128,4,1024]{0,2,1:T(8,128)(2,1)S(1)}, u32[]{:S(2)}, u32[]{:S(2)}) async-start(bf16[128,4,1024]{0,2,1:T(8,128)(2,1)} %bitcast.5), calls=%async_computation | async-start | bytes 2097152 | tf_op jit(solution)/shard_map/all_to_all | solution.py:43
  111.4 18.0 %all-to-all-start.1 = ((bf16[128,4,1024]{0,2,1:T(8,128)(2,1)}), bf16[128,4,1024]{0,2,1:T(8,128)(2,1)S(1)}, u32[]{:S(2)}, u32[]{:S(2)}) async-start(bf16[128,4,1024]{0,2,1:T(8,128)(2,1)} %bitcast.8), calls=%async_computation.1 | async-start | bytes 2097152 | tf_op jit(solution)/shard_map/all_to_all | solution.py:44
  114.9 52.4 %reduce-scatter.2.cloned.1.call-start = ((), (), s32[]{:S(2)}) async-start(), calls=%async_computation.6 | async-start | bytes 1310720 | tf_op jit(solution)/shard_map/reduce_scatter | solution.py:87
  132.6 13.8 %copy-start.1 = (bf16[128,4096]{1,0:T(8,128)(2,1)S(1)}, bf16[128,4096]{1,0:T(8,128)(2,1)}, u32[]{:S(2)}) copy-start(bf16[128,4096]{1,0:T(8,128)(2,1)} %all-gather.2.cloned.1.call-done) | copy-start | bytes 3145732
  142.7 24.6 %all-to-all-start.2 = ((bf16[4,128,1024]{1,2,0:T(8,128)(2,1)}), bf16[4,128,1024]{1,2,0:T(8,128)(2,1)S(1)}, u32[]{:S(2)}, u32[]{:S(2)}) async-start(bf16[4,128,1024]{1,2,0:T(8,128)(2,1)} %bitcast.55), calls=%async_computation.2 | async-start | bytes 2097152 | tf_op jit(solution)/shard_map/all_to_all | solution.py:85
  146.3 93.7 %all-reduce.6.cloned.1.call-start = ((), (), s32[]{:S(2)}) async-start(), calls=%async_computation.7 | async-start | bytes 524288 | tf_op jit(solution)/shard_map/psum | solution.py:98
  154.4 85.5 %copy-start = (bf16[1,32,4096]{2,1,0:T(8,128)(2,1)S(1)}, bf16[1,32,4096]{2,1,0:T(8,128)(2,1)}, u32[]{:S(2)}) copy-start(bf16[1,32,4096]{2,1,0:T(8,128)(2,1)} %param.7) | copy-start | bytes 786436
  154.5 85.5 %copy-start.2 = (f32[4096]{0:T(1024)S(1)}, f32[4096]{0:T(1024)}, u32[]{:S(2)}) copy-start(f32[4096]{0:T(1024)} %param.8) | copy-start | bytes 49156
Sparse Core Ops, SparseCore 0:
  11.9 71.1 all-reduce.3
  84.7 22.2 all-gather.1
  142.9 24.3 reduce-scatter.1
  170.5 69.4 all-reduce.5
where the time goes:
time: 292 us; the launch traced here: 290 us
  waiting for transfers between devices  151 us (52%)
  blocking collectives  58.1 us (20%)
  matrix products  28.7 us (10%)
  local copies, waits for them, and re-layouts  20.6 us (7%)
  between operations  14.6 us (5%)
  starting transfers between devices  10.7 us (4%)
  other arithmetic  7.03 us (2%)
    psum x1, waiting for transfers between devices, broadcast(): return lax.psum(block, axis)  72.9 us
    psum x1, waiting for transfers between devices, on_device(): memory_grad = lax.psum(section_part, 'section').astype(jnp.float32)  71.1 us
    psum x1, blocking collectives, on_device(): lax.psum(jnp.sum(memory_grad * normed, axis=0) * is_last, ('section', 'dp'))  40.6 us
    unnamed x1, blocking collectives  17.5 us
    broadcast_in_dim x1, local copies, waits for them, and re-layouts, on_device(): value_weight_grad = weight_grads[:, local_width:][None]  11.8 us
    dot_general x1, matrix products, on_device(): lax.dot_general(both_grads, w_both, (((1,), (1,)), ((), ())), preferred_e...  10.1 us
    dot_general x1, matrix products, on_device(): lax.dot_general(all_memory, both_grads, (((0,), (0,)), ((), ())), preferr...  8.11 us
    dot_general x1, matrix products, on_device(): jnp.dot(all_memory, w_both, preferred_element_type=jnp.float32)  7.53 us
  transfers between devices with their start and end apart: 7, of which 4 were waited for; matrix products, arithmetic and copies ran while one was open for 13% of the time, Pallas kernels for 0%

commit v1 on v0

v1 whole, which is shorter than its diff:
```python
import jax
import jax.numpy as jnp
from jax import lax
from jax.sharding import PartitionSpec as P

HEAD_DIM = 256
epsilon = 1e-06
BOTH = ("section", "dp")


def section_rounds(sections):
    half = sections // 2
    source = half - 1
    first = min(half + 1, sections - 1)
    held = {source, first}
    rounds = [[(source, first)]]
    if source > 0 and half + 2 < sections:
        rounds[0].append((source, source - 1))
        held.add(source - 1)
    stage = []
    for a, b in ((first, first + 2), (source - 1, source + 3), (first, first - 1)):
        if a in held and half <= b < sections and b not in held:
            stage.append((a, b))
            held.add(b)
    if stage:
        rounds.append(stage)
    while not held.issuperset(range(half, sections)):
        have = [s for s in sorted(held) if s >= half]
        stage = []
        for a in have:
            b = a + len(have)
            if b < sections and b not in held:
                stage.append((a, b))
                held.add(b)
        rounds.append(stage)
    return rounds


def split_pairs(stage):
    groups = []
    for a, b in stage:
        for group in groups:
            if all(a != c and b != e for c, e in group):
                group.append((a, b))
                break
        else:
            groups.append([(a, b)])
    return groups


def on_device(enc_state, final_gain, queries, w_key, w_value, ctx_grad, mem_len):
    sections = lax.axis_size("section")
    replicas = lax.axis_size("dp")
    section_index = lax.axis_index("section")
    replica = lax.axis_index("dp")
    half = sections // 2
    last_encoder = half - 1
    bits = replicas.bit_length() - 1
    assert replicas == 1 << bits and sections & (sections - 1) == 0
    src_len, width = enc_state.shape[1:]
    tgt_len = queries.shape[1]
    local_width = w_key.shape[2]
    heads_here = local_width // HEAD_DIM
    score_scale = HEAD_DIM ** (-0.5)
    is_last = section_index == last_encoder

    def over_dp(block, k, first=0):
        pairs = [
            (s * replicas + d, s * replicas + (d ^ k))
            for s in range(first, sections)
            for d in range(replicas)
        ]
        return lax.ppermute(block, BOTH, pairs)

    def over_section(block, pairs):
        pairs = [(a * replicas + d, b * replicas + d) for a, b in pairs for d in range(replicas)]
        return lax.ppermute(block, BOTH, pairs)

    order = [0]
    for bit in reversed(range(bits)):
        order = order + [k ^ (1 << bit) for k in order]

    enc_rows = enc_state[0].astype(jnp.float32)
    inverse = lax.rsqrt(jnp.mean(enc_rows * enc_rows, axis=1, keepdims=True) + epsilon)
    normed = enc_rows * inverse
    memory = (normed * final_gain).astype(jnp.bfloat16)
    rounds = section_rounds(sections)
    holding = memory
    arrived = []
    for number, stage in enumerate(rounds):
        came = []
        for group in split_pairs(stage):
            block = over_section(holding, group)
            came.append(block)
            if all(b >= half for _, b in group):
                arrived.append(block)
        passed = came if number == 0 else arrived
        holding = sum(passed[1:], passed[0])
    all_memory = sum(arrived[1:], arrived[0])
    for bit in reversed(range(bits)):
        all_memory = jnp.concatenate([all_memory, over_dp(all_memory, 1 << bit, half)], axis=0)

    lengths = [mem_len] + [over_dp(mem_len, k) for k in range(1, replicas)]
    all_len = jnp.concatenate([lengths[k] for k in order])

    both = jnp.stack([queries[0], ctx_grad[0]])
    shares = []
    for k in range(replicas):
        start = (replica ^ k) * local_width
        share = lax.dynamic_slice(both, (0, 0, start), (2, tgt_len, local_width))
        shares.append(share if k == 0 else over_dp(share, k, half))
    gathered = jnp.stack([shares[k] for k in order]).reshape(
        replicas, 2, tgt_len, heads_here, HEAD_DIM
    )
    query_rows, grad_rows = gathered[:, 0], gathered[:, 1]

    def project(weight):
        rows = jnp.dot(all_memory, weight[0], preferred_element_type=jnp.float32)
        return rows.astype(jnp.bfloat16).reshape(replicas, src_len, heads_here, HEAD_DIM)

    key_rows, value_rows = project(w_key), project(w_value)
    key_valid = jnp.arange(src_len, dtype=jnp.int32)[None, :] < all_len[:, None]
    scores = (
        jnp.einsum("btha,buha->bhut", query_rows, key_rows, preferred_element_type=jnp.float32)
        * score_scale
    )
    scores = jnp.where(key_valid[:, None, :, None], scores, -1e30)
    row_max = jnp.max(scores, axis=2, keepdims=True)
    exponent = jnp.exp(scores - row_max)
    probs = exponent / jnp.sum(exponent, axis=2, keepdims=True)
    probs_low = probs.astype(jnp.bfloat16)
    grad_probs = jnp.einsum(
        "btha,buha->bhut", grad_rows, value_rows, preferred_element_type=jnp.float32
    )
    row_delta = jnp.sum(probs * grad_probs, axis=2, keepdims=True)
    grad_scores = (probs * (grad_probs - row_delta) * score_scale).astype(jnp.bfloat16)
    key_grad = (
        jnp.einsum("bhut,btha->buha", grad_scores, query_rows, preferred_element_type=jnp.float32)
        .astype(jnp.bfloat16)
        .reshape(replicas * src_len, local_width)
    )
    value_grad = (
        jnp.einsum("bhut,btha->buha", probs_low, grad_rows, preferred_element_type=jnp.float32)
        .astype(jnp.bfloat16)
        .reshape(replicas * src_len, local_width)
    )

    across = (((1,), (1,)), ((), ()))
    part = (
        lax.dot_general(key_grad, w_key[0], across, preferred_element_type=jnp.float32)
        + lax.dot_general(value_grad, w_value[0], across, preferred_element_type=jnp.float32)
    ).astype(jnp.bfloat16)
    gain_part = jnp.sum(part.astype(jnp.float32) * all_memory.astype(jnp.float32), axis=0)
    total = part.astype(jnp.float32)
    for bit in range(bits):
        keep = total.shape[0] // 2
        sent = total[keep:].astype(jnp.bfloat16)
        total = total[:keep] + over_dp(sent, 1 << bit, half).astype(jnp.float32)
    is_decoder = section_index >= half
    total = jnp.where(is_decoder, total, 0.0)
    for stage in reversed(rounds):
        sent = total.astype(jnp.bfloat16)
        for group in split_pairs(stage):
            total = total + over_section(sent, [(b, a) for a, b in group]).astype(jnp.float32)
    memory_grad = total
    scaled_grad = memory_grad * final_gain
    last_grad = inverse * (
        scaled_grad - normed * jnp.mean(scaled_grad * normed, axis=1, keepdims=True)
    )
    state_grad = jnp.where(is_last, last_grad, 0.0).astype(jnp.bfloat16)[None]

    query_grad_heads = (
        jnp.einsum("bhut,buha->btha", grad_scores, key_rows, preferred_element_type=jnp.float32)
        .astype(jnp.bfloat16)
        .reshape(replicas, tgt_len, local_width)
    )
    query_grad = jnp.zeros((tgt_len, replicas * local_width), jnp.bfloat16)
    for place, k in enumerate(order):
        share = query_grad_heads[place]
        share = share if k == 0 else over_dp(share, k, half)
        query_grad = lax.dynamic_update_slice(query_grad, share, (0, (replica ^ k) * local_width))

    down = (((0,), (0,)), ((), ()))
    key_weight_grad = lax.dot_general(
        all_memory, key_grad, down, preferred_element_type=jnp.float32
    ).astype(jnp.bfloat16)
    value_weight_grad = lax.dot_general(
        all_memory, value_grad, down, preferred_element_type=jnp.float32
    ).astype(jnp.bfloat16)

    gain_grad = gain_part / final_gain
    for bit in range(bits):
        gain_grad = gain_grad + over_dp(gain_grad, 1 << bit)
    step = 1
    while step < sections:
        pairs = [(s, s ^ step) for s in range(sections)]
        gain_grad = gain_grad + over_section(gain_grad, pairs)
        step *= 2
    return (
        query_grad[None],
        key_weight_grad[None],
        value_weight_grad[None],
        state_grad,
        gain_grad,
    )


def solution(mesh):
    placed = (
        P("section", "dp", None),
        P(),
        P("section", "dp", None),
        P("section", None, "dp"),
        P("section", None, "dp"),
        P("section", "dp", None),
        P("dp"),
    )
    return jax.shard_map(
        on_device,
        mesh=mesh,
        in_specs=placed,
        out_specs=(
            P("section", "dp", None),
            P("section", None, "dp"),
            P("section", None, "dp"),
            P("section", "dp", None),
            P(),
        ),
        check_vma=False,
    )
```

time: 292 us -> 158 us (0.54)
  waiting for transfers between devices: 151 us -> 18.1 us
  blocking collectives: 58.1 us -> 0 us
  starting transfers between devices: 10.7 us -> 60.6 us
  matrix products: 28.7 us -> 43.6 us
  between operations: 14.6 us -> 1.71 us
  other arithmetic: 7.03 us -> 14.5 us
    psum x2 -> x0, waiting for transfers between devices: 144 us -> none  [the longest x1 72.9 us: broadcast(): return lax.psum(block, axis)]
    ppermute x0 -> x26, starting transfers between devices: none -> 60.6 us  [the longest x11 48.7 us: over_section(): return lax.ppermute(block, BOTH, pairs)]
    psum x1 -> x0, blocking collectives: 40.6 us -> none  [on_device(): lax.psum(jnp.sum(memory_grad * normed, axis=0) * is_last, ('section', 'dp'))]
    ppermute x0 -> x26, waiting for transfers between devices: none -> 18.1 us  [the longest x11 16.1 us: over_section(): return lax.ppermute(block, BOTH, pairs)]
    unnamed x1 -> x0, blocking collectives: 17.5 us -> none
    broadcast_in_dim x1 -> x2, local copies, waits for them, and re-layouts: 11.8 us -> 0.24 us  [on_device(): query_grad[None]]
    all_to_all x3 -> x0, starting transfers between devices: 10.6 us -> none  [the longest x1 3.53 us: on_device(): lax.all_to_all(query_grad_heads, 'dp', split_axis=0, concat_axis=1, tiled...]
    dot_general x3 -> x6, matrix products: 25.8 us -> 36.1 us  [the longest x2 10.7 us: project(): rows = jnp.dot(all_memory, weight[0], preferred_element_type=jnp.float32)]
  transfers between devices with their start and end apart: 7 -> 26, of which waited for: 4 -> 4; matrix products, arithmetic and copies ran while one was open for 13% -> 23% of each run, Pallas kernels for 0% -> 0%
where the time goes in v1:
time: 158 us; the launch traced here: 157 us
  starting transfers between devices  60.6 us (38%)
  matrix products  43.6 us (28%)
  local copies, waits for them, and re-layouts  18.1 us (11%)
  waiting for transfers between devices  18.1 us (11%)
  other arithmetic  14.5 us (9%)
  between operations  1.71 us (1%)
    ppermute x11, starting transfers between devices, over_section(): return lax.ppermute(block, BOTH, pairs)  48.7 us
    ppermute x11, waiting for transfers between devices, over_section(): return lax.ppermute(block, BOTH, pairs)  16.1 us
    ppermute x15, starting transfers between devices, over_dp(): return lax.ppermute(block, BOTH, pairs)  11.9 us
    dot_general x2, matrix products, project(): rows = jnp.dot(all_memory, weight[0], preferred_element_type=jnp.float32)  10.7 us
    dot_general x1, matrix products, on_device(): lax.dot_general(key_grad, w_key[0], across, preferred_element_type=jnp.fl...  7.6 us
    dot_general x1, matrix products, on_device(): lax.dot_general(value_grad, w_value[0], across, preferred_element_type=jn...  6.23 us
    dot_general x1, matrix products, on_device(): lax.dot_general(all_memory, key_grad, down, preferred_element_type=jnp.fl...  5.77 us
    dot_general x1, matrix products, on_device(): lax.dot_general(all_memory, value_grad, down, preferred_element_type=jnp....  5.77 us
  transfers between devices with their start and end apart: 26, of which 4 were waited for; matrix products, arithmetic and copies ran while one was open for 23% of the time, Pallas kernels for 0%

profile of v1, /device:TPU:12, one launch (start us, length us, event | category | flops | bytes accessed | tf_op | source)
XLA Modules:
  0.0 156.8 jit_solution(7641193447040344028)
XLA Ops:
  2.9 2.4 %collective-permute-start.1 = (bf16[32,4096]{1,0:T(8,128)(2,1)S(1)}, bf16[32,4096]{1,0:T(8,128)(2,1)S(1)}, u32[]{:S(2)}, u32[]{:S(2)}) collective-permute-start(bf16[32,4096]{1,0:T(8,128)(2,1)S(1)} %fusion.35), channel_id=1, source_target_pairs={{12,8},{13,9},{14,10},{15,11}} | collective-permute-start | bytes 786440 | tf_op jit(solution)/shard_map/ppermute | solution.py:77
  5.4 1.7 %collective-permute-start = (bf16[32,4096]{1,0:T(8,128)(2,1)S(1)}, bf16[32,4096]{1,0:T(8,128)(2,1)S(1)}, u32[]{:S(2)}, u32[]{:S(2)}) collective-permute-start(bf16[32,4096]{1,0:T(8,128)(2,1)S(1)} %fusion.35), channel_id=1, source_target_pairs={{12,20},{13,21},{14,22},{15,23}} | collective-permute-start | bytes 786440 | tf_op jit(solution)/shard_map/ppermute | solution.py:77
  7.1 3.8 %collective-permute-done.1 = bf16[32,4096]{1,0:T(8,128)(2,1)S(1)} collective-permute-done((bf16[32,4096]{1,0:T(8,128)(2,1)S(1)}, bf16[32,4096]{1,0:T(8,128)(2,1)S(1)}, u32[]{:S(2)}, u32[]{:S(2)}) %collective-permute-start.1) | collective-permute-done | bytes 262176 | tf_op jit(solution)/shard_map/ppermute | solution.py:77
  10.9 1.8 %collective-permute-done = bf16[32,4096]{1,0:T(8,128)(2,1)S(1)} collective-permute-done((bf16[32,4096]{1,0:T(8,128)(2,1)S(1)}, bf16[32,4096]{1,0:T(8,128)(2,1)S(1)}, u32[]{:S(2)}, u32[]{:S(2)}) %collective-permute-start) | collective-permute-done | bytes 262176 | tf_op jit(solution)/shard_map/ppermute | solution.py:77
  14.9 1.6 collective-permute-start.6
  17.2 1.6 %copy.20 = bf16[1,128,4096]{1,2,0:T(8,128)(2,1)S(1)} copy(bf16[1,128,4096]{2,1,0:T(8,128)(2,1)} %param.12) | data formatting | bytes 2097152 | tf_op args[5]
  25.6 2.1 %collective-permute-done.8 = s32[1]{0:T(128)} collective-permute-done((s32[1]{0:T(128)}, s32[1]{0:T(128)}, u32[]{:S(2)}, u32[]{:S(2)}) %collective-permute-start.8) | collective-permute-done | bytes 36 | tf_op jit(solution)/shard_map/ppermute | solution.py:73
  27.6 2.0 %pad_add_fusion = s32[4]{0:T(128)S(1)} fusion(s32[1]{0:T(128)} %collective-permute-done.8, s32[1]{0:T(128)} %collective-permute-done.7, s32[1]{0:T(128)} %collective-permute-done.6, s32[1]{0:T(128)S(6)} %copy.46), kind=kLoop, calls=%fused_computation.88 | loop fusion | flops 12 | bytes 32 | tf_op jit(solution)/shard_map/concatenate | solution.py:104
  32.7 1.8 %pad_maximum_fusion = bf16[4,2,128,4,256]{4,2,3,0,1:T(8,128)(2,1)S(1)} fusion(bf16[1,2,128,4,256]{4,2,3,0,1:T(8,128)(2,1)} %copy.24, bf16[1,2,128,4,256]{4,2,3,0,1:T(8,128)(2,1)} %copy.23, bf16[1,2,128,4,256]{4,2,3,0,1:T(8,128)(2,1)} %copy.22, bf16[1,2,128,4,256]{4,2,3,0,1:T(8,128)(2,1)} %copy.21), kind=kLoop, calls=%fused_computation.22 | loop fusion | flops 3145728 | bytes 4194304 | tf_op jit(solution)/shard_map/stack | solution.py:112
  34.5 5.3 %fusion.21 = bf16[128,1024]{1,0:T(8,128)(2,1)} fusion(bf16[1,4096,1024]{2,1,0:T(8,128)(2,1)} %param.11, bf16[64,4096]{1,0:T(8,128)(2,1)S(1)} %collective-permute-done.5, bf16[32,4096]{1,0:T(8,128)(2,1)S(1)} %collective-permute-done.4, bf16[32,4096]{1,0:T(8,128)(2,1)S(1)} %add_add_fusion), kind=kOutput, calls=%fused_computation.28 | convolution fusion | flops 1077018624 | bytes 9699328 | tf_op jit(solution)/shard_map/dot_general | solution.py:118
  41.0 5.3 %fusion.18 = bf16[128,1024]{1,0:T(8,128)(2,1)} fusion(bf16[1,4096,1024]{2,1,0:T(8,128)(2,1)} %param.10, bf16[64,4096]{1,0:T(8,128)(2,1)S(1)} %collective-permute-done.5, bf16[32,4096]{1,0:T(8,128)(2,1)S(1)} %collective-permute-done.4, bf16[32,4096]{1,0:T(8,128)(2,1)S(1)} %add_add_fusion), kind=kOutput, calls=%fused_computation.27 | convolution fusion | flops 1077018624 | bytes 9699328 | tf_op jit(solution)/shard_map/dot_general | solution.py:118
  46.4 1.8 %reshape.87 = bf16[4,32,4,256]{3,2,1,0:T(4,128)(2,1)} reshape(bf16[128,1024]{1,0:T(8,128)(2,1)} %fusion.18) | data formatting | bytes 524288 | tf_op jit(solution)/shard_map/reshape | solution.py:119
  52.7 2.3 %fusion.27 = bf16[4,32,4,256]{3,1,2,0:T(8,128)(2,1)} fusion(f32[4,4,32,128]{3,2,1,0:T(8,128)} %fusion.31, bf16[4,2,128,4,256]{4,2,3,0,1:T(8,128)(2,1)S(1)} %pad_maximum_fusion, f32[4,4,32,128]{3,2,1,0:T(8,128)} %get-tuple-element.16, f32[4,4,128]{2,1,0:T(4,128)S(1)} %get-tuple-element.15), kind=kOutput, calls=%fused_computation.34 | convolution fusion | flops 34146336 | bytes 2375680 | tf_op jit(solution)/shard_map/bhut,btha->buha/dot_general | solution.py:138
  56.4 6.2 %fusion.2 = f32[128,4096]{1,0:T(8,128)S(1)} fusion(bf16[128,1024]{1,0:T(8,128)(2,1)S(1)} %bitcast.72, bf16[1,4096,1024]{2,1,0:T(8,128)(2,1)} %param.11), kind=kOutput, calls=%fused_computation.2 | convolution fusion | flops 1073741824 | bytes 10747904 | tf_op jit(solution)/shard_map/dot_general | solution.py:151
  62.6 7.6 %fusion.74 = (f32[128,4096]{1,0:T(8,128)}, bf16[128,4096]{1,0:T(8,128)(2,1)S(1)}) fusion(f32[128,4096]{1,0:T(8,128)S(1)} %fusion.2, bf16[128,1024]{1,0:T(8,128)(2,1)S(1)} %bitcast.70, bf16[1,4096,1024]{2,1,0:T(8,128)(2,1)} %param.10), kind=kOutput, calls=%fused_computation.99 | convolution fusion | flops 1075314688 | bytes 13893632 | tf_op jit(solution)/shard_map/dot_general | solution.py:150
  71.1 1.5 collective-permute-start.15
  73.2 1.7 %fusion.16 = bf16[4,128,4,256]{1,3,2,0:T(8,128)(2,1)S(1)} fusion(f32[4,4,32,128]{3,2,1,0:T(8,128)} %fusion.31, bf16[4,32,4,256]{3,2,1,0:T(4,128)(2,1)S(1)} %copy-done.3, f32[4,4,32,128]{3,2,1,0:T(8,128)} %get-tuple-element.16, f32[4,4,128]{2,1,0:T(4,128)S(1)} %get-tuple-element.15), kind=kOutput, calls=%fused_computation.25 | convolution fusion | flops 34539552 | bytes 1843200 | tf_op jit(solution)/shard_map/bhut,buha->btha/dot_general | solution.py:173
  76.4 1.8 %copy.30 = bf16[128,1024]{1,0:T(8,128)(2,1)} copy(bf16[128,1024]{0,1:T(8,128)(2,1)} %bitcast.80) | data formatting | bytes 524288 | tf_op jit(solution)/shard_map/squeeze | solution.py:179
  81.9 6.3 %collective-permute-start.23 = (f32[4096]{0:T(1024)S(1)}, f32[4096]{0:T(1024)S(1)}, u32[]{:S(2)}, u32[]{:S(2)}) collective-permute-start(f32[4096]{0:T(1024)S(1)} %add.89), channel_id=1, source_target_pairs={{0,4},{1,5},{2,6},{3,7},{4,0},{5,1},{6,2},{7,3},{8,12},{9,13},{10,... | collective-permute-start | bytes 49160 | tf_op jit(solution)/shard_map/ppermute | solution.py:77
  88.2 1.4 slice_add_fusion
  90.4 5.8 %convert_bitcast_fusion.1 = bf16[1,4096,1024]{2,1,0:T(8,128)(2,1)} fusion(bf16[128,1024]{1,0:T(8,128)(2,1)S(1)} %bitcast.71, bf16[64,4096]{1,0:T(8,128)(2,1)S(1)} %collective-permute-done.5, bf16[32,4096]{1,0:T(8,128)(2,1)S(1)} %collective-permute-done.4, bf16[32,4096]{1,0:T(8,128)(2,1)S(1)} %add_add_fusion), kind=kOutput, calls=%fused_computation.11 | convolution fusion | flops 1081081856 | bytes 9699328 | tf_op jit(solution)/shard_map/dot_general | solution.py:184
  96.2 5.8 %convert_bitcast_fusion = bf16[1,4096,1024]{2,1,0:T(8,128)(2,1)} fusion(bf16[128,1024]{1,0:T(8,128)(2,1)S(1)} %bitcast.73, bf16[64,4096]{1,0:T(8,128)(2,1)S(1)} %collective-permute-done.5, bf16[32,4096]{1,0:T(8,128)(2,1)S(1)} %collective-permute-done.4, bf16[32,4096]{1,0:T(8,128)(2,1)S(1)} %add_add_fusion), kind=kOutput, calls=%fused_computation.10 | convolution fusion | flops 1081081856 | bytes 9699328 | tf_op jit(solution)/shard_map/dot_general | solution.py:187
  102.0 32.2 %collective-permute-start.25 = (f32[4096]{0:T(1024)S(1)}, f32[4096]{0:T(1024)S(1)}, u32[]{:S(2)}, u32[]{:S(2)}) collective-permute-start(f32[4096]{0:T(1024)S(1)} %add.91), channel_id=1, source_target_pairs={{0,16},{1,17},{2,18},{3,19},{4,20},{5,21},{6,22},{7,23},{8,24},{9,... | collective-permute-start | bytes 49160 | tf_op jit(solution)/shard_map/ppermute | solution.py:77
  145.1 10.5 %collective-permute-done.20 = bf16[32,4096]{1,0:T(8,128)(2,1)S(1)} collective-permute-done((bf16[32,4096]{1,0:T(8,128)(2,1)S(1)}, bf16[32,4096]{1,0:T(8,128)(2,1)S(1)}, u32[]{:S(2)}, u32[]{:S(2)}) %collective-permute-start.20) | collective-permute-done | bytes 262176 | tf_op jit(solution)/shard_map/ppermute | solution.py:77
  (99 shorter events, 40.8 us)
Async XLA Ops:
  2.9 8.0 %collective-permute-start.1 = (bf16[32,4096]{1,0:T(8,128)(2,1)S(1)}, bf16[32,4096]{1,0:T(8,128)(2,1)S(1)}, u32[]{:S(2)}, u32[]{:S(2)}) collective-permute-start(bf16[32,4096]{1,0:T(8,128)(2,1)S(1)} %fusion.35), channel_id=1, source_target_pairs={{12,8},{13,9},{14,10},{15,11}} | collective-permute-start | bytes 786440 | tf_op jit(solution)/shard_map/ppermute | solution.py:77
  5.4 7.3 %collective-permute-start = (bf16[32,4096]{1,0:T(8,128)(2,1)S(1)}, bf16[32,4096]{1,0:T(8,128)(2,1)S(1)}, u32[]{:S(2)}, u32[]{:S(2)}) collective-permute-start(bf16[32,4096]{1,0:T(8,128)(2,1)S(1)} %fusion.35), channel_id=1, source_target_pairs={{12,20},{13,21},{14,22},{15,23}} | collective-permute-start | bytes 786440 | tf_op jit(solution)/shard_map/ppermute | solution.py:77
  14.2 8.9 %collective-permute-start.4 = (bf16[32,4096]{1,0:T(8,128)(2,1)S(1)}, bf16[32,4096]{1,0:T(8,128)(2,1)S(1)}, u32[]{:S(2)}, u32[]{:S(2)}) collective-permute-start(bf16[32,4096]{1,0:T(8,128)(2,1)S(1)} %add_add_fusion), channel_id=1, source_target_pairs={{16,18},{17,19},{18,16},{19,17},{20,22},{21,23},{22,20},{23,21},{2... | collective-permute-start | bytes 786440 | tf_op jit(solution)/shard_map/ppermute | solution.py:73
  14.9 9.7 %collective-permute-start.7 = (s32[1]{0:T(128)}, s32[1]{0:T(128)}, u32[]{:S(2)}, u32[]{:S(2)}) collective-permute-start(s32[1]{0:T(128)} %param.13), channel_id=1, source_target_pairs={{0,1},{1,0},{2,3},{3,2},{4,5},{5,4},{6,7},{7,6},{8,9},{9,8},{10,11... | collective-permute-start | bytes 20 | tf_op jit(solution)/shard_map/ppermute | solution.py:73
  14.9 9.9 %collective-permute-start.6 = (s32[1]{0:T(128)}, s32[1]{0:T(128)}, u32[]{:S(2)}, u32[]{:S(2)}) collective-permute-start(s32[1]{0:T(128)} %param.13), channel_id=1, source_target_pairs={{0,2},{1,3},{2,0},{3,1},{4,6},{5,7},{6,4},{7,5},{8,10},{9,11},{10,... | collective-permute-start | bytes 20 | tf_op jit(solution)/shard_map/ppermute | solution.py:73
  20.0 9.7 %collective-permute-start.9 = (bf16[2,128,1024]{1,2,0:T(8,128)(2,1)}, bf16[2,128,1024]{1,2,0:T(8,128)(2,1)S(1)}, u32[]{:S(2)}, u32[]{:S(2)}) collective-permute-start(bf16[2,128,1024]{1,2,0:T(8,128)(2,1)} %get-tuple-element.8), channel_id=1, source_target_pairs={{16,18},{17,19},{18,16},{19,17},{20,22},{21,23},{22,20},{23,21},{2... | collective-permute-start | bytes 1572872 | tf_op jit(solution)/shard_map/ppermute | solution.py:73
  20.7 10.0 %collective-permute-start.10 = (bf16[2,128,1024]{1,2,0:T(8,128)(2,1)}, bf16[2,128,1024]{1,2,0:T(8,128)(2,1)S(1)}, u32[]{:S(2)}, u32[]{:S(2)}) collective-permute-start(bf16[2,128,1024]{1,2,0:T(8,128)(2,1)} %get-tuple-element.9), channel_id=1, source_target_pairs={{16,17},{17,16},{18,19},{19,18},{20,21},{21,20},{22,23},{23,22},{2... | collective-permute-start | bytes 1572872 | tf_op jit(solution)/shard_map/ppermute | solution.py:73
  23.0 8.7 %collective-permute-start.11 = (bf16[2,128,1024]{1,2,0:T(8,128)(2,1)}, bf16[2,128,1024]{1,2,0:T(8,128)(2,1)S(1)}, u32[]{:S(2)}, u32[]{:S(2)}) collective-permute-start(bf16[2,128,1024]{1,2,0:T(8,128)(2,1)} %get-tuple-element.10), channel_id=1, source_target_pairs={{16,19},{17,18},{18,17},{19,16},{20,23},{21,22},{22,21},{23,20},{2... | collective-permute-start | bytes 1572872 | tf_op jit(solution)/shard_map/ppermute | solution.py:73
  24.6 3.1 %collective-permute-start.8 = (s32[1]{0:T(128)}, s32[1]{0:T(128)}, u32[]{:S(2)}, u32[]{:S(2)}) collective-permute-start(s32[1]{0:T(128)} %param.13), channel_id=1, source_target_pairs={{0,3},{1,2},{2,1},{3,0},{4,7},{5,6},{6,5},{7,4},{8,11},{9,10},{10,... | collective-permute-start | bytes 20 | tf_op jit(solution)/shard_map/ppermute | solution.py:73
  24.9 9.6 %collective-permute-start.5 = (bf16[64,4096]{1,0:T(8,128)(2,1)}, bf16[64,4096]{1,0:T(8,128)(2,1)S(1)}, u32[]{:S(2)}, u32[]{:S(2)}) collective-permute-start(bf16[64,4096]{1,0:T(8,128)(2,1)} %pad_maximum_fusion.2), channel_id=1, source_target_pairs={{16,17},{17,16},{18,19},{19,18},{20,21},{21,20},{22,23},{23,22},{2... | collective-permute-start | bytes 1572872 | tf_op jit(solution)/shard_map/ppermute | solution.py:73
  71.1 17.1 %collective-permute-start.15 = (bf16[64,4096]{1,0:T(8,128)(2,1)}, bf16[64,4096]{1,0:T(8,128)(2,1)}, u32[]{:S(2)}, u32[]{:S(2)}) collective-permute-start(bf16[64,4096]{1,0:T(8,128)(2,1)} %slice.53), channel_id=1, source_target_pairs={{16,17},{17,16},{18,19},{19,18},{20,21},{21,20},{22,23},{23,22},{2... | collective-permute-start | bytes 1572872 | tf_op jit(solution)/shard_map/ppermute | solution.py:73
  72.9 2.1 %collective-permute-start.21 = (f32[4096]{0:T(1024)S(1)}, f32[4096]{0:T(1024)S(1)}, u32[]{:S(2)}, u32[]{:S(2)}) collective-permute-start(f32[4096]{0:T(1024)S(1)} %div.21), channel_id=1, source_target_pairs={{0,1},{1,0},{2,3},{3,2},{4,5},{5,4},{6,7},{7,6},{8,9},{9,8},{10,11... | collective-permute-start | bytes 49160 | tf_op jit(solution)/shard_map/ppermute | solution.py:73
  75.0 6.9 %collective-permute-start.22 = (f32[4096]{0:T(1024)S(1)}, f32[4096]{0:T(1024)S(1)}, u32[]{:S(2)}, u32[]{:S(2)}) collective-permute-start(f32[4096]{0:T(1024)S(1)} %add.88), channel_id=1, source_target_pairs={{0,2},{1,3},{2,0},{3,1},{4,6},{5,7},{6,4},{7,5},{8,10},{9,11},{10,... | collective-permute-start | bytes 49160 | tf_op jit(solution)/shard_map/ppermute | solution.py:73
  79.1 60.2 %collective-permute-start.12 = (bf16[128,1024]{1,0:T(8,128)(2,1)}, bf16[128,1024]{1,0:T(8,128)(2,1)}, u32[]{:S(2)}, u32[]{:S(2)}) collective-permute-start(bf16[128,1024]{1,0:T(8,128)(2,1)} %copy.29), channel_id=1, source_target_pairs={{16,18},{17,19},{18,16},{19,17},{20,22},{21,23},{22,20},{23,21},{2... | collective-permute-start | bytes 786440 | tf_op jit(solution)/shard_map/ppermute | solution.py:73
  80.5 63.5 %collective-permute-start.13 = (bf16[128,1024]{1,0:T(8,128)(2,1)}, bf16[128,1024]{1,0:T(8,128)(2,1)}, u32[]{:S(2)}, u32[]{:S(2)}) collective-permute-start(bf16[128,1024]{1,0:T(8,128)(2,1)} %copy.30), channel_id=1, source_target_pairs={{16,17},{17,16},{18,19},{19,18},{20,21},{21,20},{22,23},{23,22},{2... | collective-permute-start | bytes 786440 | tf_op jit(solution)/shard_map/ppermute | solution.py:73
  81.9 14.2 %collective-permute-start.23 = (f32[4096]{0:T(1024)S(1)}, f32[4096]{0:T(1024)S(1)}, u32[]{:S(2)}, u32[]{:S(2)}) collective-permute-start(f32[4096]{0:T(1024)S(1)} %add.89), channel_id=1, source_target_pairs={{0,4},{1,5},{2,6},{3,7},{4,0},{5,1},{6,2},{7,3},{8,12},{9,13},{10,... | collective-permute-start | bytes 49160 | tf_op jit(solution)/shard_map/ppermute | solution.py:77
  89.7 44.6 %collective-permute-start.16 = (bf16[32,4096]{1,0:T(8,128)(2,1)S(1)}, bf16[32,4096]{1,0:T(8,128)(2,1)S(1)}, u32[]{:S(2)}, u32[]{:S(2)}) collective-permute-start(bf16[32,4096]{1,0:T(8,128)(2,1)S(1)} %slice.71), channel_id=1, source_target_pairs={{16,18},{17,19},{18,16},{19,17},{20,22},{21,23},{22,20},{23,21},{2... | collective-permute-start | bytes 786440 | tf_op jit(solution)/shard_map/ppermute | solution.py:73
  96.1 5.8 %collective-permute-start.24 = (f32[4096]{0:T(1024)S(1)}, f32[4096]{0:T(1024)S(1)}, u32[]{:S(2)}, u32[]{:S(2)}) collective-permute-start(f32[4096]{0:T(1024)S(1)} %add.90), channel_id=1, source_target_pairs={{0,8},{1,9},{2,10},{3,11},{4,12},{5,13},{6,14},{7,15},{8,0},{9,1},... | collective-permute-start | bytes 49160 | tf_op jit(solution)/shard_map/ppermute | solution.py:77
  102.0 36.0 %collective-permute-start.25 = (f32[4096]{0:T(1024)S(1)}, f32[4096]{0:T(1024)S(1)}, u32[]{:S(2)}, u32[]{:S(2)}) collective-permute-start(f32[4096]{0:T(1024)S(1)} %add.91), channel_id=1, source_target_pairs={{0,16},{1,17},{2,18},{3,19},{4,20},{5,21},{6,22},{7,23},{8,24},{9,... | collective-permute-start | bytes 49160 | tf_op jit(solution)/shard_map/ppermute | solution.py:77
  135.0 5.3 %collective-permute-start.18 = (bf16[32,4096]{1,0:T(8,128)(2,1)}, bf16[32,4096]{1,0:T(8,128)(2,1)S(1)}, u32[]{:S(2)}, u32[]{:S(2)}) collective-permute-start(bf16[32,4096]{1,0:T(8,128)(2,1)} %fusion.51), channel_id=1, source_target_pairs={{16,20},{17,21},{18,22},{19,23}} | collective-permute-start | bytes 786440 | tf_op jit(solution)/shard_map/ppermute | solution.py:77
  135.7 4.6 %collective-permute-start.17 = (bf16[32,4096]{1,0:T(8,128)(2,1)}, bf16[32,4096]{1,0:T(8,128)(2,1)}, u32[]{:S(2)}, u32[]{:S(2)}) collective-permute-start(bf16[32,4096]{1,0:T(8,128)(2,1)} %fusion.51), channel_id=1, source_target_pairs={{28,20},{29,21},{30,22},{31,23},{24,8},{25,9},{26,10},{27,11}} | collective-permute-start | bytes 786440 | tf_op jit(solution)/shard_map/ppermute | solution.py:77
  138.0 7.0 %collective-permute-start.14 = (bf16[128,1024]{1,0:T(8,128)(2,1)}, bf16[128,1024]{1,0:T(8,128)(2,1)S(1)}, u32[]{:S(2)}, u32[]{:S(2)}) collective-permute-start(bf16[128,1024]{1,0:T(8,128)(2,1)} %copy.31), channel_id=1, source_target_pairs={{16,19},{17,18},{18,17},{19,16},{20,23},{21,22},{22,21},{23,20},{2... | collective-permute-start | bytes 786440 | tf_op jit(solution)/shard_map/ppermute | solution.py:73
  141.4 14.1 %collective-permute-start.20 = (bf16[32,4096]{1,0:T(8,128)(2,1)S(1)}, bf16[32,4096]{1,0:T(8,128)(2,1)S(1)}, u32[]{:S(2)}, u32[]{:S(2)}) collective-permute-start(bf16[32,4096]{1,0:T(8,128)(2,1)S(1)} %get-tuple-element.5), channel_id=1, source_target_pairs={{8,12},{9,13},{10,14},{11,15}} | collective-permute-start | bytes 786440 | tf_op jit(solution)/shard_map/ppermute | solution.py:77
  142.7 12.8 %collective-permute-start.19 = (bf16[32,4096]{1,0:T(8,128)(2,1)S(1)}, bf16[32,4096]{1,0:T(8,128)(2,1)S(1)}, u32[]{:S(2)}, u32[]{:S(2)}) collective-permute-start(bf16[32,4096]{1,0:T(8,128)(2,1)S(1)} %get-tuple-element.5), channel_id=1, source_target_pairs={{20,12},{21,13},{22,14},{23,15}} | collective-permute-start | bytes 786440 | tf_op jit(solution)/shard_map/ppermute | solution.py:77
  (8 other events, 57.1 us)

commit v2 on v1

v2 whole, which is shorter than its diff:
```python
import jax
import jax.numpy as jnp
from jax import lax
from jax.experimental import pallas as pl
from jax.experimental.pallas import tpu as pltpu
from jax.sharding import PartitionSpec as P

HEAD_DIM = 256
epsilon = 1e-06
BOTH = ("section", "dp")
LANES = 128


def section_rounds(sections):
    half = sections // 2
    source = half - 1
    first = min(half + 1, sections - 1)
    held = {source, first}
    rounds = [[(source, first)]]
    if source > 0 and half + 2 < sections:
        rounds[0].append((source, source - 1))
        held.add(source - 1)
    stage = []
    for a, b in ((first, first + 2), (source - 1, source + 3), (first, first - 1)):
        if a in held and half <= b < sections and b not in held:
            stage.append((a, b))
            held.add(b)
    if stage:
        rounds.append(stage)
    while not held.issuperset(range(half, sections)):
        have = [s for s in sorted(held) if s >= half]
        stage = []
        for a in have:
            b = a + len(have)
            if b < sections and b not in held:
                stage.append((a, b))
                held.add(b)
        rounds.append(stage)
    return rounds


def split_pairs(stage):
    groups = []
    for a, b in stage:
        for group in groups:
            if all(a != c and b != e for c, e in group):
                group.append((a, b))
                break
        else:
            groups.append([(a, b)])
    return groups


def call(kernel, out_shape, flops=0, moved=0, vmem=16, **options):
    return pl.pallas_call(
        kernel,
        out_shape=out_shape,
        compiler_params=pltpu.CompilerParams(vmem_limit_bytes=vmem << 20),
        cost_estimate=pl.CostEstimate(flops=flops, bytes_accessed=moved, transcendentals=0),
        **options,
    )


def shape(dims, dtype=jnp.bfloat16):
    return jax.ShapeDtypeStruct(dims, dtype)


def dot(a, b, dims=((1,), (0,))):
    return lax.dot_general(a, b, (dims, ((), ())), preferred_element_type=jnp.float32)


SMEM = pl.BlockSpec(memory_space=pltpu.SMEM)
VMEM = pl.BlockSpec(memory_space=pltpu.VMEM)
ANY = pl.BlockSpec(memory_space=pl.ANY)
TOKEN = shape((8, LANES), jnp.float32)


def mark(token_ref):
    token_ref[...] = jnp.zeros_like(token_ref)


def encode(mem_len, enc_state, gain):
    rows, width = enc_state.shape[1:]
    assert rows <= 256

    def kernel(len_ref, enc_ref, gain_ref, out_ref):
        state = enc_ref[0].astype(jnp.float32)
        inverse = lax.rsqrt(jnp.mean(state * state, axis=1, keepdims=True) + epsilon)
        out_ref[:, :width] = (state * inverse * gain_ref[...]).astype(jnp.bfloat16)
        length = jnp.full((rows, LANES), len_ref[0].astype(jnp.float32))
        out_ref[:, width:] = length.astype(jnp.bfloat16)

    return call(
        kernel,
        shape((rows, width + LANES)),
        moved=4 * rows * width,
        in_specs=[SMEM, VMEM, VMEM],
        out_specs=VMEM,
    )(mem_len, enc_state, gain)


def split_heads(scalars, queries, ctx_grad, replicas, tokens):
    rows, width = queries.shape[1:]
    piece = width // replicas
    sizes = []
    while replicas > 1 << len(sizes):
        sizes.append(replicas >> (len(sizes) + 1))
    starts = [*sizes, 0]
    sizes.append(1)

    def kernel(scalar_ref, query_ref, grad_ref, *refs):
        *out_refs, token_ref, sems = refs[len(tokens) :]
        copies = []
        for start, size, out_ref in zip(starts, sizes, out_refs, strict=True):
            for k in range(start, start + size):
                columns = pl.ds(pl.multiple_of((scalar_ref[0] ^ k) * piece, piece), piece)
                for i, ref in enumerate((query_ref, grad_ref)):
                    place = out_ref.at[k - start, i]
                    copy = pltpu.make_async_copy(ref.at[0, :, columns], place, sems.at[k, i])
                    copy.start()
                    copies.append(copy)
        mark(token_ref)
        for copy in copies:
            copy.wait()

    *shares, token = call(
        kernel,
        [shape((size, 2, rows, piece)) for size in sizes] + [TOKEN],
        moved=8 * rows * width,
        in_specs=[SMEM] + [ANY] * (2 + len(tokens)),
        out_specs=[ANY] * len(sizes) + [VMEM],
        scratch_shapes=[pltpu.SemaphoreType.DMA((replicas, 2))],
    )(scalars, queries, ctx_grad, *tokens)
    return shares, token


def add_blocks(blocks, tokens=()):
    def kernel(*refs):
        total = refs[0][...]
        for ref in refs[1 : len(blocks)]:
            total = total + ref[...]
        refs[-1][...] = total

    return call(
        kernel,
        shape(blocks[0].shape),
        moved=8 * blocks[0].size,
        in_specs=[VMEM] * len(blocks) + [ANY] * len(tokens),
        out_specs=VMEM,
    )(*blocks, *tokens)


def join_heads(shares):
    replicas, rows, piece = shares.shape

    def kernel(share_ref, out_ref, sems):
        copies = []
        for k in range(replicas):
            columns = pl.ds(k * piece, piece)
            copy = pltpu.make_async_copy(share_ref.at[k], out_ref.at[0, :, columns], sems.at[k])
            copy.start()
            copies.append(copy)
        for copy in copies:
            copy.wait()

    return call(
        kernel,
        shape((1, rows, replicas * piece)),
        moved=4 * rows * replicas * piece,
        in_specs=[ANY],
        out_specs=ANY,
        scratch_shapes=[pltpu.SemaphoreType.DMA((replicas,))],
    )(shares)


def hold_weights(w_key, w_value, tokens):
    steps = 4
    step = w_key.shape[1] // steps

    def kernel(wk_ref, wv_ref, *refs):
        *out_refs, token_ref, sems = refs[len(tokens) :]
        copies = []
        for i in range(steps):
            rows = pl.ds(i * step, step)
            for j, (ref, out_ref) in enumerate(zip((wk_ref, wv_ref), out_refs, strict=True)):
                copy = pltpu.make_async_copy(ref.at[0, rows], out_ref.at[0, rows], sems.at[i, j])
                copy.start()
                copies.append(copy)
        mark(token_ref)
        for copy in copies:
            copy.wait()

    *held, token = call(
        kernel,
        [shape(w_key.shape)] * 2 + [TOKEN],
        flops=1 << 34,
        moved=4 * w_key.size,
        vmem=36,
        in_specs=[ANY] * (2 + len(tokens)),
        out_specs=[ANY, ANY, VMEM],
        scratch_shapes=[pltpu.SemaphoreType.DMA((steps, 2))],
    )(w_key, w_value, *tokens)
    return held, token


def follow(block, tokens):
    def kernel(*refs):
        del refs

    return call(
        kernel,
        shape(block.shape, block.dtype),
        in_specs=[ANY] * (1 + len(tokens)),
        out_specs=ANY,
        input_output_aliases={0: 0},
    )(block, *tokens)


def attend(scalars, pieces, w_key, w_value, shares, order):
    count = len(pieces)
    rows = pieces[0].shape[0]
    depth, width = w_key.shape[1:]
    targets = shares[0].shape[2]
    scale = HEAD_DIM ** (-0.5)
    heads = width // HEAD_DIM

    def kernel(scalar_ref, *refs):
        wk_ref, wv_ref, *share_refs = refs[count : 2 * count + 2]
        dk_ref, dv_ref, dq_ref = refs[2 * count + 2 : 2 * count + 5]
        key_ref, value_ref, score_ref, grad_ref, low_ref = refs[2 * count + 5 :]
        memory = jnp.concatenate([ref[:, :depth] for ref in refs[:count]], axis=0)
        key_ref[...] = dot(memory, wk_ref[0]).astype(jnp.bfloat16)
        value_ref[...] = dot(memory, wv_ref[0]).astype(jnp.bfloat16)
        blocks = []
        for h in range(heads):
            for p, k in enumerate(order):
                head, own = slice(h * HEAD_DIM, (h + 1) * HEAD_DIM), slice(p * rows, (p + 1) * rows)
                blocks.append((head, own, scalar_ref[0] ^ k, share_refs[p]))
        for i, (head, own, _, share_ref) in enumerate(blocks):
            query, grad = share_ref[0, 0, :, head], share_ref[0, 1, :, head]
            score_ref[i] = dot(key_ref[own, head], query, ((1,), (1,)))
            grad_ref[i] = dot(value_ref[own, head], grad, ((1,), (1,)))
        token = lax.broadcasted_iota(jnp.int32, (rows, targets), 0).astype(jnp.float32)
        lengths = [ref[0:1, depth : depth + 1].astype(jnp.float32) for ref in refs[:count]]
        valid = jnp.stack([token < length for length in lengths])
        for h in range(heads):
            here = slice(h * count, (h + 1) * count)
            scores = jnp.where(valid, score_ref[here] * scale, -1e30)
            exponent = jnp.exp(scores - jnp.max(scores, axis=1, keepdims=True))
            probs = exponent / jnp.sum(exponent, axis=1, keepdims=True)
            grad_probs = grad_ref[here]
            delta = jnp.sum(probs * grad_probs, axis=1, keepdims=True)
            low_ref[0, here] = (probs * (grad_probs - delta) * scale).astype(jnp.bfloat16)
            low_ref[1, here] = probs.astype(jnp.bfloat16)
        is_decoder = scalar_ref[1].astype(jnp.float32)
        for i, (head, own, place, share_ref) in enumerate(blocks):
            query, grad = share_ref[0, 0, :, head], share_ref[0, 1, :, head]
            dk_ref[own, head] = dot(low_ref[0, i], query).astype(jnp.bfloat16)
            dv_ref[own, head] = (dot(low_ref[1, i], grad) * is_decoder).astype(jnp.bfloat16)
            dq = dot(low_ref[0, i], key_ref[own, head], ((0,), (0,)))
            dq_ref[place, :, head] = dq.astype(jnp.bfloat16)

    scores = (heads * count, rows, targets)
    return call(
        kernel,
        [shape((count * rows, width))] * 2 + [shape((count, targets, width))],
        flops=4 * count * rows * depth * width + 10 * count * rows * targets * width,
        moved=4 * depth * width + 8 * count * targets * width,
        in_specs=[SMEM] + [VMEM] * (2 * count + 2),
        out_specs=[VMEM] * 3,
        scratch_shapes=[
            *[pltpu.VMEM((count * rows, width), jnp.bfloat16)] * 2,
            *[pltpu.VMEM(scores, jnp.float32)] * 2,
            pltpu.VMEM((2, *scores), jnp.bfloat16),
        ],
    )(scalars, *pieces, w_key, w_value, *shares)


def memory_part(pieces, w_key, w_value, dk, dv, gain):
    count = len(pieces)
    rows = pieces[0].shape[0]
    depth, width = w_key.shape[1:]
    tile = 512
    steps = depth // tile
    keep = count * rows // 2

    def kernel(*refs):
        dk_ref, dv_ref, wk_ref, wv_ref, gain_ref, keep_ref, sent_ref, out_ref = refs[count:]
        for f in range(steps):
            here = slice(f * tile, (f + 1) * tile)
            part = dot(wk_ref[0, here, :], dk_ref[...], ((1,), (1,)))
            part = (part + dot(wv_ref[0, here, :], dv_ref[...], ((1,), (1,)))).T
            keep_ref[:, here] = part[:keep]
            sent_ref[:, here] = part[keep:].astype(jnp.bfloat16)
            total = jnp.zeros((1, tile), jnp.float32)
            for p in range(count):
                memory = refs[p][:, here].astype(jnp.float32)
                total += jnp.sum(part[p * rows : (p + 1) * rows] * memory, axis=0, keepdims=True)
            total = total / gain_ref[:, here]
            for i in range(tile // LANES):
                place = (f * tile) // LANES + i
                out_ref[place : place + 1, :] = total[:, i * LANES : (i + 1) * LANES]
        put_gain(out_ref[...], sent_ref)

    return call(
        kernel,
        [
            shape((keep, depth), jnp.float32),
            shape((keep, depth + 2 * LANES)),
            shape((depth // LANES, LANES), jnp.float32),
        ],
        flops=4 * count * rows * depth * width,
        moved=4 * depth * width,
        in_specs=[VMEM] * (count + 5),
        out_specs=[VMEM] * 3,
    )(*pieces, dk, dv, w_key, w_value, gain)


def put_gain(gain, sent_ref):
    rows = gain.shape[0]
    depth = sent_ref.shape[1] - 2 * LANES
    assert sent_ref.shape[0] >= rows
    high = gain.astype(jnp.bfloat16)
    if sent_ref.shape[0] > rows:
        sent_ref[rows:, depth:] = jnp.zeros((sent_ref.shape[0] - rows, 2 * LANES), jnp.bfloat16)
    sent_ref[:rows, depth : depth + LANES] = high
    sent_ref[:rows, depth + LANES :] = (gain - high.astype(jnp.float32)).astype(jnp.bfloat16)


def add_share(kept, came, gain, last, tokens=()):
    rows, depth = kept.shape
    half = rows if last else rows // 2

    def kernel(kept_ref, came_ref, gain_ref, *refs):
        keep_ref, sent_ref, out_ref, token_ref = refs[len(tokens) :]
        out = gain_ref.shape[0]
        came_gain = came_ref[:out, depth:].astype(jnp.float32)
        total_gain = gain_ref[...] + (came_gain[:, :LANES] + came_gain[:, LANES:])
        out_ref[...] = total_gain
        keep_ref[...] = kept_ref[:half] + came_ref[:half, :depth].astype(jnp.float32)
        if last:
            sent_ref[...] = keep_ref[...].astype(jnp.bfloat16)
        else:
            other = kept_ref[half:] + came_ref[half:, :depth].astype(jnp.float32)
            sent_ref[:, :depth] = other.astype(jnp.bfloat16)
            put_gain(total_gain, sent_ref)
        mark(token_ref)

    return call(
        kernel,
        [
            shape((half, depth), jnp.float32),
            shape((half, depth + (0 if last else 2 * LANES))),
            shape(gain.shape, jnp.float32),
            TOKEN,
        ],
        moved=10 * rows * depth,
        in_specs=[VMEM] * 3 + [ANY] * len(tokens),
        out_specs=[VMEM] * 4,
    )(kept, came, gain, *tokens)


def add_sections(kept, came, tokens=()):
    count = len(came)

    def kernel(kept_ref, *refs):
        keep_ref, sent_ref, token_ref = refs[count + len(tokens) :]
        total = kept_ref[...]
        for ref in refs[:count]:
            total = total + ref[...].astype(jnp.float32)
        keep_ref[...] = total
        sent_ref[...] = total.astype(jnp.bfloat16)
        mark(token_ref)

    return call(
        kernel,
        [shape(kept.shape, jnp.float32), shape(kept.shape), TOKEN],
        moved=12 * kept.size,
        in_specs=[VMEM] * (1 + count) + [ANY] * len(tokens),
        out_specs=[VMEM] * 3,
    )(kept, *came, *tokens)


def weight_grads(pieces, width, part, parts, dk, dv, before, tokens=()):
    count = len(pieces)
    rows = pieces[0].shape[0]
    columns = dk.shape[1]
    tile = 1024
    steps = width // (parts * tile)

    def kernel(*refs):
        memory = jnp.concatenate([ref[...] for ref in refs[:count]], axis=0)
        dk_ref, dv_ref = refs[count : count + 2]
        key_ref, value_ref, token_ref = refs[-3:]
        key_ref[0] = dot(memory, dk_ref[...], ((0,), (0,))).astype(jnp.bfloat16)
        value_ref[0] = dot(memory, dv_ref[...], ((0,), (0,))).astype(jnp.bfloat16)
        mark(token_ref)

    piece = pl.BlockSpec((rows, tile), lambda f: (0, part * steps + f))
    whole = pl.BlockSpec((count * rows, columns), lambda f: (0, 0))
    out = pl.BlockSpec((1, tile, columns), lambda f: (0, part * steps + f, 0))
    first = count + 2 + len(tokens)
    *grads, token = call(
        kernel,
        [shape((1, width, columns))] * 2 + [TOKEN],
        flops=4 * count * rows * width * columns // parts,
        moved=4 * width * columns // parts,
        vmem=24,
        grid=(steps,),
        in_specs=[piece] * count + [whole] * 2 + [ANY] * (len(tokens) + len(before)),
        out_specs=[out] * 2 + [pl.BlockSpec(TOKEN.shape, lambda f: (0, 0))],
        input_output_aliases={first + i: i for i in range(len(before))},
    )(*pieces, dk, dv, *tokens, *before)
    return grads, token


def finish(flag, enc_state, gain, terms):
    rows, width = enc_state.shape[1:]

    def kernel(flag_ref, enc_ref, gain_ref, *refs):
        state = enc_ref[0].astype(jnp.float32)
        inverse = lax.rsqrt(jnp.mean(state * state, axis=1, keepdims=True) + epsilon)
        normed = state * inverse
        own = [ref[...].astype(jnp.float32) for ref in refs[:-1]]
        scaled = sum(own[1:], own[0]) * gain_ref[...]
        mean = jnp.mean(scaled * normed, axis=1, keepdims=True)
        grad = inverse * (scaled - normed * mean)
        refs[-1][0] = jnp.where(flag_ref[0] > 0, grad, 0.0).astype(jnp.bfloat16)

    return call(
        kernel,
        shape((1, rows, width)),
        moved=8 * rows * width,
        in_specs=[SMEM] + [VMEM] * (2 + len(terms)),
        out_specs=VMEM,
    )(flag, enc_state, gain, *terms)


def on_device(enc_state, final_gain, queries, w_key, w_value, ctx_grad, mem_len):
    sections = lax.axis_size("section")
    replicas = lax.axis_size("dp")
    section_index = lax.axis_index("section")
    half = sections // 2
    bits = replicas.bit_length() - 1
    assert replicas == 1 << bits and half & (half - 1) == 0 and half > 1 and bits > 1
    is_decoder = (section_index >= half).astype(jnp.int32)
    is_last = (section_index == half - 1).astype(jnp.int32)[None]
    scalars = jnp.stack([lax.axis_index("dp").astype(jnp.int32), is_decoder])
    gain = final_gain[None]

    def over_dp(block, k):
        pairs = [
            (s * replicas + d, s * replicas + (d ^ k))
            for s in range(half, sections)
            for d in range(replicas)
        ]
        return lax.ppermute(block, BOTH, pairs)

    def over_section(block, pairs):
        pairs = [(a * replicas + d, b * replicas + d) for a, b in pairs for d in range(replicas)]
        return lax.ppermute(block, BOTH, pairs)

    order = [0]
    for bit in reversed(range(bits)):
        order = order + [k ^ (1 << bit) for k in order]
    rounds = section_rounds(sections)

    memory = encode(mem_len, enc_state, gain)
    shares, split = split_heads(scalars, queries, ctx_grad, replicas, [memory])
    came = {}
    for bit, share in zip(reversed(range(bits)), shares, strict=False):
        size = 1 << bit
        passed = {k ^ size: over_dp(block[size : 2 * size], size) for k, block in came.items()}
        came = came | passed | {size: over_dp(share, size)}
    came[0] = shares[-1]
    shares = [came[k] for k in order]
    came = [over_section(memory, group) for group in split_pairs(rounds[0])]
    arrived = [came[0]]
    holding = add_blocks(came, [split])
    weights, held = hold_weights(w_key, w_value, [holding])
    for stage in rounds[1:]:
        arrived += [over_section(holding, group) for group in split_pairs(stage)]
        holding = add_blocks(arrived, [held])
    pieces = {0: holding}
    for bit in reversed(range(bits)):
        pieces |= {k ^ (1 << bit): over_dp(pieces[k], 1 << bit) for k in list(pieces)}
    pieces = [pieces[k] for k in order]
    dk, dv, dq = attend(scalars, pieces, *weights, shares, order)

    kept, sent, gain_part = memory_part(pieces, *weights, dk, dv, gain)
    width = enc_state.shape[2]
    decoders = range(half, sections)
    parts = 4
    grads, token = [], None
    for bit in range(bits):
        last = bit == bits - 1
        came = over_dp(sent, 1 << bit)
        tokens = []
        if last:
            for part in range(parts - 1):
                grads, token = weight_grads(pieces, width, part, parts, dk, dv, grads, [token])
            tokens = [token]
        kept, sent, gain_part, token = add_share(kept, came, gain_part, last, tokens)
    dq = follow(dq, [token])
    grads, token = weight_grads(pieces, width, parts - 1, parts, dk, dv, grads, [token])
    key_weight_grad, value_weight_grad = grads
    step = 1
    while step < half // 2:
        gain_part = gain_part + over_section(gain_part, [(s, s ^ step) for s in decoders])
        step *= 2
    tokens = [token, gain_part]
    for number, stage in reversed(list(enumerate(rounds))):
        came = [over_section(sent, [(b, a) for a, b in group]) for group in split_pairs(stage)]
        if number:
            kept, sent, _ = add_sections(kept, came, tokens)
            tokens = []
    state_grad = finish(is_last, enc_state, gain, came)
    gain_part = (
        gain_part
        + over_section(gain_part, [(s, s ^ step) for s in decoders])
        + over_section(gain_part, [(s, s - half) for s in decoders])
        + over_section(gain_part, [(s, (s ^ step) - half) for s in decoders])
    )

    query_grad = join_heads(lax.all_to_all(dq, "dp", split_axis=0, concat_axis=0, tiled=True))

    gain_grad = gain_part.reshape(width)
    return (query_grad, key_weight_grad, value_weight_grad, state_grad, gain_grad)


def solution(mesh):
    placed = (
        P("section", "dp", None),
        P(),
        P("section", "dp", None),
        P("section", None, "dp"),
        P("section", None, "dp"),
        P("section", "dp", None),
        P("dp"),
    )
    return jax.shard_map(
        on_device,
        mesh=mesh,
        in_specs=placed,
        out_specs=(
            P("section", "dp", None),
            P("section", None, "dp"),
            P("section", None, "dp"),
            P("section", "dp", None),
            P(),
        ),
        check_vma=False,
    )
```

time: 158 us -> 103 us (0.65)
  matrix products: 43.6 us -> 0 us
  starting transfers between devices: 60.6 us -> 22.6 us
  Pallas kernels: 0 us -> 30.5 us
  waiting for transfers between devices: 18.1 us -> 39.9 us
  other arithmetic: 14.5 us -> 0.69 us
  local copies, waits for them, and re-layouts: 18.1 us -> 5.83 us
    dot_general x11 -> x0, matrix products: 43.6 us -> none  [the longest x2 10.7 us: project(): rows = jnp.dot(all_memory, weight[0], preferred_element_type=jnp.float32)]
    ppermute x11 -> x12, starting transfers between devices: 48.7 us -> 13.4 us  [over_section(): return lax.ppermute(block, BOTH, pairs)]
    pallas_call x0 -> x17, Pallas kernels: none -> 30.5 us  [the longest x4 11.4 us: weight_grads(): call(kernel, [shape((1, width, columns))] * 2 + [TOKEN], flops=4 * count...]
    ppermute x11 -> x12, waiting for transfers between devices: 16.1 us -> 39.9 us  [over_section(): return lax.ppermute(block, BOTH, pairs)]
    ppermute x15 -> x8, starting transfers between devices: 11.9 us -> 5.7 us  [over_dp(): return lax.ppermute(block, BOTH, pairs)]
    another operation x4 -> x0, local copies, waits for them, and re-layouts: 4.07 us -> none  [on_device(): jnp.stack([shares[k] for k in order])]
    all_to_all x0 -> x1, starting transfers between devices: none -> 3.52 us  [on_device(): lax.all_to_all(dq, 'dp', split_axis=0, concat_axis=0, tiled=True)]
    squeeze x3 -> x0, local copies, waits for them, and re-layouts: 3.49 us -> none  [on_device(): share = query_grad_heads[place]]
  transfers between devices with their start and end apart: 26 -> 21, of which waited for: 4 -> 2; matrix products, arithmetic and copies ran while one was open for 23% -> 1% of each run, Pallas kernels for 0% -> 20%
where the time goes in v2:
time: 103 us; the launch traced here: 101 us
  waiting for transfers between devices  39.9 us (39%)
  Pallas kernels  30.5 us (30%)
  starting transfers between devices  22.6 us (22%)
  local copies, waits for them, and re-layouts  5.83 us (6%)
  between operations  1.82 us (2%)
    ppermute x12, waiting for transfers between devices, over_section(): return lax.ppermute(block, BOTH, pairs)  39.9 us
    ppermute x12, starting transfers between devices, over_section(): return lax.ppermute(block, BOTH, pairs)  13.4 us
    pallas_call x4, Pallas kernels, weight_grads(): call(kernel, [shape((1, width, columns))] * 2 + [TOKEN], flops=4 * count...  11.4 us
    pallas_call x1, Pallas kernels, hold_weights(): call(kernel, [shape(w_key.shape)] * 2 + [TOKEN], flops=1 << 34, moved=4 *...  5.93 us
    unnamed x16, local copies, waits for them, and re-layouts  5.79 us
    ppermute x8, starting transfers between devices, over_dp(): return lax.ppermute(block, BOTH, pairs)  5.7 us
    pallas_call x1, Pallas kernels, memory_part(): call(kernel, [shape((keep, depth), jnp.float32), shape((keep, depth + 2 *...  4.62 us
    pallas_call x1, Pallas kernels, attend(): call(kernel, [shape((count * rows, width))] * 2 + [shape((count, targets,...  4.25 us
  transfers between devices with their start and end apart: 21, of which 2 were waited for; matrix products, arithmetic and copies ran while one was open for 1% of the time, Pallas kernels for 20%

profile of v2, /device:TPU:12, one launch (start us, length us, event | category | flops | bytes accessed | tf_op | source)
XLA Modules:
  0.0 101.3 jit_solution(1254958933230017054)
XLA Ops:
  1.3 0.9 copy-done.1
  3.1 2.4 %collective-permute-start.1 = (bf16[32,4224]{1,0:T(8,128)(2,1)S(1)}, bf16[32,4224]{1,0:T(8,128)(2,1)S(1)}, u32[]{:S(2)}, u32[]{:S(2)}) collective-permute-start(bf16[32,4224]{1,0:T(8,128)(2,1)S(1)} %shard_map.110.refs_0_), channel_id=1, source_target_pairs={{12,8},{13,9},{14,10},{15,11}} | collective-permute-start | bytes 811016 | tf_op jit(solution)/shard_map/ppermute | solution.py:461
  5.6 1.7 %collective-permute-start = (bf16[32,4224]{1,0:T(8,128)(2,1)S(1)}, bf16[32,4224]{1,0:T(8,128)(2,1)S(1)}, u32[]{:S(2)}, u32[]{:S(2)}) collective-permute-start(bf16[32,4224]{1,0:T(8,128)(2,1)S(1)} %shard_map.110.refs_0_), channel_id=1, source_target_pairs={{12,20},{13,21},{14,22},{15,23}} | collective-permute-start | bytes 811016 | tf_op jit(solution)/shard_map/ppermute | solution.py:461
  7.4 1.2 %copy-done.3 = bf16[1,128,4096]{2,1,0:T(8,128)(2,1)S(1)} copy-done((bf16[1,128,4096]{2,1,0:T(8,128)(2,1)S(1)}, bf16[1,128,4096]{2,1,0:T(8,128)(2,1)}, u32[]{:S(2)}) %copy-start.3) | copy-done | bytes 1048600
  8.6 1.2 %copy-done.4 = bf16[1,128,4096]{2,1,0:T(8,128)(2,1)S(1)} copy-done((bf16[1,128,4096]{2,1,0:T(8,128)(2,1)S(1)}, bf16[1,128,4096]{2,1,0:T(8,128)(2,1)}, u32[]{:S(2)}) %copy-start.4) | copy-done | bytes 1048600
  11.4 1.6 %collective-permute-done.refs_0_ = bf16[32,4224]{1,0:T(8,128)(2,1)S(1)} collective-permute-done((bf16[32,4224]{1,0:T(8,128)(2,1)S(1)}, bf16[32,4224]{1,0:T(8,128)(2,1)S(1)}, u32[]{:S(2)}, u32[]{:S(2)}) %collective-permute-start) | collective-permute-done | bytes 270368 | tf_op jit(solution)/shard_map/ppermute | solution.py:461
  14.4 5.9 %shard_map.113 = (bf16[1,4096,1024]{2,1,0:T(8,128)(2,1)S(1)}, bf16[1,4096,1024]{2,1,0:T(8,128)(2,1)S(1)}, f32[8,128]{1,0:T(8,128)S(1)}) custom-call(bf16[1,4096,1024]{2,1,0:T(8,128)(2,1)} %wk_ref.1, bf16[1,4096,1024]{2,1,0:T(8,128)(2,1)} %wv_ref.1, bf16[32,4224]{1,0:T(8,128)(2,1)S(1)} %shard_map.112.refs_0_), custom_call_target="tpu_custom_call" | custom-call | flops 17179869184 | bytes 16777216 | tf_op jit(solution)/shard_map/pallas_call | solution.py:193
  24.0 4.2 %shard_map.115 = (bf16[128,1024]{1,0:T(8,128)(2,1)S(1)}, bf16[128,1024]{1,0:T(8,128)(2,1)S(1)}, bf16[4,128,1024]{2,1,0:T(8,128)(2,1)S(1)}) custom-call(s32[2]{0:T(128)S(1)} %pad_add_fusion.scalar_ref, bf16[32,4224]{1,0:T(8,128)(2,1)S(1)} %shard_map.114.refs_0_, bf16[32,4224]{1,0:T(8,128)(2,1)S(1)} %collective-permute-done.4.refs_1_, ...), custom_call_target="tpu_custom_call" | custom-call | flops 2315255808 | bytes 20971520 | tf_op jit(solution)/shard_map/pallas_call | solution.py:264
  28.3 4.6 %shard_map.116 = (f32[64,4096]{1,0:T(8,128)S(1)}, bf16[64,4352]{1,0:T(8,128)(2,1)S(1)}, f32[32,128]{1,0:T(8,128)S(1)}) custom-call(bf16[32,4224]{1,0:T(8,128)(2,1)S(1)} %shard_map.114.refs_0_, bf16[32,4224]{1,0:T(8,128)(2,1)S(1)} %collective-permute-done.4.refs_1_, bf16[32,4224]{1,0:T(8,128)(2,1)S(1)} %collective-permute-done.5.refs_2_, ...), custom_call_target="tpu_custom_call" | custom-call | flops 2147483648 | bytes 16777216 | tf_op jit(solution)/shard_map/pallas_call | solution.py:305
  33.7 0.9 collective-permute-start.11
  34.6 2.8 %shard_map.118 = (bf16[1,4096,1024]{2,1,0:T(8,128)(2,1)}, bf16[1,4096,1024]{2,1,0:T(8,128)(2,1)}, f32[8,128]{1,0:T(8,128)S(1)}) custom-call(bf16[32,4224]{1,0:T(8,128)(2,1)S(1)} %shard_map.114.refs_0_, bf16[32,4224]{1,0:T(8,128)(2,1)S(1)} %collective-permute-done.4.refs_1_, bf16[32,4224]{1,0:T(8,128)(2,1)S(1)} %collective-permute-done.5.refs_2_, ...), custom_call_target="tpu_custom_call" | custom-call | flops 536870912 | bytes 4194304 | tf_op jit(solution)/shard_map/pallas_call | solution.py:403
  37.4 2.9 %shard_map.119 = (bf16[1,4096,1024]{2,1,0:T(8,128)(2,1)}, bf16[1,4096,1024]{2,1,0:T(8,128)(2,1)}, f32[8,128]{1,0:T(8,128)S(1)}) custom-call(bf16[32,4224]{1,0:T(8,128)(2,1)S(1)} %shard_map.114.refs_0_, bf16[32,4224]{1,0:T(8,128)(2,1)S(1)} %collective-permute-done.4.refs_1_, ...), custom_call_target="tpu_custom_call", output_to_operand_aliasing={{0}: (7, {}), {1}: (8, {})} | custom-call | flops 536870912 | bytes 4194304 | tf_op jit(solution)/shard_map/pallas_call | solution.py:403
  40.3 2.9 %shard_map.120 = (bf16[1,4096,1024]{2,1,0:T(8,128)(2,1)}, bf16[1,4096,1024]{2,1,0:T(8,128)(2,1)}, f32[8,128]{1,0:T(8,128)S(1)}) custom-call(bf16[32,4224]{1,0:T(8,128)(2,1)S(1)} %shard_map.114.refs_0_, bf16[32,4224]{1,0:T(8,128)(2,1)S(1)} %collective-permute-done.4.refs_1_, ...), custom_call_target="tpu_custom_call", output_to_operand_aliasing={{0}: (7, {}), {1}: (8, {})} | custom-call | flops 536870912 | bytes 4194304 | tf_op jit(solution)/shard_map/pallas_call | solution.py:403
  44.0 1.0 copy-done
  44.9 3.5 %all-to-all-start = ((bf16[4,128,1024]{2,1,0:T(8,128)(2,1)}), bf16[4,128,1024]{2,1,0:T(8,128)(2,1)S(1)}, u32[]{:S(2)}, u32[]{:S(2)}) async-start(bf16[4,128,1024]{2,1,0:T(8,128)(2,1)} %copy-done), calls=%async_computation | async-start | bytes 2097152 | tf_op jit(solution)/shard_map/all_to_all | solution.py:525
  50.5 2.9 %shard_map.124 = (bf16[1,4096,1024]{2,1,0:T(8,128)(2,1)}, bf16[1,4096,1024]{2,1,0:T(8,128)(2,1)}, f32[8,128]{1,0:T(8,128)S(1)}) custom-call(bf16[32,4224]{1,0:T(8,128)(2,1)S(1)} %shard_map.114.refs_0_, bf16[32,4224]{1,0:T(8,128)(2,1)S(1)} %collective-permute-done.4.refs_1_, ...), custom_call_target="tpu_custom_call", output_to_operand_aliasing={{0}: (7, {}), {1}: (8, {})} | custom-call | flops 536870912 | bytes 4194304 | tf_op jit(solution)/shard_map/pallas_call | solution.py:403
  53.4 0.9 shard_map.125
  54.3 1.3 %collective-permute-start.16 = (bf16[32,4096]{1,0:T(8,128)(2,1)S(1)}, bf16[32,4096]{1,0:T(8,128)(2,1)S(1)}, u32[]{:S(2)}, u32[]{:S(2)}) collective-permute-start(bf16[32,4096]{1,0:T(8,128)(2,1)S(1)} %get-tuple-element.72), channel_id=1, source_target_pairs={{8,12},{9,13},{10,14},{11,15}} | collective-permute-start | bytes 786440 | tf_op jit(solution)/shard_map/ppermute | solution.py:461
  55.6 1.3 %collective-permute-start.15 = (bf16[32,4096]{1,0:T(8,128)(2,1)S(1)}, bf16[32,4096]{1,0:T(8,128)(2,1)S(1)}, u32[]{:S(2)}, u32[]{:S(2)}) collective-permute-start(bf16[32,4096]{1,0:T(8,128)(2,1)S(1)} %get-tuple-element.72), channel_id=1, source_target_pairs={{20,12},{21,13},{22,14},{23,15}} | collective-permute-start | bytes 786440 | tf_op jit(solution)/shard_map/ppermute | solution.py:461
  56.9 1.3 %collective-permute-start.19 = (f32[32,128]{1,0:T(8,128)S(1)}, f32[32,128]{1,0:T(8,128)S(1)}, u32[]{:S(2)}, u32[]{:S(2)}) collective-permute-start(f32[32,128]{1,0:T(8,128)S(1)} %add.12.refs_3_), channel_id=1, source_target_pairs={{16,8},{17,9},{18,10},{19,11},{20,12},{21,13},{22,14},{23,15},{24,... | collective-permute-start | bytes 49160 | tf_op jit(solution)/shard_map/ppermute | solution.py:461
  58.2 1.3 %collective-permute-start.18 = (f32[32,128]{1,0:T(8,128)S(1)}, f32[32,128]{1,0:T(8,128)S(1)}, u32[]{:S(2)}, u32[]{:S(2)}) collective-permute-start(f32[32,128]{1,0:T(8,128)S(1)} %add.12.refs_3_), channel_id=1, source_target_pairs={{16,0},{17,1},{18,2},{19,3},{20,4},{21,5},{22,6},{23,7},{24,8},{25... | collective-permute-start | bytes 49160 | tf_op jit(solution)/shard_map/ppermute | solution.py:461
  60.2 38.2 %collective-permute-done.19 = f32[32,128]{1,0:T(8,128)S(1)} collective-permute-done((f32[32,128]{1,0:T(8,128)S(1)}, f32[32,128]{1,0:T(8,128)S(1)}, u32[]{:S(2)}, u32[]{:S(2)}) %collective-permute-start.19) | collective-permute-done | bytes 16416 | tf_op jit(solution)/shard_map/ppermute | solution.py:461
  99.1 1.1 %shard_map.126 = bf16[1,32,4096]{2,1,0:T(8,128)(2,1)} custom-call(s32[1]{0:T(128)} %bitcast.3.flag_ref, bf16[1,32,4096]{2,1,0:T(8,128)(2,1)S(1)} %copy-done.2, f32[1,4096]{1,0:T(1,128)S(1)} %bitcast.8, bf16[32,4096]{1,0:T(8,128)(2,1)S(1)} %collective-permute-done.15.refs_0_, bf16[32,4096]{1,0:T(8,128)(2,1)S(1)} %collective-permute-done.16.refs_1_), custom_call_target="tpu_custom_call" | custom-call | bytes 1048576 | tf_op jit(solution)/shard_map/pallas_call | solution.py:430
  100.1 1.0 shard_map.123
  (55 shorter events, 12.4 us)
Async XLA Ops:
  3.1 8.3 %collective-permute-start.1 = (bf16[32,4224]{1,0:T(8,128)(2,1)S(1)}, bf16[32,4224]{1,0:T(8,128)(2,1)S(1)}, u32[]{:S(2)}, u32[]{:S(2)}) collective-permute-start(bf16[32,4224]{1,0:T(8,128)(2,1)S(1)} %shard_map.110.refs_0_), channel_id=1, source_target_pairs={{12,8},{13,9},{14,10},{15,11}} | collective-permute-start | bytes 811016 | tf_op jit(solution)/shard_map/ppermute | solution.py:461
  5.6 7.5 %collective-permute-start = (bf16[32,4224]{1,0:T(8,128)(2,1)S(1)}, bf16[32,4224]{1,0:T(8,128)(2,1)S(1)}, u32[]{:S(2)}, u32[]{:S(2)}) collective-permute-start(bf16[32,4224]{1,0:T(8,128)(2,1)S(1)} %shard_map.110.refs_0_), channel_id=1, source_target_pairs={{12,20},{13,21},{14,22},{15,23}} | collective-permute-start | bytes 811016 | tf_op jit(solution)/shard_map/ppermute | solution.py:461
  7.4 1.2 %copy-start.3 = (bf16[1,128,4096]{2,1,0:T(8,128)(2,1)S(1)}, bf16[1,128,4096]{2,1,0:T(8,128)(2,1)}, u32[]{:S(2)}) copy-start(bf16[1,128,4096]{2,1,0:T(8,128)(2,1)} %query_ref.1) | copy-start | bytes 3145732
  10.7 11.2 %collective-permute-start.7 = (bf16[2,2,128,1024]{3,2,1,0:T(8,128)(2,1)S(1)}, bf16[2,2,128,1024]{3,2,1,0:T(8,128)(2,1)S(1)}, u32[]{:S(2)}, u32[]{:S(2)}) collective-permute-start(bf16[2,2,128,1024]{3,2,1,0:T(8,128)(2,1)S(1)} %get-tuple-element.44), channel_id=1, source_target_pairs={{16,18},{17,19},{18,16},{19,17},{20,22},{21,23},{22,20},{23,21},{2... | collective-permute-start | bytes 3145736 | tf_op jit(solution)/shard_map/ppermute | solution.py:457
  13.1 7.3 %collective-permute-start.3 = (bf16[32,4224]{1,0:T(8,128)(2,1)S(1)}, bf16[32,4224]{1,0:T(8,128)(2,1)S(1)}, u32[]{:S(2)}, u32[]{:S(2)}) collective-permute-start(bf16[32,4224]{1,0:T(8,128)(2,1)S(1)} %shard_map.112.refs_0_), channel_id=1, source_target_pairs={{20,16},{21,17},{22,18},{23,19}} | collective-permute-start | bytes 811016 | tf_op jit(solution)/shard_map/ppermute | solution.py:461
  13.7 6.6 %collective-permute-start.2 = (bf16[32,4224]{1,0:T(8,128)(2,1)S(1)}, bf16[32,4224]{1,0:T(8,128)(2,1)S(1)}, u32[]{:S(2)}, u32[]{:S(2)}) collective-permute-start(bf16[32,4224]{1,0:T(8,128)(2,1)S(1)} %shard_map.112.refs_0_), channel_id=1, source_target_pairs={{20,28},{21,29},{22,30},{23,31},{8,24},{9,25},{10,26},{11,27}} | collective-permute-start | bytes 811016 | tf_op jit(solution)/shard_map/ppermute | solution.py:461
  20.4 2.8 %collective-permute-start.4 = (bf16[32,4224]{1,0:T(8,128)(2,1)S(1)}, bf16[32,4224]{1,0:T(8,128)(2,1)S(1)}, u32[]{:S(2)}, u32[]{:S(2)}) collective-permute-start(bf16[32,4224]{1,0:T(8,128)(2,1)S(1)} %shard_map.114.refs_0_), channel_id=1, source_target_pairs={{16,18},{17,19},{18,16},{19,17},{20,22},{21,23},{22,20},{23,21},{2... | collective-permute-start | bytes 811016 | tf_op jit(solution)/shard_map/ppermute | solution.py:457
  21.1 2.8 %collective-permute-start.8 = (bf16[1,2,128,1024]{3,2,1,0:T(8,128)(2,1)S(1)}, bf16[1,2,128,1024]{3,2,1,0:T(8,128)(2,1)S(1)}, u32[]{:S(2)}, u32[]{:S(2)}) collective-permute-start(bf16[1,2,128,1024]{3,2,1,0:T(8,128)(2,1)S(1)} %get-tuple-element.45), channel_id=1, source_target_pairs={{16,17},{17,16},{18,19},{19,18},{20,21},{21,20},{22,23},{23,22},{2... | collective-permute-start | bytes 1572872 | tf_op jit(solution)/shard_map/ppermute | solution.py:457
  21.9 2.1 %collective-permute-start.9 = (bf16[1,2,128,1024]{3,2,1,0:T(8,128)(2,1)S(1)}, bf16[1,2,128,1024]{3,2,1,0:T(8,128)(2,1)S(1)}, u32[]{:S(2)}, u32[]{:S(2)}) collective-permute-start(bf16[1,2,128,1024]{3,2,1,0:T(8,128)(2,1)S(1)} %slice.4), channel_id=1, source_target_pairs={{16,17},{17,16},{18,19},{19,18},{20,21},{21,20},{22,23},{23,22},{2... | collective-permute-start | bytes 1572872 | tf_op jit(solution)/shard_map/ppermute | solution.py:457
  22.6 1.4 %collective-permute-start.5 = (bf16[32,4224]{1,0:T(8,128)(2,1)S(1)}, bf16[32,4224]{1,0:T(8,128)(2,1)S(1)}, u32[]{:S(2)}, u32[]{:S(2)}) collective-permute-start(bf16[32,4224]{1,0:T(8,128)(2,1)S(1)} %shard_map.114.refs_0_), channel_id=1, source_target_pairs={{16,17},{17,16},{18,19},{19,18},{20,21},{21,20},{22,23},{23,22},{2... | collective-permute-start | bytes 811016 | tf_op jit(solution)/shard_map/ppermute | solution.py:457
  23.3 0.7 collective-permute-start.6
  24.0 4.3 %copy-start.6 = (f32[4096]{0:T(1024)S(1)}, f32[4096]{0:T(1024)}, u32[]{:S(2)}) copy-start(f32[4096]{0:T(1024)} %param.8) | copy-start | bytes 49156
  32.9 0.7 collective-permute-start.10
  33.7 9.4 %collective-permute-start.11 = (bf16[32,4352]{1,0:T(8,128)(2,1)S(1)}, bf16[32,4352]{1,0:T(8,128)(2,1)S(1)}, u32[]{:S(2)}, u32[]{:S(2)}) collective-permute-start(bf16[32,4352]{1,0:T(8,128)(2,1)S(1)} %get-tuple-element.53), channel_id=1, source_target_pairs={{16,18},{17,19},{18,16},{19,17},{20,22},{21,23},{22,20},{23,21},{2... | collective-permute-start | bytes 835592 | tf_op jit(solution)/shard_map/ppermute | solution.py:457
  44.9 55.2 %all-to-all-start = ((bf16[4,128,1024]{2,1,0:T(8,128)(2,1)}), bf16[4,128,1024]{2,1,0:T(8,128)(2,1)S(1)}, u32[]{:S(2)}, u32[]{:S(2)}) async-start(bf16[4,128,1024]{2,1,0:T(8,128)(2,1)} %copy-done), calls=%async_computation | async-start | bytes 2097152 | tf_op jit(solution)/shard_map/all_to_all | solution.py:525
  48.5 5.0 %collective-permute-start.13 = (bf16[32,4096]{1,0:T(8,128)(2,1)}, bf16[32,4096]{1,0:T(8,128)(2,1)S(1)}, u32[]{:S(2)}, u32[]{:S(2)}) collective-permute-start(bf16[32,4096]{1,0:T(8,128)(2,1)} %copy-done.7), channel_id=1, source_target_pairs={{16,20},{17,21},{18,22},{19,23}} | collective-permute-start | bytes 786440 | tf_op jit(solution)/shard_map/ppermute | solution.py:461
  49.1 4.3 %collective-permute-start.12 = (bf16[32,4096]{1,0:T(8,128)(2,1)}, bf16[32,4096]{1,0:T(8,128)(2,1)S(1)}, u32[]{:S(2)}, u32[]{:S(2)}) collective-permute-start(bf16[32,4096]{1,0:T(8,128)(2,1)} %copy-done.7), channel_id=1, source_target_pairs={{28,20},{29,21},{30,22},{31,23},{24,8},{25,9},{26,10},{27,11}} | collective-permute-start | bytes 786440 | tf_op jit(solution)/shard_map/ppermute | solution.py:461
  49.8 3.6 %collective-permute-start.14 = (f32[32,128]{1,0:T(8,128)S(1)}, f32[32,128]{1,0:T(8,128)S(1)}, u32[]{:S(2)}, u32[]{:S(2)}) collective-permute-start(f32[32,128]{1,0:T(8,128)S(1)} %get-tuple-element.71), channel_id=1, source_target_pairs={{16,20},{17,21},{18,22},{19,23},{20,16},{21,17},{22,18},{23,19},{2... | collective-permute-start | bytes 49160 | tf_op jit(solution)/shard_map/ppermute | solution.py:461
  50.5 48.6 %copy-start.2 = (bf16[1,32,4096]{2,1,0:T(8,128)(2,1)S(1)}, bf16[1,32,4096]{2,1,0:T(8,128)(2,1)}, u32[]{:S(2)}) copy-start(bf16[1,32,4096]{2,1,0:T(8,128)(2,1)} %enc_ref.3) | copy-start | bytes 786436
  54.3 44.7 %collective-permute-start.16 = (bf16[32,4096]{1,0:T(8,128)(2,1)S(1)}, bf16[32,4096]{1,0:T(8,128)(2,1)S(1)}, u32[]{:S(2)}, u32[]{:S(2)}) collective-permute-start(bf16[32,4096]{1,0:T(8,128)(2,1)S(1)} %get-tuple-element.72), channel_id=1, source_target_pairs={{8,12},{9,13},{10,14},{11,15}} | collective-permute-start | bytes 786440 | tf_op jit(solution)/shard_map/ppermute | solution.py:461
  55.6 43.5 %collective-permute-start.15 = (bf16[32,4096]{1,0:T(8,128)(2,1)S(1)}, bf16[32,4096]{1,0:T(8,128)(2,1)S(1)}, u32[]{:S(2)}, u32[]{:S(2)}) collective-permute-start(bf16[32,4096]{1,0:T(8,128)(2,1)S(1)} %get-tuple-element.72), channel_id=1, source_target_pairs={{20,12},{21,13},{22,14},{23,15}} | collective-permute-start | bytes 786440 | tf_op jit(solution)/shard_map/ppermute | solution.py:461
  56.9 41.5 %collective-permute-start.19 = (f32[32,128]{1,0:T(8,128)S(1)}, f32[32,128]{1,0:T(8,128)S(1)}, u32[]{:S(2)}, u32[]{:S(2)}) collective-permute-start(f32[32,128]{1,0:T(8,128)S(1)} %add.12.refs_3_), channel_id=1, source_target_pairs={{16,8},{17,9},{18,10},{19,11},{20,12},{21,13},{22,14},{23,15},{24,... | collective-permute-start | bytes 49160 | tf_op jit(solution)/shard_map/ppermute | solution.py:461
  58.2 40.2 %collective-permute-start.18 = (f32[32,128]{1,0:T(8,128)S(1)}, f32[32,128]{1,0:T(8,128)S(1)}, u32[]{:S(2)}, u32[]{:S(2)}) collective-permute-start(f32[32,128]{1,0:T(8,128)S(1)} %add.12.refs_3_), channel_id=1, source_target_pairs={{16,0},{17,1},{18,2},{19,3},{20,4},{21,5},{22,6},{23,7},{24,8},{25... | collective-permute-start | bytes 49160 | tf_op jit(solution)/shard_map/ppermute | solution.py:461
  59.5 38.9 %collective-permute-start.17 = (f32[32,128]{1,0:T(8,128)S(1)}, f32[32,128]{1,0:T(8,128)S(1)}, u32[]{:S(2)}, u32[]{:S(2)}) collective-permute-start(f32[32,128]{1,0:T(8,128)S(1)} %add.12.refs_3_), channel_id=1, source_target_pairs={{16,24},{17,25},{18,26},{19,27},{20,28},{21,29},{22,30},{23,31},{2... | collective-permute-start | bytes 49160 | tf_op jit(solution)/shard_map/ppermute | solution.py:461
  (5 other events, 4.6 us)

commit v3 on v2

v3 whole, which is shorter than its diff:
```python
import jax
import jax.numpy as jnp
from jax import lax
from jax.experimental import pallas as pl
from jax.experimental.pallas import tpu as pltpu
from jax.sharding import PartitionSpec as P

HEAD_DIM = 256
epsilon = 1e-06
BOTH = ("section", "dp")
LANES = 128
TILE = 1024
VMEM_BEGIN = 54
COST_HOLD = 1 << 32
COST_SUM = 1 << 32


def section_rounds(sections):
    half = sections // 2
    source = half - 1
    first = min(half + 1, sections - 1)
    held = {source, first}
    rounds = [[(source, first)]]
    if source > 0 and half + 2 < sections:
        rounds[0].append((source, source - 1))
        held.add(source - 1)
    stage = []
    for a, b in ((first, first + 2), (source - 1, source + 3), (first, first - 1)):
        if a in held and half <= b < sections and b not in held:
            stage.append((a, b))
            held.add(b)
    if stage:
        rounds.append(stage)
    while not held.issuperset(range(half, sections)):
        have = [s for s in sorted(held) if s >= half]
        stage = []
        for a in have:
            b = a + len(have)
            if b < sections and b not in held:
                stage.append((a, b))
                held.add(b)
        rounds.append(stage)
    return rounds


def split_pairs(stage):
    groups = []
    for a, b in stage:
        for group in groups:
            if all(a != c and b != e for c, e in group):
                group.append((a, b))
                break
        else:
            groups.append([(a, b)])
    return groups


def call(kernel, out_shape, flops=0, moved=0, vmem=16, **options):
    return pl.pallas_call(
        kernel,
        out_shape=out_shape,
        compiler_params=pltpu.CompilerParams(vmem_limit_bytes=vmem << 20),
        cost_estimate=pl.CostEstimate(flops=flops, bytes_accessed=moved, transcendentals=0),
        **options,
    )


def shape(dims, dtype=jnp.bfloat16):
    return jax.ShapeDtypeStruct(dims, dtype)


def dot(a, b, dims=((1,), (0,))):
    return lax.dot_general(a, b, (dims, ((), ())), preferred_element_type=jnp.float32)


SMEM = pl.BlockSpec(memory_space=pltpu.SMEM)
VMEM = pl.BlockSpec(memory_space=pltpu.VMEM)
ANY = pl.BlockSpec(memory_space=pl.ANY)
TOKEN = shape((8, LANES), jnp.float32)


def mark(token_ref):
    token_ref[...] = jnp.zeros_like(token_ref)


def begin(enc_state, gain, queries, ctx_grad, replicas):
    rows, width = enc_state.shape[1:]
    targets = queries.shape[1]
    piece = width // replicas
    half = replicas // 2

    def kernel(enc_ref, gain_ref, query_ref, grad_ref, out_ref, far_ref, held, held_gain, sems, far_sems):
        first = [
            pltpu.make_async_copy(enc_ref.at[0], held, sems.at[0]),
            pltpu.make_async_copy(gain_ref, held_gain, sems.at[1]),
        ]
        for copy in first:
            copy.start()
        index = lax.axis_index("dp")
        copies = []
        for i in range(half):
            columns = pl.ds(pl.multiple_of((index ^ (half + i)) * piece, piece), piece)
            for j, ref in enumerate((query_ref, grad_ref)):
                place = far_ref.at[i, j]
                copy = pltpu.make_async_copy(ref.at[0, :, columns], place, far_sems.at[i, j])
                copy.start()
                copies.append(copy)
        for copy in first:
            copy.wait()
        state = held[...].astype(jnp.float32)
        inverse = lax.rsqrt(jnp.mean(state * state, axis=1, keepdims=True) + epsilon)
        out_ref[...] = (state * inverse * held_gain[...]).astype(jnp.bfloat16)
        for copy in copies:
            copy.wait()

    return call(
        kernel,
        [shape((rows, width)), shape((half, 2, targets, piece))],
        moved=4 * rows * width + 4 * targets * width,
        vmem=VMEM_BEGIN,
        in_specs=[ANY] * 4,
        out_specs=[VMEM] * 2,
        scratch_shapes=[
            pltpu.VMEM((rows, width), jnp.bfloat16),
            pltpu.VMEM((1, width), jnp.float32),
            pltpu.SemaphoreType.DMA((2,)),
            pltpu.SemaphoreType.DMA((half, 2)),
        ],
    )(enc_state, gain, queries, ctx_grad)


def split_heads(queries, ctx_grad, groups, replicas, tokens):
    rows, width = queries.shape[1:]
    piece = width // replicas
    count = sum(len(group) for group in groups)

    def kernel(query_ref, grad_ref, *refs):
        *out_refs, token_ref, sems = refs[len(tokens) :]
        index = lax.axis_index("dp")
        copies = []
        for group, out_ref in zip(groups, out_refs, strict=True):
            for i, k in enumerate(group):
                columns = pl.ds(pl.multiple_of((index ^ k) * piece, piece), piece)
                for j, ref in enumerate((query_ref, grad_ref)):
                    sem = sems.at[len(copies)]
                    copy = pltpu.make_async_copy(ref.at[0, :, columns], out_ref.at[i, j], sem)
                    copy.start()
                    copies.append(copy)
        mark(token_ref)
        for copy in copies:
            copy.wait()

    *shares, token = call(
        kernel,
        [shape((len(group), 2, rows, piece)) for group in groups] + [TOKEN],
        moved=8 * rows * width,
        in_specs=[ANY] * (2 + len(tokens)),
        out_specs=[VMEM] * (len(groups) + 1),
        scratch_shapes=[pltpu.SemaphoreType.DMA((2 * count,))],
    )(queries, ctx_grad, *tokens)
    return shares, token


def add_blocks(blocks, tokens=(), mem_len=None):
    rows, width = blocks[0].shape
    assert rows <= 256
    scalars = [] if mem_len is None else [mem_len]

    def kernel(*refs):
        total = refs[0][...]
        for ref in refs[1 : len(blocks)]:
            total = total + ref[...]
        out_ref = refs[-1]
        out_ref[:, :width] = total
        if scalars:
            columns = jnp.full((rows, LANES), refs[len(blocks)][0].astype(jnp.float32))
            out_ref[:, width:] = columns.astype(jnp.bfloat16)

    return call(
        kernel,
        shape((rows, width + LANES * len(scalars))),
        moved=8 * blocks[0].size,
        in_specs=[VMEM] * len(blocks) + [SMEM] * len(scalars) + [ANY] * len(tokens),
        out_specs=VMEM,
    )(*blocks, *scalars, *tokens)


def stack_rows(first, second, tokens):
    rows, width = first.shape

    def kernel(first_ref, second_ref, *refs):
        out_ref = refs[-1]
        out_ref[:rows] = first_ref[...]
        out_ref[rows:] = second_ref[...]

    return call(
        kernel,
        shape((2 * rows, width)),
        moved=8 * first.size,
        in_specs=[VMEM] * 2 + [ANY] * len(tokens),
        out_specs=VMEM,
    )(first, second, *tokens)


def join_heads(shares):
    replicas, rows, piece = shares.shape

    def kernel(share_ref, out_ref, token_ref, sems):
        copies = []
        for k in range(replicas):
            columns = pl.ds(k * piece, piece)
            copy = pltpu.make_async_copy(share_ref.at[k], out_ref.at[0, :, columns], sems.at[k])
            copy.start()
            copies.append(copy)
        mark(token_ref)
        for copy in copies:
            copy.wait()

    return call(
        kernel,
        [shape((1, rows, replicas * piece)), TOKEN],
        moved=4 * rows * replicas * piece,
        in_specs=[VMEM],
        out_specs=[ANY, VMEM],
        scratch_shapes=[pltpu.SemaphoreType.DMA((replicas,))],
    )(shares)


def hold_weights(w_key, w_value, tokens):
    steps = 4
    step = w_key.shape[1] // steps

    def kernel(wk_ref, wv_ref, *refs):
        *out_refs, token_ref, sems = refs[len(tokens) :]
        copies = []
        for i in range(steps):
            rows = pl.ds(i * step, step)
            for j, (ref, out_ref) in enumerate(zip((wk_ref, wv_ref), out_refs, strict=True)):
                copy = pltpu.make_async_copy(ref.at[0, rows], out_ref.at[0, rows], sems.at[i, j])
                copy.start()
                copies.append(copy)
        mark(token_ref)
        for copy in copies:
            copy.wait()

    *held, token = call(
        kernel,
        [shape(w_key.shape)] * 2 + [TOKEN],
        flops=COST_HOLD,
        moved=4 * w_key.size,
        vmem=36,
        in_specs=[ANY] * (2 + len(tokens)),
        out_specs=[ANY, ANY, VMEM],
        scratch_shapes=[pltpu.SemaphoreType.DMA((steps, 2))],
    )(w_key, w_value, *tokens)
    return held, token


def follow(block, tokens):
    def kernel(*refs):
        del refs

    return call(
        kernel,
        shape(block.shape, block.dtype),
        in_specs=[ANY] * (1 + len(tokens)),
        out_specs=ANY,
        input_output_aliases={0: 0},
    )(block, *tokens)


def project(memory, w_key, w_value):
    rows = memory.shape[0]
    depth, width = w_key.shape[1:]

    def kernel(memory_ref, wk_ref, wv_ref, key_ref, value_ref):
        key_ref[...] = dot(memory_ref[:, :depth], wk_ref[0]).astype(jnp.bfloat16)
        value_ref[...] = dot(memory_ref[:, :depth], wv_ref[0]).astype(jnp.bfloat16)

    return call(
        kernel,
        [shape((rows, width))] * 2,
        flops=4 * rows * depth * width,
        moved=4 * depth * width,
        in_specs=[VMEM] * 3,
        out_specs=[VMEM] * 2,
    )(memory, w_key, w_value)


def attend(memory, keys, values, shares, order, half):
    count = len(shares)
    rows = memory.shape[0] // count
    depth = memory.shape[1] - LANES
    width = keys.shape[1]
    targets = shares[0].shape[2]
    scale = HEAD_DIM ** (-0.5)
    heads = width // HEAD_DIM

    def kernel(memory_ref, key_ref, value_ref, *refs):
        share_refs = refs[:count]
        dk_ref, dv_ref, dq_ref, score_ref, grad_ref, low_ref = refs[count:]
        index = lax.axis_index("dp")
        blocks = []
        for h in range(heads):
            for p, k in enumerate(order):
                head, own = slice(h * HEAD_DIM, (h + 1) * HEAD_DIM), slice(p * rows, (p + 1) * rows)
                blocks.append((head, own, index ^ k, share_refs[p]))
        for i, (head, own, _, share_ref) in enumerate(blocks):
            query, grad = share_ref[0, 0, :, head], share_ref[0, 1, :, head]
            score_ref[i] = dot(key_ref[own, head], query, ((1,), (1,)))
            grad_ref[i] = dot(value_ref[own, head], grad, ((1,), (1,)))
        token = lax.broadcasted_iota(jnp.int32, (rows, targets), 0).astype(jnp.float32)
        firsts = [memory_ref[p * rows : p * rows + 1, depth : depth + 1] for p in range(count)]
        valid = jnp.stack([token < first.astype(jnp.float32) for first in firsts])
        for h in range(heads):
            here = slice(h * count, (h + 1) * count)
            scores = jnp.where(valid, score_ref[here] * scale, -1e30)
            exponent = jnp.exp(scores - jnp.max(scores, axis=1, keepdims=True))
            probs = exponent / jnp.sum(exponent, axis=1, keepdims=True)
            grad_probs = grad_ref[here]
            delta = jnp.sum(probs * grad_probs, axis=1, keepdims=True)
            low_ref[0, here] = (probs * (grad_probs - delta) * scale).astype(jnp.bfloat16)
            low_ref[1, here] = probs.astype(jnp.bfloat16)
        is_decoder = (lax.axis_index("section") >= half).astype(jnp.float32)
        for i, (head, own, place, share_ref) in enumerate(blocks):
            query, grad = share_ref[0, 0, :, head], share_ref[0, 1, :, head]
            dk_ref[own, head] = dot(low_ref[0, i], query).astype(jnp.bfloat16)
            dv_ref[own, head] = (dot(low_ref[1, i], grad) * is_decoder).astype(jnp.bfloat16)
            dq = dot(low_ref[0, i], key_ref[own, head], ((0,), (0,)))
            dq_ref[place, :, head] = dq.astype(jnp.bfloat16)

    scores = (heads * count, rows, targets)
    return call(
        kernel,
        [shape((count * rows, width))] * 2 + [shape((count, targets, width))],
        flops=10 * count * rows * targets * width,
        moved=8 * count * targets * width,
        in_specs=[VMEM] * (count + 3),
        out_specs=[VMEM] * 3,
        scratch_shapes=[
            *[pltpu.VMEM(scores, jnp.float32)] * 2,
            pltpu.VMEM((2, *scores), jnp.bfloat16),
        ],
    )(memory, keys, values, *shares)


def memory_part(memory, w_key, w_value, dk, dv, gain):
    rows = memory.shape[0]
    depth, width = w_key.shape[1:]
    tile = 512
    steps = depth // tile
    keep = rows // 2

    def kernel(memory_ref, dk_ref, dv_ref, wk_ref, wv_ref, gain_ref, keep_ref, sent_ref, out_ref):
        for f in range(steps):
            here = slice(f * tile, (f + 1) * tile)
            part = dot(wk_ref[0, here, :], dk_ref[...], ((1,), (1,)))
            part = (part + dot(wv_ref[0, here, :], dv_ref[...], ((1,), (1,)))).T
            keep_ref[:, here] = part[:keep]
            sent_ref[:, here] = part[keep:].astype(jnp.bfloat16)
            terms = part * memory_ref[:, here].astype(jnp.float32)
            total = jnp.sum(terms, axis=0, keepdims=True) / gain_ref[:, here]
            for i in range(tile // LANES):
                place = (f * tile) // LANES + i
                out_ref[place : place + 1, :] = total[:, i * LANES : (i + 1) * LANES]
        put_gain(out_ref[...], sent_ref)

    return call(
        kernel,
        [
            shape((keep, depth), jnp.float32),
            shape((keep, depth + 2 * LANES)),
            shape((depth // LANES, LANES), jnp.float32),
        ],
        flops=4 * rows * depth * width,
        moved=4 * depth * width,
        in_specs=[VMEM] * 6,
        out_specs=[VMEM] * 3,
    )(memory, dk, dv, w_key, w_value, gain)


def put_gain(gain, sent_ref):
    rows = gain.shape[0]
    depth = sent_ref.shape[1] - 2 * LANES
    assert sent_ref.shape[0] >= rows
    high = gain.astype(jnp.bfloat16)
    if sent_ref.shape[0] > rows:
        sent_ref[rows:, depth:] = jnp.zeros((sent_ref.shape[0] - rows, 2 * LANES), jnp.bfloat16)
    sent_ref[:rows, depth : depth + LANES] = high
    sent_ref[:rows, depth + LANES :] = (gain - high.astype(jnp.float32)).astype(jnp.bfloat16)


def add_share(kept, came, gain, last, tokens=()):
    rows, depth = kept.shape
    half = rows if last else rows // 2

    def kernel(kept_ref, came_ref, gain_ref, *refs):
        sent_ref, out_ref, *more_refs = refs[len(tokens) :]
        out = gain_ref.shape[0]
        came_gain = came_ref[:out, depth:].astype(jnp.float32)
        total_gain = gain_ref[...] + (came_gain[:, :LANES] + came_gain[:, LANES:])
        out_ref[...] = total_gain
        total = kept_ref[:half] + came_ref[:half, :depth].astype(jnp.float32)
        if last:
            sent_ref[...] = total.astype(jnp.bfloat16)
        else:
            keep_ref, token_ref = more_refs
            keep_ref[...] = total
            other = kept_ref[half:] + came_ref[half:, :depth].astype(jnp.float32)
            sent_ref[:, :depth] = other.astype(jnp.bfloat16)
            put_gain(total_gain, sent_ref)
            mark(token_ref)

    more = [] if last else [shape((half, depth), jnp.float32), TOKEN]
    return call(
        kernel,
        [
            shape((half, depth + (0 if last else 2 * LANES))),
            shape(gain.shape, jnp.float32),
            *more,
        ],
        moved=10 * rows * depth,
        in_specs=[VMEM] * 3 + [ANY] * len(tokens),
        out_specs=[VMEM] * (2 + len(more)),
    )(kept, came, gain, *tokens)


def add_sections(own, came, gain):
    count = len(came)

    def kernel(own_ref, *refs):
        gain_ref = refs[count]
        out_ref, gain_out_ref = refs[-2:]
        total = own_ref[...].astype(jnp.float32)
        for ref in refs[:count]:
            total = total + ref[...].astype(jnp.float32)
        out_ref[...] = total.astype(jnp.bfloat16)
        gain_out_ref[...] = gain_ref[...]

    return call(
        kernel,
        [shape(own.shape), shape(gain.shape, jnp.float32)],
        flops=COST_SUM,
        moved=6 * own.size,
        in_specs=[VMEM] * (2 + count),
        out_specs=[VMEM] * 2,
    )(own, *came, gain)


def add_gains(terms, token):
    def kernel(own_ref, other_ref, first_ref, second_ref, _, out_ref):
        out_ref[...] = (own_ref[...] + other_ref[...]) + (first_ref[...] + second_ref[...])

    return call(
        kernel,
        shape(terms[0].shape, jnp.float32),
        in_specs=[VMEM] * 4 + [ANY],
        out_specs=VMEM,
    )(*terms, token)


def weight_grads(memory, width, first, last, dk, dv, before, tokens=()):
    rows = memory.shape[0]
    columns = dk.shape[1]
    tile = TILE

    def kernel(memory_ref, dk_ref, dv_ref, *refs):
        key_ref, value_ref, token_ref = refs[-3:]
        key_ref[0] = dot(memory_ref[...], dk_ref[...], ((0,), (0,))).astype(jnp.bfloat16)
        value_ref[0] = dot(memory_ref[...], dv_ref[...], ((0,), (0,))).astype(jnp.bfloat16)
        mark(token_ref)

    piece = pl.BlockSpec((rows, tile), lambda f: (0, first + f))
    whole = pl.BlockSpec((rows, columns), lambda f: (0, 0))
    out = pl.BlockSpec((1, tile, columns), lambda f: (0, first + f, 0))
    inputs = 3 + len(tokens)
    *grads, token = call(
        kernel,
        [shape((1, width, columns))] * 2 + [TOKEN],
        flops=4 * rows * tile * columns * (last - first),
        moved=4 * tile * columns * (last - first),
        grid=(last - first,),
        in_specs=[piece, whole, whole] + [ANY] * (len(tokens) + len(before)),
        out_specs=[out] * 2 + [pl.BlockSpec(TOKEN.shape, lambda f: (0, 0))],
        vmem=24,
        input_output_aliases={inputs + i: i for i in range(len(before))},
    )(memory, dk, dv, *tokens, *before)
    return grads, token


def finish(holder, enc_state, gain, terms, tokens):
    rows, width = enc_state.shape[1:]

    def kernel(enc_ref, gain_ref, *refs):
        state = enc_ref[0].astype(jnp.float32)
        inverse = lax.rsqrt(jnp.mean(state * state, axis=1, keepdims=True) + epsilon)
        normed = state * inverse
        own = [ref[...].astype(jnp.float32) for ref in refs[: len(terms)]]
        scaled = sum(own[1:], own[0]) * gain_ref[...]
        mean = jnp.mean(scaled * normed, axis=1, keepdims=True)
        grad = inverse * (scaled - normed * mean)
        is_holder = lax.axis_index("section") == holder
        refs[-2][0] = jnp.where(is_holder, grad, 0.0).astype(jnp.bfloat16)
        mark(refs[-1])

    return call(
        kernel,
        [shape((1, rows, width)), TOKEN],
        moved=8 * rows * width,
        in_specs=[VMEM] * (2 + len(terms)) + [ANY] * len(tokens),
        out_specs=[VMEM] * 2,
    )(enc_state, gain, *terms, *tokens)


def on_device(enc_state, final_gain, queries, w_key, w_value, ctx_grad, mem_len):
    sections = lax.axis_size("section")
    replicas = lax.axis_size("dp")
    half = sections // 2
    bits = replicas.bit_length() - 1
    assert replicas == 1 << bits and half & (half - 1) == 0 and half > 1 and bits > 1
    gain = final_gain[None]

    def over_dp(block, k):
        pairs = [
            (s * replicas + d, s * replicas + (d ^ k))
            for s in range(half, sections)
            for d in range(replicas)
        ]
        return lax.ppermute(block, BOTH, pairs)

    def over_section(block, pairs):
        pairs = [(a * replicas + d, b * replicas + d) for a, b in pairs for d in range(replicas)]
        return lax.ppermute(block, BOTH, pairs)

    order = [0]
    for bit in reversed(range(bits)):
        order = order + [k ^ (1 << bit) for k in order]
    rounds = section_rounds(sections)

    memory, far = begin(enc_state, gain, queries, ctx_grad, replicas)
    came_far = over_dp(far, replicas // 2)
    groups = [[k for k in range(1 << bit, 2 << bit)] for bit in reversed(range(bits - 1))]
    near, split = split_heads(queries, ctx_grad, [*groups, [0]], replicas, [])
    came = [over_section(memory, group) for group in split_pairs(rounds[0])]
    arrived = [came[0]]
    holding = add_blocks(came, [split])
    weights, held = hold_weights(w_key, w_value, [holding])
    for stage in rounds[1:]:
        arrived += [over_section(holding, group) for group in split_pairs(stage)]
        length = mem_len if stage is rounds[-1] else None
        holding = add_blocks(arrived, [held], length)
    blocks, tokens = {replicas // 2: came_far}, []
    for bit, share in zip(reversed(range(bits - 1)), near, strict=False):
        size = 1 << bit
        passed = {k ^ size: over_dp(b[size : 2 * size], size) for k, b in blocks.items()}
        blocks = blocks | passed | {size: over_dp(share, size)}
        tokens.append(blocks[size])
    blocks[0] = near[-1]
    shares = [blocks[k] for k in order]
    for bit in reversed(range(bits)):
        holding = stack_rows(holding, over_dp(holding, 1 << bit), tokens)
        tokens = []
    pieces = holding
    keys, values = project(pieces, *weights)
    dk, dv, dq = attend(pieces, keys, values, shares, order, half)

    kept, sent, gain_part = memory_part(pieces, *weights, dk, dv, gain)
    width = enc_state.shape[2]
    decoders = range(half, sections)
    token = None
    for bit in range(bits):
        last = bit == bits - 1
        came = over_dp(sent, 1 << bit)
        tokens = []
        if last:
            grads, done = weight_grads(pieces, width, 0, width // TILE, dk, dv, [], [token])
            tokens = [done]
        sent, gain_part, *more = add_share(kept, came, gain_part, last, tokens)
        if not last:
            kept, token = more
    key_weight_grad, value_weight_grad = grads
    dq = follow(dq, [gain_part])
    step = half // 2
    while step > 1:
        gain_part = gain_part + over_section(gain_part, [(s, s ^ step) for s in decoders])
        step //= 2
    for number, stage in reversed(list(enumerate(rounds))):
        came = [over_section(sent, [(b, a) for a, b in group]) for group in split_pairs(stage)]
        if number:
            sent, gain_part = add_sections(sent, came, gain_part)
    terms = [
        gain_part,
        over_section(gain_part, [(s, s ^ step) for s in decoders]),
        over_section(gain_part, [(s, s - half) for s in decoders]),
        over_section(gain_part, [(s, (s ^ step) - half) for s in decoders]),
    ]

    query_grad, joined = join_heads(
        lax.all_to_all(dq, "dp", split_axis=0, concat_axis=0, tiled=True)
    )
    state_grad, done = finish(half - 1, enc_state, gain, came, [joined])
    gain_grad = add_gains(terms, done).reshape(width)
    return (query_grad, key_weight_grad, value_weight_grad, state_grad, gain_grad)


def solution(mesh):
    placed = (
        P("section", "dp", None),
        P(),
        P("section", "dp", None),
        P("section", None, "dp"),
        P("section", None, "dp"),
        P("section", "dp", None),
        P("dp"),
    )
    return jax.shard_map(
        on_device,
        mesh=mesh,
        in_specs=placed,
        out_specs=(
            P("section", "dp", None),
            P("section", None, "dp"),
            P("section", None, "dp"),
            P("section", "dp", None),
            P(),
        ),
        check_vma=False,
    )
```

time: 103 us -> 94.7 us (0.919)
  the two profiles are of different devices: /device:TPU:12 before, /device:TPU:0 now
where the time goes in v3:
time: 94.7 us; the launch traced here: 94 us
  waiting for transfers between devices  43.7 us (46%)
  Pallas kernels  27.7 us (29%)
  starting transfers between devices  18.4 us (19%)
  local copies, waits for them, and re-layouts  2.49 us (3%)
  between operations  1.69 us (2%)
    ppermute x12, waiting for transfers between devices, over_section(): return lax.ppermute(block, BOTH, pairs)  34.6 us
    ppermute x12, starting transfers between devices, over_section(): return lax.ppermute(block, BOTH, pairs)  9.32 us
    all_to_all x1, waiting for transfers between devices, on_device(): lax.all_to_all(dq, 'dp', split_axis=0, concat_axis=0, tiled=True)  9 us
    pallas_call x1, Pallas kernels, weight_grads(): call(kernel, [shape((1, width, columns))] * 2 + [TOKEN], flops=4 * rows *...  6.88 us
    pallas_call x1, Pallas kernels, hold_weights(): call(kernel, [shape(w_key.shape)] * 2 + [TOKEN], flops=COST_HOLD, moved=4...  5.93 us
    ppermute x7, starting transfers between devices, over_dp(): return lax.ppermute(block, BOTH, pairs)  4.86 us
    pallas_call x1, Pallas kernels, memory_part(): call(kernel, [shape((keep, depth), jnp.float32), shape((keep, depth + 2 *...  4.6 us
    all_to_all x1, starting transfers between devices, on_device(): lax.all_to_all(dq, 'dp', split_axis=0, concat_axis=0, tiled=True)  4.22 us
  transfers between devices with their start and end apart: 20, of which 2 were waited for; matrix products, arithmetic and copies ran while one was open for 0% of the time, Pallas kernels for 19%

profile of v3, /device:TPU:0, one launch (start us, length us, event | category | flops | bytes accessed | tf_op | source)
XLA Modules:
  0.0 94.0 jit_solution(4139604715020025622)
XLA Ops:
  0.6 2.4 %shard_map.110 = (bf16[32,4096]{1,0:T(8,128)(2,1)}, bf16[2,2,128,1024]{3,2,1,0:T(8,128)(2,1)}) custom-call(bf16[1,32,4096]{2,1,0:T(8,128)(2,1)} %enc_ref.3, f32[1,4096]{1,0:T(1,128)} %bitcast.2, bf16[1,128,4096]{2,1,0:T(8,128)(2,1)} %query_ref.3, bf16[1,128,4096]{2,1,0:T(8,128)(2,1)} %grad_ref.3), custom_call_target="tpu_custom_call" | custom-call | bytes 2621440 | tf_op jit(solution)/shard_map/pallas_call | solution.py:116
  3.0 0.7 collective-permute-start.1
  4.4 0.7 collective-permute-start.7
  5.2 1.2 %copy-done = bf16[1,128,4096]{2,1,0:T(8,128)(2,1)S(1)} copy-done((bf16[1,128,4096]{2,1,0:T(8,128)(2,1)S(1)}, bf16[1,128,4096]{2,1,0:T(8,128)(2,1)}, u32[]{:S(2)}) %copy-start) | copy-done | bytes 1048600
  6.4 1.2 %copy-done.1 = bf16[1,128,4096]{2,1,0:T(8,128)(2,1)S(1)} copy-done((bf16[1,128,4096]{2,1,0:T(8,128)(2,1)S(1)}, bf16[1,128,4096]{2,1,0:T(8,128)(2,1)}, u32[]{:S(2)}) %copy-start.1) | copy-done | bytes 1048600
  7.7 0.7 collective-permute-start.5
  10.5 5.9 %shard_map.113 = (bf16[1,4096,1024]{2,1,0:T(8,128)(2,1)S(1)}, bf16[1,4096,1024]{2,1,0:T(8,128)(2,1)S(1)}, f32[8,128]{1,0:T(8,128)S(1)}) custom-call(bf16[1,4096,1024]{2,1,0:T(8,128)(2,1)} %wk_ref.1, bf16[1,4096,1024]{2,1,0:T(8,128)(2,1)} %wv_ref.1, bf16[32,4096]{1,0:T(8,128)(2,1)S(1)} %shard_map.112.refs_0_), custom_call_target="tpu_custom_call" | custom-call | flops 4294967296 | bytes 16777216 | tf_op jit(solution)/shard_map/pallas_call | solution.py:246
  16.5 0.7 collective-permute-start.4
  17.3 0.7 collective-permute-start.6
  18.0 0.7 collective-permute-start.8
  18.8 2.3 %shard_map.117 = (bf16[128,1024]{1,0:T(8,128)(2,1)S(1)}, bf16[128,1024]{1,0:T(8,128)(2,1)S(1)}) custom-call(bf16[128,4224]{1,0:T(8,128)(2,1)S(1)} %shard_map.116.memory_ref, bf16[1,4096,1024]{2,1,0:T(8,128)(2,1)S(1)} %get-tuple-element.40.wk_ref, bf16[1,4096,1024]{2,1,0:T(8,128)(2,1)S(1)} %get-tuple-element.41.wv_ref), custom_call_target="tpu_custom_call" | custom-call | flops 2147483648 | bytes 16777216 | tf_op jit(solution)/shard_map/pallas_call | solution.py:280
  21.2 2.4 %shard_map.118 = (bf16[128,1024]{1,0:T(8,128)(2,1)S(1)}, bf16[128,1024]{1,0:T(8,128)(2,1)S(1)}, bf16[4,128,1024]{2,1,0:T(8,128)(2,1)}) custom-call(bf16[128,4224]{1,0:T(8,128)(2,1)S(1)} %shard_map.116.memory_ref, bf16[128,1024]{1,0:T(8,128)(2,1)S(1)} %get-tuple-element.42.key_ref, bf16[128,1024]{1,0:T(8,128)(2,1)S(1)} %get-tuple-element.43.value_ref, ...), custom_call_target="tpu_custom_call" | custom-call | flops 167772160 | bytes 4194304 | tf_op jit(solution)/shard_map/pallas_call | solution.py:333
  23.6 4.6 %shard_map.119 = (f32[64,4096]{1,0:T(8,128)S(1)}, bf16[64,4352]{1,0:T(8,128)(2,1)S(1)}, f32[32,128]{1,0:T(8,128)S(1)}) custom-call(bf16[128,4224]{1,0:T(8,128)(2,1)S(1)} %shard_map.116.memory_ref, bf16[128,1024]{1,0:T(8,128)(2,1)S(1)} %get-tuple-element.47.dk_ref, bf16[128,1024]{1,0:T(8,128)(2,1)S(1)} %get-tuple-element.48.dv_ref, ...), custom_call_target="tpu_custom_call" | custom-call | flops 2147483648 | bytes 16777216 | tf_op jit(solution)/shard_map/pallas_call | solution.py:368
  28.2 0.7 collective-permute-start.9
  29.0 0.7 collective-permute-start.10
  29.7 6.9 %shard_map.121 = (bf16[1,4096,1024]{2,1,0:T(8,128)(2,1)}, bf16[1,4096,1024]{2,1,0:T(8,128)(2,1)}, f32[8,128]{1,0:T(8,128)S(1)}) custom-call(bf16[128,4224]{1,0:T(8,128)(2,1)S(1)} %shard_map.116.memory_ref, bf16[128,1024]{1,0:T(8,128)(2,1)S(1)} %get-tuple-element.47.dk_ref, bf16[128,1024]{1,0:T(8,128)(2,1)S(1)} %get-tuple-element.48.dv_ref, ...), custom_call_target="tpu_custom_call" | custom-call | flops 2147483648 | bytes 16777216 | tf_op jit(solution)/shard_map/pallas_call | solution.py:477
  38.0 4.2 %all-to-all-start = ((bf16[4,128,1024]{2,1,0:T(8,128)(2,1)}), bf16[4,128,1024]{2,1,0:T(8,128)(2,1)S(1)}, u32[]{:S(2)}, u32[]{:S(2)}) async-start(bf16[4,128,1024]{2,1,0:T(8,128)(2,1)} %shard_map.123), calls=%async_computation | async-start | bytes 2097152 | tf_op jit(solution)/shard_map/all_to_all | solution.py:599
  43.7 0.7 collective-permute-start.14
  44.4 1.3 %collective-permute-start.18 = (f32[32,128]{1,0:T(8,128)S(1)}, f32[32,128]{1,0:T(8,128)S(1)}, u32[]{:S(2)}, u32[]{:S(2)}) collective-permute-start(f32[32,128]{1,0:T(8,128)S(1)} %get-tuple-element.65.own_ref), channel_id=1, source_target_pairs={{16,4},{17,5},{18,6},{19,7},{20,0},{21,1},{22,2},{23,3},{24,12},{2... | collective-permute-start | bytes 49160 | tf_op jit(solution)/shard_map/ppermute | solution.py:533
  45.7 1.3 %collective-permute-start.17 = (f32[32,128]{1,0:T(8,128)S(1)}, f32[32,128]{1,0:T(8,128)S(1)}, u32[]{:S(2)}, u32[]{:S(2)}) collective-permute-start(f32[32,128]{1,0:T(8,128)S(1)} %get-tuple-element.65.own_ref), channel_id=1, source_target_pairs={{16,0},{17,1},{18,2},{19,3},{20,4},{21,5},{22,6},{23,7},{24,8},{25... | collective-permute-start | bytes 49160 | tf_op jit(solution)/shard_map/ppermute | solution.py:533
  47.7 9.0 %all-to-all-done.share_ref = bf16[4,128,1024]{2,1,0:T(8,128)(2,1)S(1)} async-done(((bf16[4,128,1024]{2,1,0:T(8,128)(2,1)}), bf16[4,128,1024]{2,1,0:T(8,128)(2,1)S(1)}, u32[]{:S(2)}, u32[]{:S(2)}) %all-to-all-start) | async-done | bytes 1048608 | tf_op jit(solution)/shard_map/all_to_all | solution.py:599
  56.7 1.0 %shard_map.124 = (bf16[1,128,4096]{2,1,0:T(8,128)(2,1)}, f32[8,128]{1,0:T(8,128)S(1)}) custom-call(bf16[4,128,1024]{2,1,0:T(8,128)(2,1)S(1)} %all-to-all-done.share_ref), custom_call_target="tpu_custom_call" | custom-call | bytes 2097152 | tf_op jit(solution)/shard_map/pallas_call | solution.py:219
  57.7 1.1 %shard_map.126 = (bf16[1,32,4096]{2,1,0:T(8,128)(2,1)}, f32[8,128]{1,0:T(8,128)S(1)}) custom-call(bf16[1,32,4096]{2,1,0:T(8,128)(2,1)S(1)} %copy-done.2, f32[1,4096]{1,0:T(1,128)S(1)} %bitcast.4, bf16[32,4096]{1,0:T(8,128)(2,1)S(1)} %collective-permute-done.14.refs_0_, bf16[32,4096]{1,0:T(8,128)(2,1)S(1)} %collective-permute-done.15.refs_1_, ...), custom_call_target="tpu_custom_call" | custom-call | bytes 1048576 | tf_op jit(solution)/shard_map/pallas_call | solution.py:506
  58.8 34.6 %collective-permute-done.18.second_ref = f32[32,128]{1,0:T(8,128)S(1)} collective-permute-done((f32[32,128]{1,0:T(8,128)S(1)}, f32[32,128]{1,0:T(8,128)S(1)}, u32[]{:S(2)}, u32[]{:S(2)}) %collective-permute-start.18) | collective-permute-done | bytes 16416 | tf_op jit(solution)/shard_map/ppermute | solution.py:533
  (44 shorter events, 6.7 us)
Async XLA Ops:
  3.0 6.0 %collective-permute-start.1 = (bf16[32,4096]{1,0:T(8,128)(2,1)}, bf16[32,4096]{1,0:T(8,128)(2,1)S(1)}, u32[]{:S(2)}, u32[]{:S(2)}) collective-permute-start(bf16[32,4096]{1,0:T(8,128)(2,1)} %get-tuple-element.36), channel_id=1, source_target_pairs={{12,8},{13,9},{14,10},{15,11}} | collective-permute-start | bytes 786440 | tf_op jit(solution)/shard_map/ppermute | solution.py:533
  3.7 5.4 %collective-permute-start = (bf16[32,4096]{1,0:T(8,128)(2,1)}, bf16[32,4096]{1,0:T(8,128)(2,1)S(1)}, u32[]{:S(2)}, u32[]{:S(2)}) collective-permute-start(bf16[32,4096]{1,0:T(8,128)(2,1)} %get-tuple-element.36), channel_id=1, source_target_pairs={{12,20},{13,21},{14,22},{15,23}} | collective-permute-start | bytes 786440 | tf_op jit(solution)/shard_map/ppermute | solution.py:533
  4.4 13.6 %collective-permute-start.7 = (bf16[2,2,128,1024]{3,2,1,0:T(8,128)(2,1)}, bf16[2,2,128,1024]{3,2,1,0:T(8,128)(2,1)S(1)}, u32[]{:S(2)}, u32[]{:S(2)}) collective-permute-start(bf16[2,2,128,1024]{3,2,1,0:T(8,128)(2,1)} %get-tuple-element.45), channel_id=1, source_target_pairs={{16,18},{17,19},{18,16},{19,17},{20,22},{21,23},{22,20},{23,21},{2... | collective-permute-start | bytes 3145736 | tf_op jit(solution)/shard_map/ppermute | solution.py:529
  5.1 1.2 %copy-start = (bf16[1,128,4096]{2,1,0:T(8,128)(2,1)S(1)}, bf16[1,128,4096]{2,1,0:T(8,128)(2,1)}, u32[]{:S(2)}) copy-start(bf16[1,128,4096]{2,1,0:T(8,128)(2,1)} %query_ref.3) | copy-start | bytes 3145732
  6.4 1.2 %copy-start.1 = (bf16[1,128,4096]{2,1,0:T(8,128)(2,1)S(1)}, bf16[1,128,4096]{2,1,0:T(8,128)(2,1)}, u32[]{:S(2)}) copy-start(bf16[1,128,4096]{2,1,0:T(8,128)(2,1)} %grad_ref.3) | copy-start | bytes 3145732
  7.7 9.5 %collective-permute-start.5 = (bf16[1,2,128,1024]{3,2,1,0:T(8,128)(2,1)S(1)}, bf16[1,2,128,1024]{3,2,1,0:T(8,128)(2,1)S(1)}, u32[]{:S(2)}, u32[]{:S(2)}) collective-permute-start(bf16[1,2,128,1024]{3,2,1,0:T(8,128)(2,1)S(1)} %get-tuple-element.39), channel_id=1, source_target_pairs={{16,17},{17,16},{18,19},{19,18},{20,21},{21,20},{22,23},{23,22},{2... | collective-permute-start | bytes 1572872 | tf_op jit(solution)/shard_map/ppermute | solution.py:529
  9.1 7.3 %collective-permute-start.3 = (bf16[32,4096]{1,0:T(8,128)(2,1)S(1)}, bf16[32,4096]{1,0:T(8,128)(2,1)S(1)}, u32[]{:S(2)}, u32[]{:S(2)}) collective-permute-start(bf16[32,4096]{1,0:T(8,128)(2,1)S(1)} %shard_map.112.refs_0_), channel_id=1, source_target_pairs={{20,16},{21,17},{22,18},{23,19}} | collective-permute-start | bytes 786440 | tf_op jit(solution)/shard_map/ppermute | solution.py:533
  9.8 6.6 %collective-permute-start.2 = (bf16[32,4096]{1,0:T(8,128)(2,1)S(1)}, bf16[32,4096]{1,0:T(8,128)(2,1)S(1)}, u32[]{:S(2)}, u32[]{:S(2)}) collective-permute-start(bf16[32,4096]{1,0:T(8,128)(2,1)S(1)} %shard_map.112.refs_0_), channel_id=1, source_target_pairs={{20,28},{21,29},{22,30},{23,31},{8,24},{9,25},{10,26},{11,27}} | collective-permute-start | bytes 786440 | tf_op jit(solution)/shard_map/ppermute | solution.py:533
  16.5 0.7 collective-permute-start.4
  17.3 1.5 %collective-permute-start.6 = (bf16[64,4224]{1,0:T(8,128)(2,1)S(1)}, bf16[64,4224]{1,0:T(8,128)(2,1)S(1)}, u32[]{:S(2)}, u32[]{:S(2)}) collective-permute-start(bf16[64,4224]{1,0:T(8,128)(2,1)S(1)} %shard_map.115.first_ref), channel_id=1, source_target_pairs={{16,17},{17,16},{18,19},{19,18},{20,21},{21,20},{22,23},{23,22},{2... | collective-permute-start | bytes 1622024 | tf_op jit(solution)/shard_map/ppermute | solution.py:529
  18.0 3.2 %collective-permute-start.8 = (bf16[1,2,128,1024]{3,2,1,0:T(8,128)(2,1)S(1)}, bf16[1,2,128,1024]{3,2,1,0:T(8,128)(2,1)S(1)}, u32[]{:S(2)}, u32[]{:S(2)}) collective-permute-start(bf16[1,2,128,1024]{3,2,1,0:T(8,128)(2,1)S(1)} %slice.4), channel_id=1, source_target_pairs={{16,17},{17,16},{18,19},{19,18},{20,21},{21,20},{22,23},{23,22},{2... | collective-permute-start | bytes 1572872 | tf_op jit(solution)/shard_map/ppermute | solution.py:529
  18.8 4.8 %copy-start.3 = (f32[4096]{0:T(1024)S(1)}, f32[4096]{0:T(1024)}, u32[]{:S(2)}) copy-start(f32[4096]{0:T(1024)} %param.8) | copy-start | bytes 49156
  28.2 0.7 collective-permute-start.9
  29.0 7.6 %collective-permute-start.10 = (bf16[32,4352]{1,0:T(8,128)(2,1)S(1)}, bf16[32,4352]{1,0:T(8,128)(2,1)S(1)}, u32[]{:S(2)}, u32[]{:S(2)}) collective-permute-start(bf16[32,4352]{1,0:T(8,128)(2,1)S(1)} %get-tuple-element.53), channel_id=1, source_target_pairs={{16,18},{17,19},{18,16},{19,17},{20,22},{21,23},{22,20},{23,21},{2... | collective-permute-start | bytes 835592 | tf_op jit(solution)/shard_map/ppermute | solution.py:529
  36.6 6.3 %collective-permute-start.12 = (bf16[32,4096]{1,0:T(8,128)(2,1)S(1)}, bf16[32,4096]{1,0:T(8,128)(2,1)S(1)}, u32[]{:S(2)}, u32[]{:S(2)}) collective-permute-start(bf16[32,4096]{1,0:T(8,128)(2,1)S(1)} %get-tuple-element.61.own_ref), channel_id=1, source_target_pairs={{16,20},{17,21},{18,22},{19,23}} | collective-permute-start | bytes 786440 | tf_op jit(solution)/shard_map/ppermute | solution.py:533
  37.3 5.6 %collective-permute-start.11 = (bf16[32,4096]{1,0:T(8,128)(2,1)S(1)}, bf16[32,4096]{1,0:T(8,128)(2,1)S(1)}, u32[]{:S(2)}, u32[]{:S(2)}) collective-permute-start(bf16[32,4096]{1,0:T(8,128)(2,1)S(1)} %get-tuple-element.61.own_ref), channel_id=1, source_target_pairs={{28,20},{29,21},{30,22},{31,23},{24,8},{25,9},{26,10},{27,11}} | collective-permute-start | bytes 786440 | tf_op jit(solution)/shard_map/ppermute | solution.py:533
  38.0 18.7 %all-to-all-start = ((bf16[4,128,1024]{2,1,0:T(8,128)(2,1)}), bf16[4,128,1024]{2,1,0:T(8,128)(2,1)S(1)}, u32[]{:S(2)}, u32[]{:S(2)}) async-start(bf16[4,128,1024]{2,1,0:T(8,128)(2,1)} %shard_map.123), calls=%async_computation | async-start | bytes 2097152 | tf_op jit(solution)/shard_map/all_to_all | solution.py:599
  42.2 0.7 collective-permute-start.13
  42.9 14.8 %copy-start.2 = (bf16[1,32,4096]{2,1,0:T(8,128)(2,1)S(1)}, bf16[1,32,4096]{2,1,0:T(8,128)(2,1)}, u32[]{:S(2)}) copy-start(bf16[1,32,4096]{2,1,0:T(8,128)(2,1)} %enc_ref.3) | copy-start | bytes 786436
  43.0 14.6 %collective-permute-start.15 = (bf16[32,4096]{1,0:T(8,128)(2,1)S(1)}, bf16[32,4096]{1,0:T(8,128)(2,1)S(1)}, u32[]{:S(2)}, u32[]{:S(2)}) collective-permute-start(bf16[32,4096]{1,0:T(8,128)(2,1)S(1)} %get-tuple-element.62), channel_id=1, source_target_pairs={{8,12},{9,13},{10,14},{11,15}} | collective-permute-start | bytes 786440 | tf_op jit(solution)/shard_map/ppermute | solution.py:533
  43.7 14.0 %collective-permute-start.14 = (bf16[32,4096]{1,0:T(8,128)(2,1)S(1)}, bf16[32,4096]{1,0:T(8,128)(2,1)S(1)}, u32[]{:S(2)}, u32[]{:S(2)}) collective-permute-start(bf16[32,4096]{1,0:T(8,128)(2,1)S(1)} %get-tuple-element.62), channel_id=1, source_target_pairs={{20,12},{21,13},{22,14},{23,15}} | collective-permute-start | bytes 786440 | tf_op jit(solution)/shard_map/ppermute | solution.py:533
  44.4 49.0 %collective-permute-start.18 = (f32[32,128]{1,0:T(8,128)S(1)}, f32[32,128]{1,0:T(8,128)S(1)}, u32[]{:S(2)}, u32[]{:S(2)}) collective-permute-start(f32[32,128]{1,0:T(8,128)S(1)} %get-tuple-element.65.own_ref), channel_id=1, source_target_pairs={{16,4},{17,5},{18,6},{19,7},{20,0},{21,1},{22,2},{23,3},{24,12},{2... | collective-permute-start | bytes 49160 | tf_op jit(solution)/shard_map/ppermute | solution.py:533
  45.7 47.7 %collective-permute-start.17 = (f32[32,128]{1,0:T(8,128)S(1)}, f32[32,128]{1,0:T(8,128)S(1)}, u32[]{:S(2)}, u32[]{:S(2)}) collective-permute-start(f32[32,128]{1,0:T(8,128)S(1)} %get-tuple-element.65.own_ref), channel_id=1, source_target_pairs={{16,0},{17,1},{18,2},{19,3},{20,4},{21,5},{22,6},{23,7},{24,8},{25... | collective-permute-start | bytes 49160 | tf_op jit(solution)/shard_map/ppermute | solution.py:533
  47.0 46.4 %collective-permute-start.16 = (f32[32,128]{1,0:T(8,128)S(1)}, f32[32,128]{1,0:T(8,128)S(1)}, u32[]{:S(2)}, u32[]{:S(2)}) collective-permute-start(f32[32,128]{1,0:T(8,128)S(1)} %get-tuple-element.65.own_ref), channel_id=1, source_target_pairs={{16,20},{17,21},{18,22},{19,23},{20,16},{21,17},{22,18},{23,19},{2... | collective-permute-start | bytes 49160 | tf_op jit(solution)/shard_map/ppermute | solution.py:533

commit v4 on v3

--- a/solution.py
+++ b/solution.py
@@ -11,7 +11,7 @@
 LANES = 128
 TILE = 1024
 VMEM_BEGIN = 54
-COST_HOLD = 1 << 32
+COST_HOLD = 1 << 30
 COST_SUM = 1 << 32
 
 
@@ -89,7 +89,9 @@
     piece = width // replicas
     half = replicas // 2
 
-    def kernel(enc_ref, gain_ref, query_ref, grad_ref, out_ref, far_ref, held, held_gain, sems, far_sems):
+    def kernel(enc_ref, gain_ref, query_ref, grad_ref, *refs):
+        out_ref, far_ref, token_ref, held, held_gain, sems, far_sems = refs
+        mark(token_ref)
         first = [
             pltpu.make_async_copy(enc_ref.at[0], held, sems.at[0]),
             pltpu.make_async_copy(gain_ref, held_gain, sems.at[1]),
@@ -115,11 +117,11 @@
 
     return call(
         kernel,
-        [shape((rows, width)), shape((half, 2, targets, piece))],
+        [shape((rows, width)), shape((half, 2, targets, piece)), TOKEN],
         moved=4 * rows * width + 4 * targets * width,
         vmem=VMEM_BEGIN,
         in_specs=[ANY] * 4,
-        out_specs=[VMEM] * 2,
+        out_specs=[VMEM] * 3,
         scratch_shapes=[
             pltpu.VMEM((rows, width), jnp.bfloat16),
             pltpu.VMEM((1, width), jnp.float32),
@@ -256,19 +258,6 @@
     return held, token
 
 
-def follow(block, tokens):
-    def kernel(*refs):
-        del refs
-
-    return call(
-        kernel,
-        shape(block.shape, block.dtype),
-        in_specs=[ANY] * (1 + len(tokens)),
-        out_specs=ANY,
-        input_output_aliases={0: 0},
-    )(block, *tokens)
-
-
 def project(memory, w_key, w_value):
     rows = memory.shape[0]
     depth, width = w_key.shape[1:]
@@ -287,7 +276,7 @@
     )(memory, w_key, w_value)
 
 
-def attend(memory, keys, values, shares, order, half):
+def attend(memory, keys, values, shares, half):
     count = len(shares)
     rows = memory.shape[0] // count
     depth = memory.shape[1] - LANES
@@ -298,14 +287,13 @@
 
     def kernel(memory_ref, key_ref, value_ref, *refs):
         share_refs = refs[:count]
-        dk_ref, dv_ref, dq_ref, score_ref, grad_ref, low_ref = refs[count:]
-        index = lax.axis_index("dp")
+        dk_ref, dv_ref, low_ref, score_ref, grad_ref = refs[count:]
         blocks = []
         for h in range(heads):
-            for p, k in enumerate(order):
+            for p in range(count):
                 head, own = slice(h * HEAD_DIM, (h + 1) * HEAD_DIM), slice(p * rows, (p + 1) * rows)
-                blocks.append((head, own, index ^ k, share_refs[p]))
-        for i, (head, own, _, share_ref) in enumerate(blocks):
+                blocks.append((head, own, share_refs[p]))
+        for i, (head, own, share_ref) in enumerate(blocks):
             query, grad = share_ref[0, 0, :, head], share_ref[0, 1, :, head]
             score_ref[i] = dot(key_ref[own, head], query, ((1,), (1,)))
             grad_ref[i] = dot(value_ref[own, head], grad, ((1,), (1,)))
@@ -322,26 +310,49 @@
             low_ref[0, here] = (probs * (grad_probs - delta) * scale).astype(jnp.bfloat16)
             low_ref[1, here] = probs.astype(jnp.bfloat16)
         is_decoder = (lax.axis_index("section") >= half).astype(jnp.float32)
-        for i, (head, own, place, share_ref) in enumerate(blocks):
+        for i, (head, own, share_ref) in enumerate(blocks):
             query, grad = share_ref[0, 0, :, head], share_ref[0, 1, :, head]
             dk_ref[own, head] = dot(low_ref[0, i], query).astype(jnp.bfloat16)
             dv_ref[own, head] = (dot(low_ref[1, i], grad) * is_decoder).astype(jnp.bfloat16)
-            dq = dot(low_ref[0, i], key_ref[own, head], ((0,), (0,)))
-            dq_ref[place, :, head] = dq.astype(jnp.bfloat16)
 
     scores = (heads * count, rows, targets)
     return call(
         kernel,
-        [shape((count * rows, width))] * 2 + [shape((count, targets, width))],
-        flops=10 * count * rows * targets * width,
+        [shape((count * rows, width))] * 2 + [shape((2, *scores))],
+        flops=8 * count * rows * targets * width,
         moved=8 * count * targets * width,
         in_specs=[VMEM] * (count + 3),
         out_specs=[VMEM] * 3,
         scratch_shapes=[
             *[pltpu.VMEM(scores, jnp.float32)] * 2,
-            pltpu.VMEM((2, *scores), jnp.bfloat16),
         ],
     )(memory, keys, values, *shares)
+
+
+def query_grads(scores, keys, order, tokens):
+    count = len(order)
+    rows = keys.shape[0] // count
+    width = keys.shape[1]
+    targets = scores.shape[3]
+
+    def kernel(score_ref, key_ref, *refs):
+        out_ref = refs[-1]
+        index = lax.axis_index("dp")
+        for h in range(width // HEAD_DIM):
+            head = slice(h * HEAD_DIM, (h + 1) * HEAD_DIM)
+            for p, k in enumerate(order):
+                key = key_ref[p * rows : (p + 1) * rows, head]
+                grad = dot(score_ref[0, h * count + p], key, ((0,), (0,)))
+                out_ref[index ^ k, :, head] = grad.astype(jnp.bfloat16)
+
+    return call(
+        kernel,
+        shape((count, targets, width)),
+        flops=2 * count * rows * targets * width,
+        moved=4 * count * targets * width,
+        in_specs=[VMEM] * 2 + [ANY] * len(tokens),
+        out_specs=VMEM,
+    )(scores, keys, *tokens)
 
 
 def memory_part(memory, w_key, w_value, dk, dv, gain):
@@ -537,18 +548,18 @@
         order = order + [k ^ (1 << bit) for k in order]
     rounds = section_rounds(sections)
 
-    memory, far = begin(enc_state, gain, queries, ctx_grad, replicas)
+    memory, far, begun = begin(enc_state, gain, queries, ctx_grad, replicas)
     came_far = over_dp(far, replicas // 2)
     groups = [[k for k in range(1 << bit, 2 << bit)] for bit in reversed(range(bits - 1))]
-    near, split = split_heads(queries, ctx_grad, [*groups, [0]], replicas, [])
     came = [over_section(memory, group) for group in split_pairs(rounds[0])]
     arrived = [came[0]]
-    holding = add_blocks(came, [split])
-    weights, held = hold_weights(w_key, w_value, [holding])
+    weights, held = hold_weights(w_key, w_value, [begun])
+    holding = add_blocks(came, [held])
+    near, split = split_heads(queries, ctx_grad, [*groups, [0]], replicas, [holding])
     for stage in rounds[1:]:
         arrived += [over_section(holding, group) for group in split_pairs(stage)]
         length = mem_len if stage is rounds[-1] else None
-        holding = add_blocks(arrived, [held], length)
+        holding = add_blocks(arrived, [split], length)
     blocks, tokens = {replicas // 2: came_far}, []
     for bit, share in zip(reversed(range(bits - 1)), near, strict=False):
         size = 1 << bit
@@ -562,7 +573,7 @@
         tokens = []
     pieces = holding
     keys, values = project(pieces, *weights)
-    dk, dv, dq = attend(pieces, keys, values, shares, order, half)
+    dk, dv, scores = attend(pieces, keys, values, shares, half)
 
     kept, sent, gain_part = memory_part(pieces, *weights, dk, dv, gain)
     width = enc_state.shape[2]
@@ -579,20 +590,21 @@
         if not last:
             kept, token = more
     key_weight_grad, value_weight_grad = grads
-    dq = follow(dq, [gain_part])
-    step = half // 2
-    while step > 1:
+    dq = query_grads(scores, keys, order, [gain_part])
+    step = 1
+    while step < half // 2:
         gain_part = gain_part + over_section(gain_part, [(s, s ^ step) for s in decoders])
-        step //= 2
+        step *= 2
     for number, stage in reversed(list(enumerate(rounds))):
         came = [over_section(sent, [(b, a) for a, b in group]) for group in split_pairs(stage)]
         if number:
             sent, gain_part = add_sections(sent, came, gain_part)
+    places = [(i % step) * 2 + i // step for i in range(half)]
     terms = [
         gain_part,
         over_section(gain_part, [(s, s ^ step) for s in decoders]),
-        over_section(gain_part, [(s, s - half) for s in decoders]),
-        over_section(gain_part, [(s, (s ^ step) - half) for s in decoders]),
+        over_section(gain_part, [(half + i, places[i]) for i in range(half)]),
+        over_section(gain_part, [(half + i, places[i ^ step]) for i in range(half)]),
     ]
 
     query_grad, joined = join_heads(

time: 94.7 us -> 90.3 us (0.954)
  the two profiles are of different devices: /device:TPU:0 before, /device:TPU:12 now
where the time goes in v4:
time: 90.3 us; the launch traced here: 89.2 us
  waiting for transfers between devices  34.1 us (38%)
  Pallas kernels  28.2 us (31%)
  starting transfers between devices  24.4 us (27%)
  between operations  1.71 us (2%)
    ppermute x12, waiting for transfers between devices, over_section(): return lax.ppermute(block, BOTH, pairs)  26.4 us
    ppermute x12, starting transfers between devices, over_section(): return lax.ppermute(block, BOTH, pairs)  16 us
    all_to_all x1, waiting for transfers between devices, on_device(): lax.all_to_all(dq, 'dp', split_axis=0, concat_axis=0, tiled=True)  7.73 us
    pallas_call x1, Pallas kernels, weight_grads(): call(kernel, [shape((1, width, columns))] * 2 + [TOKEN], flops=4 * rows *...  6.88 us
    pallas_call x1, Pallas kernels, hold_weights(): call(kernel, [shape(w_key.shape)] * 2 + [TOKEN], flops=COST_HOLD, moved=4...  6.06 us
    ppermute x7, starting transfers between devices, over_dp(): return lax.ppermute(block, BOTH, pairs)  4.86 us
    pallas_call x1, Pallas kernels, memory_part(): call(kernel, [shape((keep, depth), jnp.float32), shape((keep, depth + 2 *...  4.66 us
    all_to_all x1, starting transfers between devices, on_device(): lax.all_to_all(dq, 'dp', split_axis=0, concat_axis=0, tiled=True)  3.52 us
  transfers between devices with their start and end apart: 20, of which 3 were waited for; matrix products, arithmetic and copies ran while one was open for 0% of the time, Pallas kernels for 22%

profile of v4, /device:TPU:12, one launch (start us, length us, event | category | flops | bytes accessed | tf_op | source)
XLA Modules:
  0.0 89.2 jit_solution(3977559105406400890)
XLA Ops:
  0.6 2.4 %shard_map.110 = (bf16[32,4096]{1,0:T(8,128)(2,1)}, bf16[2,2,128,1024]{3,2,1,0:T(8,128)(2,1)}, f32[8,128]{1,0:T(8,128)}) custom-call(bf16[1,32,4096]{2,1,0:T(8,128)(2,1)} %enc_ref.3, f32[1,4096]{1,0:T(1,128)} %bitcast.2, bf16[1,128,4096]{2,1,0:T(8,128)(2,1)} %query_ref.3, bf16[1,128,4096]{2,1,0:T(8,128)(2,1)} %grad_ref.3), custom_call_target="tpu_custom_call" | custom-call | bytes 2621440 | tf_op jit(solution)/shard_map/pallas_call | solution.py:118
  3.0 0.7 collective-permute-start.7
  3.8 2.4 %collective-permute-start.1 = (bf16[32,4096]{1,0:T(8,128)(2,1)}, bf16[32,4096]{1,0:T(8,128)(2,1)S(1)}, u32[]{:S(2)}, u32[]{:S(2)}) collective-permute-start(bf16[32,4096]{1,0:T(8,128)(2,1)} %get-tuple-element.37), channel_id=1, source_target_pairs={{12,8},{13,9},{14,10},{15,11}} | collective-permute-start | bytes 786440 | tf_op jit(solution)/shard_map/ppermute | solution.py:544
  6.2 4.4 %collective-permute-start = (bf16[32,4096]{1,0:T(8,128)(2,1)}, bf16[32,4096]{1,0:T(8,128)(2,1)S(1)}, u32[]{:S(2)}, u32[]{:S(2)}) collective-permute-start(bf16[32,4096]{1,0:T(8,128)(2,1)} %get-tuple-element.37), channel_id=1, source_target_pairs={{12,20},{13,21},{14,22},{15,23}} | collective-permute-start | bytes 786440 | tf_op jit(solution)/shard_map/ppermute | solution.py:544
  11.3 6.1 %shard_map.111 = (bf16[1,4096,1024]{2,1,0:T(8,128)(2,1)S(1)}, bf16[1,4096,1024]{2,1,0:T(8,128)(2,1)S(1)}, f32[8,128]{1,0:T(8,128)S(1)}) custom-call(bf16[1,4096,1024]{2,1,0:T(8,128)(2,1)} %wk_ref.1, bf16[1,4096,1024]{2,1,0:T(8,128)(2,1)} %wv_ref.1, f32[8,128]{1,0:T(8,128)S(1)} %copy-done.4), custom_call_target="tpu_custom_call" | custom-call | flops 1073741824 | bytes 16777216 | tf_op jit(solution)/shard_map/pallas_call | solution.py:248
  19.0 0.7 collective-permute-start.5
  21.1 0.7 collective-permute-start.6
  21.9 0.7 collective-permute-start.8
  22.7 2.5 %shard_map.117 = (bf16[128,1024]{1,0:T(8,128)(2,1)S(1)}, bf16[128,1024]{1,0:T(8,128)(2,1)S(1)}) custom-call(bf16[128,4224]{1,0:T(8,128)(2,1)S(1)} %shard_map.116.memory_ref, bf16[1,4096,1024]{2,1,0:T(8,128)(2,1)S(1)} %get-tuple-element.42.wk_ref, bf16[1,4096,1024]{2,1,0:T(8,128)(2,1)S(1)} %get-tuple-element.43.wv_ref), custom_call_target="tpu_custom_call" | custom-call | flops 2147483648 | bytes 16777216 | tf_op jit(solution)/shard_map/pallas_call | solution.py:269
  25.2 1.1 %shard_map.118 = (bf16[128,1024]{1,0:T(8,128)(2,1)S(1)}, bf16[128,1024]{1,0:T(8,128)(2,1)S(1)}, bf16[2,16,32,128]{3,2,1,0:T(8,128)(2,1)S(1)}) custom-call(bf16[128,4224]{1,0:T(8,128)(2,1)S(1)} %shard_map.116.memory_ref, bf16[128,1024]{1,0:T(8,128)(2,1)S(1)} %get-tuple-element.44.key_ref, bf16[128,1024]{1,0:T(8,128)(2,1)S(1)} %get-tuple-element.45.value_ref, ...), custom_call_target="tpu_custom_call" | custom-call | flops 134217728 | bytes 4194304 | tf_op jit(solution)/shard_map/pallas_call | solution.py:319
  26.3 4.7 %shard_map.119 = (f32[64,4096]{1,0:T(8,128)S(1)}, bf16[64,4352]{1,0:T(8,128)(2,1)S(1)}, f32[32,128]{1,0:T(8,128)S(1)}) custom-call(bf16[128,4224]{1,0:T(8,128)(2,1)S(1)} %shard_map.116.memory_ref, bf16[128,1024]{1,0:T(8,128)(2,1)S(1)} %get-tuple-element.49.dk_ref, bf16[128,1024]{1,0:T(8,128)(2,1)S(1)} %get-tuple-element.50.dv_ref, ...), custom_call_target="tpu_custom_call" | custom-call | flops 2147483648 | bytes 16777216 | tf_op jit(solution)/shard_map/pallas_call | solution.py:379
  31.0 0.7 collective-permute-start.9
  32.5 6.9 %shard_map.121 = (bf16[1,4096,1024]{2,1,0:T(8,128)(2,1)}, bf16[1,4096,1024]{2,1,0:T(8,128)(2,1)}, f32[8,128]{1,0:T(8,128)S(1)}) custom-call(bf16[128,4224]{1,0:T(8,128)(2,1)S(1)} %shard_map.116.memory_ref, bf16[128,1024]{1,0:T(8,128)(2,1)S(1)} %get-tuple-element.49.dk_ref, bf16[128,1024]{1,0:T(8,128)(2,1)S(1)} %get-tuple-element.50.dv_ref, ...), custom_call_target="tpu_custom_call" | custom-call | flops 2147483648 | bytes 16777216 | tf_op jit(solution)/shard_map/pallas_call | solution.py:488
  40.8 1.5 %shard_map.123 = bf16[4,128,1024]{2,1,0:T(8,128)(2,1)} custom-call(bf16[2,16,32,128]{3,2,1,0:T(8,128)(2,1)S(1)} %get-tuple-element.48.score_ref, bf16[128,1024]{1,0:T(8,128)(2,1)S(1)} %get-tuple-element.44.key_ref, f32[32,128]{1,0:T(8,128)S(1)} %get-tuple-element.59.refs_0_), custom_call_target="tpu_custom_call" | custom-call | flops 33554432 | bytes 2097152 | tf_op jit(solution)/shard_map/pallas_call | solution.py:348
  42.2 3.5 %all-to-all-start = ((bf16[4,128,1024]{2,1,0:T(8,128)(2,1)}), bf16[4,128,1024]{2,1,0:T(8,128)(2,1)S(1)}, u32[]{:S(2)}, u32[]{:S(2)}) async-start(bf16[4,128,1024]{2,1,0:T(8,128)(2,1)} %shard_map.123), calls=%async_computation | async-start | bytes 2097152 | tf_op jit(solution)/shard_map/all_to_all | solution.py:611
  46.6 1.3 %collective-permute-start.15 = (bf16[32,4096]{1,0:T(8,128)(2,1)S(1)}, bf16[32,4096]{1,0:T(8,128)(2,1)S(1)}, u32[]{:S(2)}, u32[]{:S(2)}) collective-permute-start(bf16[32,4096]{1,0:T(8,128)(2,1)S(1)} %get-tuple-element.64), channel_id=1, source_target_pairs={{8,12},{9,13},{10,14},{11,15}} | collective-permute-start | bytes 786440 | tf_op jit(solution)/shard_map/ppermute | solution.py:544
  47.9 1.3 %collective-permute-start.14 = (bf16[32,4096]{1,0:T(8,128)(2,1)S(1)}, bf16[32,4096]{1,0:T(8,128)(2,1)S(1)}, u32[]{:S(2)}, u32[]{:S(2)}) collective-permute-start(bf16[32,4096]{1,0:T(8,128)(2,1)S(1)} %get-tuple-element.64), channel_id=1, source_target_pairs={{20,12},{21,13},{22,14},{23,15}} | collective-permute-start | bytes 786440 | tf_op jit(solution)/shard_map/ppermute | solution.py:544
  49.2 1.3 %collective-permute-start.18 = (f32[32,128]{1,0:T(8,128)S(1)}, f32[32,128]{1,0:T(8,128)S(1)}, u32[]{:S(2)}, u32[]{:S(2)}) collective-permute-start(f32[32,128]{1,0:T(8,128)S(1)} %get-tuple-element.67.own_ref), channel_id=1, source_target_pairs={{16,4},{17,5},{18,6},{19,7},{20,12},{21,13},{22,14},{23,15},{24,0}... | collective-permute-start | bytes 49160 | tf_op jit(solution)/shard_map/ppermute | solution.py:544
  50.5 1.3 %collective-permute-start.17 = (f32[32,128]{1,0:T(8,128)S(1)}, f32[32,128]{1,0:T(8,128)S(1)}, u32[]{:S(2)}, u32[]{:S(2)}) collective-permute-start(f32[32,128]{1,0:T(8,128)S(1)} %get-tuple-element.67.own_ref), channel_id=1, source_target_pairs={{16,0},{17,1},{18,2},{19,3},{20,8},{21,9},{22,10},{23,11},{24,4},{... | collective-permute-start | bytes 49160 | tf_op jit(solution)/shard_map/ppermute | solution.py:544
  52.5 7.7 %all-to-all-done.share_ref = bf16[4,128,1024]{2,1,0:T(8,128)(2,1)S(1)} async-done(((bf16[4,128,1024]{2,1,0:T(8,128)(2,1)}), bf16[4,128,1024]{2,1,0:T(8,128)(2,1)S(1)}, u32[]{:S(2)}, u32[]{:S(2)}) %all-to-all-start) | async-done | bytes 1048608 | tf_op jit(solution)/shard_map/all_to_all | solution.py:611
  60.2 1.0 %shard_map.124 = (bf16[1,128,4096]{2,1,0:T(8,128)(2,1)}, f32[8,128]{1,0:T(8,128)S(1)}) custom-call(bf16[4,128,1024]{2,1,0:T(8,128)(2,1)S(1)} %all-to-all-done.share_ref), custom_call_target="tpu_custom_call" | custom-call | bytes 2097152 | tf_op jit(solution)/shard_map/pallas_call | solution.py:221
  61.2 19.9 %collective-permute-done.15.refs_1_ = bf16[32,4096]{1,0:T(8,128)(2,1)S(1)} collective-permute-done((bf16[32,4096]{1,0:T(8,128)(2,1)S(1)}, bf16[32,4096]{1,0:T(8,128)(2,1)S(1)}, u32[]{:S(2)}, u32[]{:S(2)}) %collective-permute-start.15) | collective-permute-done | bytes 262176 | tf_op jit(solution)/shard_map/ppermute | solution.py:544
  81.1 6.4 %collective-permute-done.14.refs_0_ = bf16[32,4096]{1,0:T(8,128)(2,1)S(1)} collective-permute-done((bf16[32,4096]{1,0:T(8,128)(2,1)S(1)}, bf16[32,4096]{1,0:T(8,128)(2,1)S(1)}, u32[]{:S(2)}, u32[]{:S(2)}) %collective-permute-start.14) | collective-permute-done | bytes 262176 | tf_op jit(solution)/shard_map/ppermute | solution.py:544
  87.6 1.1 %shard_map.126 = (bf16[1,32,4096]{2,1,0:T(8,128)(2,1)}, f32[8,128]{1,0:T(8,128)S(1)}) custom-call(bf16[1,32,4096]{2,1,0:T(8,128)(2,1)S(1)} %copy-done.2, f32[1,4096]{1,0:T(1,128)S(1)} %bitcast.4, bf16[32,4096]{1,0:T(8,128)(2,1)S(1)} %collective-permute-done.14.refs_0_, bf16[32,4096]{1,0:T(8,128)(2,1)S(1)} %collective-permute-done.15.refs_1_, ...), custom_call_target="tpu_custom_call" | custom-call | bytes 1048576 | tf_op jit(solution)/shard_map/pallas_call | solution.py:517
  (46 shorter events, 7.4 us)
Async XLA Ops:
  3.0 18.8 %collective-permute-start.7 = (bf16[2,2,128,1024]{3,2,1,0:T(8,128)(2,1)}, bf16[2,2,128,1024]{3,2,1,0:T(8,128)(2,1)S(1)}, u32[]{:S(2)}, u32[]{:S(2)}) collective-permute-start(bf16[2,2,128,1024]{3,2,1,0:T(8,128)(2,1)} %get-tuple-element.47), channel_id=1, source_target_pairs={{16,18},{17,19},{18,16},{19,17},{20,22},{21,23},{22,20},{23,21},{2... | collective-permute-start | bytes 3145736 | tf_op jit(solution)/shard_map/ppermute | solution.py:540
  3.8 13.6 %collective-permute-start.1 = (bf16[32,4096]{1,0:T(8,128)(2,1)}, bf16[32,4096]{1,0:T(8,128)(2,1)S(1)}, u32[]{:S(2)}, u32[]{:S(2)}) collective-permute-start(bf16[32,4096]{1,0:T(8,128)(2,1)} %get-tuple-element.37), channel_id=1, source_target_pairs={{12,8},{13,9},{14,10},{15,11}} | collective-permute-start | bytes 786440 | tf_op jit(solution)/shard_map/ppermute | solution.py:544
  6.2 11.2 %collective-permute-start = (bf16[32,4096]{1,0:T(8,128)(2,1)}, bf16[32,4096]{1,0:T(8,128)(2,1)S(1)}, u32[]{:S(2)}, u32[]{:S(2)}) collective-permute-start(bf16[32,4096]{1,0:T(8,128)(2,1)} %get-tuple-element.37), channel_id=1, source_target_pairs={{12,20},{13,21},{14,22},{15,23}} | collective-permute-start | bytes 786440 | tf_op jit(solution)/shard_map/ppermute | solution.py:544
  11.3 7.5 %copy-start = (bf16[1,128,4096]{2,1,0:T(8,128)(2,1)S(1)}, bf16[1,128,4096]{2,1,0:T(8,128)(2,1)}, u32[]{:S(2)}) copy-start(bf16[1,128,4096]{2,1,0:T(8,128)(2,1)} %query_ref.3) | copy-start | bytes 3145732
  11.3 7.5 %copy-start.1 = (bf16[1,128,4096]{2,1,0:T(8,128)(2,1)S(1)}, bf16[1,128,4096]{2,1,0:T(8,128)(2,1)}, u32[]{:S(2)}) copy-start(bf16[1,128,4096]{2,1,0:T(8,128)(2,1)} %grad_ref.3) | copy-start | bytes 3145732
  17.4 2.9 %collective-permute-start.3 = (bf16[32,4096]{1,0:T(8,128)(2,1)S(1)}, bf16[32,4096]{1,0:T(8,128)(2,1)S(1)}, u32[]{:S(2)}, u32[]{:S(2)}) collective-permute-start(bf16[32,4096]{1,0:T(8,128)(2,1)S(1)} %shard_map.112.refs_0_), channel_id=1, source_target_pairs={{20,16},{21,17},{22,18},{23,19}} | collective-permute-start | bytes 786440 | tf_op jit(solution)/shard_map/ppermute | solution.py:544
  18.1 2.2 %collective-permute-start.2 = (bf16[32,4096]{1,0:T(8,128)(2,1)S(1)}, bf16[32,4096]{1,0:T(8,128)(2,1)S(1)}, u32[]{:S(2)}, u32[]{:S(2)}) collective-permute-start(bf16[32,4096]{1,0:T(8,128)(2,1)S(1)} %shard_map.112.refs_0_), channel_id=1, source_target_pairs={{20,28},{21,29},{22,30},{23,31},{8,24},{9,25},{10,26},{11,27}} | collective-permute-start | bytes 786440 | tf_op jit(solution)/shard_map/ppermute | solution.py:544
  19.0 2.1 %collective-permute-start.5 = (bf16[1,2,128,1024]{3,2,1,0:T(8,128)(2,1)S(1)}, bf16[1,2,128,1024]{3,2,1,0:T(8,128)(2,1)S(1)}, u32[]{:S(2)}, u32[]{:S(2)}) collective-permute-start(bf16[1,2,128,1024]{3,2,1,0:T(8,128)(2,1)S(1)} %get-tuple-element.41), channel_id=1, source_target_pairs={{16,17},{17,16},{18,19},{19,18},{20,21},{21,20},{22,23},{23,22},{2... | collective-permute-start | bytes 1572872 | tf_op jit(solution)/shard_map/ppermute | solution.py:540
  20.4 0.7 collective-permute-start.4
  21.1 1.5 %collective-permute-start.6 = (bf16[64,4224]{1,0:T(8,128)(2,1)S(1)}, bf16[64,4224]{1,0:T(8,128)(2,1)S(1)}, u32[]{:S(2)}, u32[]{:S(2)}) collective-permute-start(bf16[64,4224]{1,0:T(8,128)(2,1)S(1)} %shard_map.115.first_ref), channel_id=1, source_target_pairs={{16,17},{17,16},{18,19},{19,18},{20,21},{21,20},{22,23},{23,22},{2... | collective-permute-start | bytes 1622024 | tf_op jit(solution)/shard_map/ppermute | solution.py:540
  21.9 3.3 %collective-permute-start.8 = (bf16[1,2,128,1024]{3,2,1,0:T(8,128)(2,1)S(1)}, bf16[1,2,128,1024]{3,2,1,0:T(8,128)(2,1)S(1)}, u32[]{:S(2)}, u32[]{:S(2)}) collective-permute-start(bf16[1,2,128,1024]{3,2,1,0:T(8,128)(2,1)S(1)} %slice.4), channel_id=1, source_target_pairs={{16,17},{17,16},{18,19},{19,18},{20,21},{21,20},{22,23},{23,22},{2... | collective-permute-start | bytes 1572872 | tf_op jit(solution)/shard_map/ppermute | solution.py:540
  22.7 3.6 %copy-start.3 = (f32[4096]{0:T(1024)S(1)}, f32[4096]{0:T(1024)}, u32[]{:S(2)}) copy-start(f32[4096]{0:T(1024)} %param.8) | copy-start | bytes 49156
  31.0 0.7 collective-permute-start.9
  31.8 7.6 %collective-permute-start.10 = (bf16[32,4352]{1,0:T(8,128)(2,1)S(1)}, bf16[32,4352]{1,0:T(8,128)(2,1)S(1)}, u32[]{:S(2)}, u32[]{:S(2)}) collective-permute-start(bf16[32,4352]{1,0:T(8,128)(2,1)S(1)} %get-tuple-element.55), channel_id=1, source_target_pairs={{16,18},{17,19},{18,16},{19,17},{20,22},{21,23},{22,20},{23,21},{2... | collective-permute-start | bytes 835592 | tf_op jit(solution)/shard_map/ppermute | solution.py:540
  39.4 7.1 %collective-permute-start.12 = (bf16[32,4096]{1,0:T(8,128)(2,1)S(1)}, bf16[32,4096]{1,0:T(8,128)(2,1)S(1)}, u32[]{:S(2)}, u32[]{:S(2)}) collective-permute-start(bf16[32,4096]{1,0:T(8,128)(2,1)S(1)} %get-tuple-element.63.own_ref), channel_id=1, source_target_pairs={{16,20},{17,21},{18,22},{19,23}} | collective-permute-start | bytes 786440 | tf_op jit(solution)/shard_map/ppermute | solution.py:544
  40.1 6.4 %collective-permute-start.11 = (bf16[32,4096]{1,0:T(8,128)(2,1)S(1)}, bf16[32,4096]{1,0:T(8,128)(2,1)S(1)}, u32[]{:S(2)}, u32[]{:S(2)}) collective-permute-start(bf16[32,4096]{1,0:T(8,128)(2,1)S(1)} %get-tuple-element.63.own_ref), channel_id=1, source_target_pairs={{28,20},{29,21},{30,22},{31,23},{24,8},{25,9},{26,10},{27,11}} | collective-permute-start | bytes 786440 | tf_op jit(solution)/shard_map/ppermute | solution.py:544
  42.2 18.0 %all-to-all-start = ((bf16[4,128,1024]{2,1,0:T(8,128)(2,1)}), bf16[4,128,1024]{2,1,0:T(8,128)(2,1)S(1)}, u32[]{:S(2)}, u32[]{:S(2)}) async-start(bf16[4,128,1024]{2,1,0:T(8,128)(2,1)} %shard_map.123), calls=%async_computation | async-start | bytes 2097152 | tf_op jit(solution)/shard_map/all_to_all | solution.py:611
  45.8 0.7 collective-permute-start.13
  46.5 41.1 %copy-start.2 = (bf16[1,32,4096]{2,1,0:T(8,128)(2,1)S(1)}, bf16[1,32,4096]{2,1,0:T(8,128)(2,1)}, u32[]{:S(2)}) copy-start(bf16[1,32,4096]{2,1,0:T(8,128)(2,1)} %enc_ref.3) | copy-start | bytes 786436
  46.6 34.5 %collective-permute-start.15 = (bf16[32,4096]{1,0:T(8,128)(2,1)S(1)}, bf16[32,4096]{1,0:T(8,128)(2,1)S(1)}, u32[]{:S(2)}, u32[]{:S(2)}) collective-permute-start(bf16[32,4096]{1,0:T(8,128)(2,1)S(1)} %get-tuple-element.64), channel_id=1, source_target_pairs={{8,12},{9,13},{10,14},{11,15}} | collective-permute-start | bytes 786440 | tf_op jit(solution)/shard_map/ppermute | solution.py:544
  47.9 39.6 %collective-permute-start.14 = (bf16[32,4096]{1,0:T(8,128)(2,1)S(1)}, bf16[32,4096]{1,0:T(8,128)(2,1)S(1)}, u32[]{:S(2)}, u32[]{:S(2)}) collective-permute-start(bf16[32,4096]{1,0:T(8,128)(2,1)S(1)} %get-tuple-element.64), channel_id=1, source_target_pairs={{20,12},{21,13},{22,14},{23,15}} | collective-permute-start | bytes 786440 | tf_op jit(solution)/shard_map/ppermute | solution.py:544
  49.2 39.4 %collective-permute-start.18 = (f32[32,128]{1,0:T(8,128)S(1)}, f32[32,128]{1,0:T(8,128)S(1)}, u32[]{:S(2)}, u32[]{:S(2)}) collective-permute-start(f32[32,128]{1,0:T(8,128)S(1)} %get-tuple-element.67.own_ref), channel_id=1, source_target_pairs={{16,4},{17,5},{18,6},{19,7},{20,12},{21,13},{22,14},{23,15},{24,0}... | collective-permute-start | bytes 49160 | tf_op jit(solution)/shard_map/ppermute | solution.py:544
  50.5 38.1 %collective-permute-start.17 = (f32[32,128]{1,0:T(8,128)S(1)}, f32[32,128]{1,0:T(8,128)S(1)}, u32[]{:S(2)}, u32[]{:S(2)}) collective-permute-start(f32[32,128]{1,0:T(8,128)S(1)} %get-tuple-element.67.own_ref), channel_id=1, source_target_pairs={{16,0},{17,1},{18,2},{19,3},{20,8},{21,9},{22,10},{23,11},{24,4},{... | collective-permute-start | bytes 49160 | tf_op jit(solution)/shard_map/ppermute | solution.py:544
  51.8 36.8 %collective-permute-start.16 = (f32[32,128]{1,0:T(8,128)S(1)}, f32[32,128]{1,0:T(8,128)S(1)}, u32[]{:S(2)}, u32[]{:S(2)}) collective-permute-start(f32[32,128]{1,0:T(8,128)S(1)} %get-tuple-element.67.own_ref), channel_id=1, source_target_pairs={{16,24},{17,25},{18,26},{19,27},{20,28},{21,29},{22,30},{23,31},{2... | collective-permute-start | bytes 49160 | tf_op jit(solution)/shard_map/ppermute | solution.py:544
  (1 other events, 0.7 us)

commit v5 on v4

--- a/solution.py
+++ b/solution.py
@@ -12,7 +12,8 @@
 TILE = 1024
 VMEM_BEGIN = 54
 COST_HOLD = 1 << 30
-COST_SUM = 1 << 32
+COST_SUM = 3 << 30
+COST_GAIN = 1 << 32
 
 
 def section_rounds(sections):
@@ -336,7 +337,8 @@
     targets = scores.shape[3]
 
     def kernel(score_ref, key_ref, *refs):
-        out_ref = refs[-1]
+        out_ref, token_ref = refs[-2:]
+        mark(token_ref)
         index = lax.axis_index("dp")
         for h in range(width // HEAD_DIM):
             head = slice(h * HEAD_DIM, (h + 1) * HEAD_DIM)
@@ -347,12 +349,25 @@
 
     return call(
         kernel,
-        shape((count, targets, width)),
+        [shape((count, targets, width)), TOKEN],
         flops=2 * count * rows * targets * width,
         moved=4 * count * targets * width,
         in_specs=[VMEM] * 2 + [ANY] * len(tokens),
-        out_specs=VMEM,
+        out_specs=[VMEM] * 2,
     )(scores, keys, *tokens)
+
+
+def follow(block, tokens):
+    def kernel(*refs):
+        del refs
+
+    return call(
+        kernel,
+        shape(block.shape, block.dtype),
+        in_specs=[ANY] * (1 + len(tokens)),
+        out_specs=ANY,
+        input_output_aliases={0: 0},
+    )(block, *tokens)
 
 
 def memory_part(memory, w_key, w_value, dk, dv, gain):
@@ -436,26 +451,38 @@
     )(kept, came, gain, *tokens)
 
 
-def add_sections(own, came, gain):
+def add_sections(own, came):
     count = len(came)
 
     def kernel(own_ref, *refs):
-        gain_ref = refs[count]
-        out_ref, gain_out_ref = refs[-2:]
+        out_ref, token_ref = refs[-2:]
         total = own_ref[...].astype(jnp.float32)
         for ref in refs[:count]:
             total = total + ref[...].astype(jnp.float32)
         out_ref[...] = total.astype(jnp.bfloat16)
-        gain_out_ref[...] = gain_ref[...]
-
-    return call(
-        kernel,
-        [shape(own.shape), shape(gain.shape, jnp.float32)],
+        mark(token_ref)
+
+    return call(
+        kernel,
+        [shape(own.shape), TOKEN],
         flops=COST_SUM,
         moved=6 * own.size,
-        in_specs=[VMEM] * (2 + count),
+        in_specs=[VMEM] * (1 + count),
         out_specs=[VMEM] * 2,
-    )(own, *came, gain)
+    )(own, *came)
+
+
+def add_gain(own, came, token):
+    def kernel(own_ref, came_ref, _, out_ref):
+        out_ref[...] = own_ref[...] + came_ref[...]
+
+    return call(
+        kernel,
+        shape(own.shape, jnp.float32),
+        flops=COST_GAIN,
+        in_specs=[VMEM] * 2 + [ANY],
+        out_specs=VMEM,
+    )(own, came, token)
 
 
 def add_gains(terms, token):
@@ -583,6 +610,9 @@
         last = bit == bits - 1
         came = over_dp(sent, 1 << bit)
         tokens = []
+        if not bit:
+            dq, done = query_grads(scores, keys, order, [gain_part])
+            tokens = [done]
         if last:
             grads, done = weight_grads(pieces, width, 0, width // TILE, dk, dv, [], [token])
             tokens = [done]
@@ -590,15 +620,16 @@
         if not last:
             kept, token = more
     key_weight_grad, value_weight_grad = grads
-    dq = query_grads(scores, keys, order, [gain_part])
-    step = 1
-    while step < half // 2:
-        gain_part = gain_part + over_section(gain_part, [(s, s ^ step) for s in decoders])
-        step *= 2
+    dq = follow(dq, [gain_part])
     for number, stage in reversed(list(enumerate(rounds))):
         came = [over_section(sent, [(b, a) for a, b in group]) for group in split_pairs(stage)]
         if number:
-            sent, gain_part = add_sections(sent, came, gain_part)
+            sent, token = add_sections(sent, came)
+    step = 1
+    while step < half // 2:
+        came_gain = over_section(gain_part, [(s, s ^ step) for s in decoders])
+        gain_part = add_gain(gain_part, came_gain, token)
+        step *= 2
     places = [(i % step) * 2 + i // step for i in range(half)]
     terms = [
         gain_part,

time: 90.3 us -> 88.7 us (0.982)
  the two profiles are of different devices: /device:TPU:12 before, /device:TPU:16 now
where the time goes in v5:
time: 88.7 us; the launch traced here: 88.1 us
  starting transfers between devices  36.9 us (42%)
  Pallas kernels  28.3 us (32%)
  waiting for transfers between devices  20.5 us (23%)
  between operations  1.67 us (2%)
    ppermute x7, starting transfers between devices, over_dp(): return lax.ppermute(block, BOTH, pairs)  17.4 us
    ppermute x12, starting transfers between devices, over_section(): return lax.ppermute(block, BOTH, pairs)  16 us
    ppermute x7, waiting for transfers between devices, over_dp(): return lax.ppermute(block, BOTH, pairs)  9.16 us
    ppermute x12, waiting for transfers between devices, over_section(): return lax.ppermute(block, BOTH, pairs)  7.82 us
    pallas_call x1, Pallas kernels, weight_grads(): call(kernel, [shape((1, width, columns))] * 2 + [TOKEN], flops=4 * rows *...  6.88 us
    pallas_call x1, Pallas kernels, hold_weights(): call(kernel, [shape(w_key.shape)] * 2 + [TOKEN], flops=COST_HOLD, moved=4...  6.06 us
    pallas_call x1, Pallas kernels, memory_part(): call(kernel, [shape((keep, depth), jnp.float32), shape((keep, depth + 2 *...  4.66 us
    all_to_all x1, starting transfers between devices, on_device(): lax.all_to_all(dq, 'dp', split_axis=0, concat_axis=0, tiled=True)  3.53 us
  transfers between devices with their start and end apart: 20, of which 6 were waited for; matrix products, arithmetic and copies ran while one was open for 0% of the time, Pallas kernels for 22%

profile of v5, /device:TPU:16, one launch (start us, length us, event | category | flops | bytes accessed | tf_op | source)
XLA Modules:
  0.0 88.1 jit_solution(14420203290953651992)
XLA Ops:
  0.6 2.4 %shard_map.110 = (bf16[32,4096]{1,0:T(8,128)(2,1)}, bf16[2,2,128,1024]{3,2,1,0:T(8,128)(2,1)}, f32[8,128]{1,0:T(8,128)}) custom-call(bf16[1,32,4096]{2,1,0:T(8,128)(2,1)} %enc_ref.3, f32[1,4096]{1,0:T(1,128)} %bitcast.2, bf16[1,128,4096]{2,1,0:T(8,128)(2,1)} %query_ref.3, bf16[1,128,4096]{2,1,0:T(8,128)(2,1)} %grad_ref.3), custom_call_target="tpu_custom_call" | custom-call | bytes 2621440 | tf_op jit(solution)/shard_map/pallas_call | solution.py:119
  3.0 3.4 %collective-permute-start.7 = (bf16[2,2,128,1024]{3,2,1,0:T(8,128)(2,1)}, bf16[2,2,128,1024]{3,2,1,0:T(8,128)(2,1)S(1)}, u32[]{:S(2)}, u32[]{:S(2)}) collective-permute-start(bf16[2,2,128,1024]{3,2,1,0:T(8,128)(2,1)} %get-tuple-element.49), channel_id=1, source_target_pairs={{16,18},{17,19},{18,16},{19,17},{20,22},{21,23},{22,20},{23,21},{2... | collective-permute-start | bytes 3145736 | tf_op jit(solution)/shard_map/ppermute | solution.py:567
  8.5 6.1 %shard_map.111 = (bf16[1,4096,1024]{2,1,0:T(8,128)(2,1)S(1)}, bf16[1,4096,1024]{2,1,0:T(8,128)(2,1)S(1)}, f32[8,128]{1,0:T(8,128)S(1)}) custom-call(bf16[1,4096,1024]{2,1,0:T(8,128)(2,1)} %wk_ref.1, bf16[1,4096,1024]{2,1,0:T(8,128)(2,1)} %wv_ref.1, f32[8,128]{1,0:T(8,128)S(1)} %copy-done.4), custom_call_target="tpu_custom_call" | custom-call | flops 1073741824 | bytes 16777216 | tf_op jit(solution)/shard_map/pallas_call | solution.py:249
  14.6 1.3 %collective-permute-start.3 = (bf16[32,4096]{1,0:T(8,128)(2,1)S(1)}, bf16[32,4096]{1,0:T(8,128)(2,1)S(1)}, u32[]{:S(2)}, u32[]{:S(2)}) collective-permute-start(bf16[32,4096]{1,0:T(8,128)(2,1)S(1)} %shard_map.112.refs_0_), channel_id=1, source_target_pairs={{20,16},{21,17},{22,18},{23,19}} | collective-permute-start | bytes 786440 | tf_op jit(solution)/shard_map/ppermute | solution.py:571
  16.8 1.9 %collective-permute-start.5 = (bf16[1,2,128,1024]{3,2,1,0:T(8,128)(2,1)S(1)}, bf16[1,2,128,1024]{3,2,1,0:T(8,128)(2,1)S(1)}, u32[]{:S(2)}, u32[]{:S(2)}) collective-permute-start(bf16[1,2,128,1024]{3,2,1,0:T(8,128)(2,1)S(1)} %get-tuple-element.43), channel_id=1, source_target_pairs={{16,17},{17,16},{18,19},{19,18},{20,21},{21,20},{22,23},{23,22},{2... | collective-permute-start | bytes 1572872 | tf_op jit(solution)/shard_map/ppermute | solution.py:567
  19.3 5.6 %collective-permute-done.3.refs_2_ = bf16[32,4096]{1,0:T(8,128)(2,1)S(1)} collective-permute-done((bf16[32,4096]{1,0:T(8,128)(2,1)S(1)}, bf16[32,4096]{1,0:T(8,128)(2,1)S(1)}, u32[]{:S(2)}, u32[]{:S(2)}) %collective-permute-start.3) | collective-permute-done | bytes 262176 | tf_op jit(solution)/shard_map/ppermute | solution.py:571
  25.0 2.4 %collective-permute-start.4 = (bf16[32,4224]{1,0:T(8,128)(2,1)S(1)}, bf16[32,4224]{1,0:T(8,128)(2,1)S(1)}, u32[]{:S(2)}, u32[]{:S(2)}) collective-permute-start(bf16[32,4224]{1,0:T(8,128)(2,1)S(1)} %shard_map.114.first_ref), channel_id=1, source_target_pairs={{16,18},{17,19},{18,16},{19,17},{20,22},{21,23},{22,20},{23,21},{2... | collective-permute-start | bytes 811016 | tf_op jit(solution)/shard_map/ppermute | solution.py:567
  27.4 8.4 %collective-permute-done.4.second_ref = bf16[32,4224]{1,0:T(8,128)(2,1)S(1)} collective-permute-done((bf16[32,4224]{1,0:T(8,128)(2,1)S(1)}, bf16[32,4224]{1,0:T(8,128)(2,1)S(1)}, u32[]{:S(2)}, u32[]{:S(2)}) %collective-permute-start.4) | collective-permute-done | bytes 270368 | tf_op jit(solution)/shard_map/ppermute | solution.py:567
  35.9 1.9 %collective-permute-start.6 = (bf16[64,4224]{1,0:T(8,128)(2,1)S(1)}, bf16[64,4224]{1,0:T(8,128)(2,1)S(1)}, u32[]{:S(2)}, u32[]{:S(2)}) collective-permute-start(bf16[64,4224]{1,0:T(8,128)(2,1)S(1)} %shard_map.115.first_ref), channel_id=1, source_target_pairs={{16,17},{17,16},{18,19},{19,18},{20,21},{21,20},{22,23},{23,22},{2... | collective-permute-start | bytes 1622024 | tf_op jit(solution)/shard_map/ppermute | solution.py:567
  37.8 2.4 %collective-permute-start.8 = (bf16[1,2,128,1024]{3,2,1,0:T(8,128)(2,1)S(1)}, bf16[1,2,128,1024]{3,2,1,0:T(8,128)(2,1)S(1)}, u32[]{:S(2)}, u32[]{:S(2)}) collective-permute-start(bf16[1,2,128,1024]{3,2,1,0:T(8,128)(2,1)S(1)} %slice.4), channel_id=1, source_target_pairs={{16,17},{17,16},{18,19},{19,18},{20,21},{21,20},{22,23},{23,22},{2... | collective-permute-start | bytes 1572872 | tf_op jit(solution)/shard_map/ppermute | solution.py:567
  40.4 2.5 %shard_map.117 = (bf16[128,1024]{1,0:T(8,128)(2,1)S(1)}, bf16[128,1024]{1,0:T(8,128)(2,1)S(1)}) custom-call(bf16[128,4224]{1,0:T(8,128)(2,1)S(1)} %shard_map.116.memory_ref, bf16[1,4096,1024]{2,1,0:T(8,128)(2,1)S(1)} %get-tuple-element.44.wk_ref, bf16[1,4096,1024]{2,1,0:T(8,128)(2,1)S(1)} %get-tuple-element.45.wv_ref), custom_call_target="tpu_custom_call" | custom-call | flops 2147483648 | bytes 16777216 | tf_op jit(solution)/shard_map/pallas_call | solution.py:270
  44.0 4.7 %shard_map.119 = (f32[64,4096]{1,0:T(8,128)S(1)}, bf16[64,4352]{1,0:T(8,128)(2,1)S(1)}, f32[32,128]{1,0:T(8,128)S(1)}) custom-call(bf16[128,4224]{1,0:T(8,128)(2,1)S(1)} %shard_map.116.memory_ref, bf16[128,1024]{1,0:T(8,128)(2,1)S(1)} %get-tuple-element.51.dk_ref, bf16[128,1024]{1,0:T(8,128)(2,1)S(1)} %get-tuple-element.52.dv_ref, ...), custom_call_target="tpu_custom_call" | custom-call | flops 2147483648 | bytes 16777216 | tf_op jit(solution)/shard_map/pallas_call | solution.py:394
  48.6 1.9 %collective-permute-start.9 = (bf16[64,4352]{1,0:T(8,128)(2,1)S(1)}, bf16[64,4352]{1,0:T(8,128)(2,1)S(1)}, u32[]{:S(2)}, u32[]{:S(2)}) collective-permute-start(bf16[64,4352]{1,0:T(8,128)(2,1)S(1)} %get-tuple-element.56), channel_id=1, source_target_pairs={{16,17},{17,16},{18,19},{19,18},{20,21},{21,20},{22,23},{23,22},{2... | collective-permute-start | bytes 1671176 | tf_op jit(solution)/shard_map/ppermute | solution.py:567
  50.6 1.5 %shard_map.120 = (bf16[4,128,1024]{2,1,0:T(8,128)(2,1)}, f32[8,128]{1,0:T(8,128)S(1)}) custom-call(bf16[2,16,32,128]{3,2,1,0:T(8,128)(2,1)S(1)} %get-tuple-element.50.score_ref, bf16[128,1024]{1,0:T(8,128)(2,1)S(1)} %get-tuple-element.46.key_ref, f32[32,128]{1,0:T(8,128)S(1)} %get-tuple-element.53.refs_0_.gain_ref), custom_call_target="tpu_custom_call" | custom-call | flops 33554432 | bytes 2097152 | tf_op jit(solution)/shard_map/pallas_call | solution.py:350
  52.6 3.4 %collective-permute-start.10 = (bf16[32,4352]{1,0:T(8,128)(2,1)S(1)}, bf16[32,4352]{1,0:T(8,128)(2,1)S(1)}, u32[]{:S(2)}, u32[]{:S(2)}) collective-permute-start(bf16[32,4352]{1,0:T(8,128)(2,1)S(1)} %get-tuple-element.59), channel_id=1, source_target_pairs={{16,18},{17,19},{18,16},{19,17},{20,22},{21,23},{22,20},{23,21},{2... | collective-permute-start | bytes 835592 | tf_op jit(solution)/shard_map/ppermute | solution.py:567
  56.0 6.9 %shard_map.122 = (bf16[1,4096,1024]{2,1,0:T(8,128)(2,1)}, bf16[1,4096,1024]{2,1,0:T(8,128)(2,1)}, f32[8,128]{1,0:T(8,128)S(1)}) custom-call(bf16[128,4224]{1,0:T(8,128)(2,1)S(1)} %shard_map.116.memory_ref, bf16[128,1024]{1,0:T(8,128)(2,1)S(1)} %get-tuple-element.51.dk_ref, bf16[128,1024]{1,0:T(8,128)(2,1)S(1)} %get-tuple-element.52.dv_ref, ...), custom_call_target="tpu_custom_call" | custom-call | flops 2147483648 | bytes 16777216 | tf_op jit(solution)/shard_map/pallas_call | solution.py:515
  63.3 3.5 %collective-permute-start.12 = (bf16[32,4096]{1,0:T(8,128)(2,1)S(1)}, bf16[32,4096]{1,0:T(8,128)(2,1)S(1)}, u32[]{:S(2)}, u32[]{:S(2)}) collective-permute-start(bf16[32,4096]{1,0:T(8,128)(2,1)S(1)} %get-tuple-element.67.own_ref), channel_id=1, source_target_pairs={{16,20},{17,21},{18,22},{19,23}} | collective-permute-start | bytes 786440 | tf_op jit(solution)/shard_map/ppermute | solution.py:571
  67.4 3.5 %all-to-all-start = ((bf16[4,128,1024]{2,1,0:T(8,128)(2,1)}), bf16[4,128,1024]{2,1,0:T(8,128)(2,1)S(1)}, u32[]{:S(2)}, u32[]{:S(2)}) async-start(bf16[4,128,1024]{2,1,0:T(8,128)(2,1)} %shard_map.124), calls=%async_computation | async-start | bytes 2097152 | tf_op jit(solution)/shard_map/all_to_all | solution.py:642
  71.0 1.9 %collective-permute-start.15 = (f32[32,128]{1,0:T(8,128)S(1)}, f32[32,128]{1,0:T(8,128)S(1)}, u32[]{:S(2)}, u32[]{:S(2)}) collective-permute-start(f32[32,128]{1,0:T(8,128)S(1)} %get-tuple-element.63.refs_1_.own_ref), channel_id=1, source_target_pairs={{16,20},{17,21},{18,22},{19,23},{20,16},{21,17},{22,18},{23,19},{2... | collective-permute-start | bytes 49160 | tf_op jit(solution)/shard_map/ppermute | solution.py:571
  74.4 2.2 %collective-permute-done.15.came_ref = f32[32,128]{1,0:T(8,128)S(1)} collective-permute-done((f32[32,128]{1,0:T(8,128)S(1)}, f32[32,128]{1,0:T(8,128)S(1)}, u32[]{:S(2)}, u32[]{:S(2)}) %collective-permute-start.15) | collective-permute-done | bytes 16416 | tf_op jit(solution)/shard_map/ppermute | solution.py:571
  76.6 1.4 %collective-permute-start.18 = (f32[32,128]{1,0:T(8,128)S(1)}, f32[32,128]{1,0:T(8,128)S(1)}, u32[]{:S(2)}, u32[]{:S(2)}) collective-permute-start(f32[32,128]{1,0:T(8,128)S(1)} %shard_map.128.own_ref), channel_id=1, source_target_pairs={{16,4},{17,5},{18,6},{19,7},{20,12},{21,13},{22,14},{23,15},{24,0}... | collective-permute-start | bytes 49160 | tf_op jit(solution)/shard_map/ppermute | solution.py:571
  78.0 1.3 %collective-permute-start.17 = (f32[32,128]{1,0:T(8,128)S(1)}, f32[32,128]{1,0:T(8,128)S(1)}, u32[]{:S(2)}, u32[]{:S(2)}) collective-permute-start(f32[32,128]{1,0:T(8,128)S(1)} %shard_map.128.own_ref), channel_id=1, source_target_pairs={{16,0},{17,1},{18,2},{19,3},{20,8},{21,9},{22,10},{23,11},{24,4},{... | collective-permute-start | bytes 49160 | tf_op jit(solution)/shard_map/ppermute | solution.py:571
  79.3 2.5 %collective-permute-start.16 = (f32[32,128]{1,0:T(8,128)S(1)}, f32[32,128]{1,0:T(8,128)S(1)}, u32[]{:S(2)}, u32[]{:S(2)}) collective-permute-start(f32[32,128]{1,0:T(8,128)S(1)} %shard_map.128.own_ref), channel_id=1, source_target_pairs={{16,24},{17,25},{18,26},{19,27},{20,28},{21,29},{22,30},{23,31},{2... | collective-permute-start | bytes 49160 | tf_op jit(solution)/shard_map/ppermute | solution.py:571
  81.9 3.5 %all-to-all-done.share_ref = bf16[4,128,1024]{2,1,0:T(8,128)(2,1)S(1)} async-done(((bf16[4,128,1024]{2,1,0:T(8,128)(2,1)}), bf16[4,128,1024]{2,1,0:T(8,128)(2,1)S(1)}, u32[]{:S(2)}, u32[]{:S(2)}) %all-to-all-start) | async-done | bytes 1048608 | tf_op jit(solution)/shard_map/all_to_all | solution.py:642
  (47 shorter events, 10.0 us)
Async XLA Ops:
  3.0 34.8 %collective-permute-start.7 = (bf16[2,2,128,1024]{3,2,1,0:T(8,128)(2,1)}, bf16[2,2,128,1024]{3,2,1,0:T(8,128)(2,1)S(1)}, u32[]{:S(2)}, u32[]{:S(2)}) collective-permute-start(bf16[2,2,128,1024]{3,2,1,0:T(8,128)(2,1)} %get-tuple-element.49), channel_id=1, source_target_pairs={{16,18},{17,19},{18,16},{19,17},{20,22},{21,23},{22,20},{23,21},{2... | collective-permute-start | bytes 3145736 | tf_op jit(solution)/shard_map/ppermute | solution.py:567
  6.4 8.1 %collective-permute-start.1 = (bf16[32,4096]{1,0:T(8,128)(2,1)}, bf16[32,4096]{1,0:T(8,128)(2,1)S(1)}, u32[]{:S(2)}, u32[]{:S(2)}) collective-permute-start(bf16[32,4096]{1,0:T(8,128)(2,1)} %get-tuple-element.39), channel_id=1, source_target_pairs={{12,8},{13,9},{14,10},{15,11}} | collective-permute-start | bytes 786440 | tf_op jit(solution)/shard_map/ppermute | solution.py:571
  7.1 7.5 %collective-permute-start = (bf16[32,4096]{1,0:T(8,128)(2,1)}, bf16[32,4096]{1,0:T(8,128)(2,1)S(1)}, u32[]{:S(2)}, u32[]{:S(2)}) collective-permute-start(bf16[32,4096]{1,0:T(8,128)(2,1)} %get-tuple-element.39), channel_id=1, source_target_pairs={{12,20},{13,21},{14,22},{15,23}} | collective-permute-start | bytes 786440 | tf_op jit(solution)/shard_map/ppermute | solution.py:571
  8.5 8.1 %copy-start = (bf16[1,128,4096]{2,1,0:T(8,128)(2,1)S(1)}, bf16[1,128,4096]{2,1,0:T(8,128)(2,1)}, u32[]{:S(2)}) copy-start(bf16[1,128,4096]{2,1,0:T(8,128)(2,1)} %query_ref.3) | copy-start | bytes 3145732
  8.5 8.1 %copy-start.1 = (bf16[1,128,4096]{2,1,0:T(8,128)(2,1)S(1)}, bf16[1,128,4096]{2,1,0:T(8,128)(2,1)}, u32[]{:S(2)}) copy-start(bf16[1,128,4096]{2,1,0:T(8,128)(2,1)} %grad_ref.3) | copy-start | bytes 3145732
  14.6 10.3 %collective-permute-start.3 = (bf16[32,4096]{1,0:T(8,128)(2,1)S(1)}, bf16[32,4096]{1,0:T(8,128)(2,1)S(1)}, u32[]{:S(2)}, u32[]{:S(2)}) collective-permute-start(bf16[32,4096]{1,0:T(8,128)(2,1)S(1)} %shard_map.112.refs_0_), channel_id=1, source_target_pairs={{20,16},{21,17},{22,18},{23,19}} | collective-permute-start | bytes 786440 | tf_op jit(solution)/shard_map/ppermute | solution.py:571
  15.9 9.0 %collective-permute-start.2 = (bf16[32,4096]{1,0:T(8,128)(2,1)S(1)}, bf16[32,4096]{1,0:T(8,128)(2,1)S(1)}, u32[]{:S(2)}, u32[]{:S(2)}) collective-permute-start(bf16[32,4096]{1,0:T(8,128)(2,1)S(1)} %shard_map.112.refs_0_), channel_id=1, source_target_pairs={{20,28},{21,29},{22,30},{23,31},{8,24},{9,25},{10,26},{11,27}} | collective-permute-start | bytes 786440 | tf_op jit(solution)/shard_map/ppermute | solution.py:571
  16.8 10.7 %collective-permute-start.5 = (bf16[1,2,128,1024]{3,2,1,0:T(8,128)(2,1)S(1)}, bf16[1,2,128,1024]{3,2,1,0:T(8,128)(2,1)S(1)}, u32[]{:S(2)}, u32[]{:S(2)}) collective-permute-start(bf16[1,2,128,1024]{3,2,1,0:T(8,128)(2,1)S(1)} %get-tuple-element.43), channel_id=1, source_target_pairs={{16,17},{17,16},{18,19},{19,18},{20,21},{21,20},{22,23},{23,22},{2... | collective-permute-start | bytes 1572872 | tf_op jit(solution)/shard_map/ppermute | solution.py:567
  25.0 10.8 %collective-permute-start.4 = (bf16[32,4224]{1,0:T(8,128)(2,1)S(1)}, bf16[32,4224]{1,0:T(8,128)(2,1)S(1)}, u32[]{:S(2)}, u32[]{:S(2)}) collective-permute-start(bf16[32,4224]{1,0:T(8,128)(2,1)S(1)} %shard_map.114.first_ref), channel_id=1, source_target_pairs={{16,18},{17,19},{18,16},{19,17},{20,22},{21,23},{22,20},{23,21},{2... | collective-permute-start | bytes 811016 | tf_op jit(solution)/shard_map/ppermute | solution.py:567
  35.9 4.4 %collective-permute-start.6 = (bf16[64,4224]{1,0:T(8,128)(2,1)S(1)}, bf16[64,4224]{1,0:T(8,128)(2,1)S(1)}, u32[]{:S(2)}, u32[]{:S(2)}) collective-permute-start(bf16[64,4224]{1,0:T(8,128)(2,1)S(1)} %shard_map.115.first_ref), channel_id=1, source_target_pairs={{16,17},{17,16},{18,19},{19,18},{20,21},{21,20},{22,23},{23,22},{2... | collective-permute-start | bytes 1622024 | tf_op jit(solution)/shard_map/ppermute | solution.py:567
  37.8 5.0 %collective-permute-start.8 = (bf16[1,2,128,1024]{3,2,1,0:T(8,128)(2,1)S(1)}, bf16[1,2,128,1024]{3,2,1,0:T(8,128)(2,1)S(1)}, u32[]{:S(2)}, u32[]{:S(2)}) collective-permute-start(bf16[1,2,128,1024]{3,2,1,0:T(8,128)(2,1)S(1)} %slice.4), channel_id=1, source_target_pairs={{16,17},{17,16},{18,19},{19,18},{20,21},{21,20},{22,23},{23,22},{2... | collective-permute-start | bytes 1572872 | tf_op jit(solution)/shard_map/ppermute | solution.py:567
  40.4 3.6 %copy-start.3 = (f32[4096]{0:T(1024)S(1)}, f32[4096]{0:T(1024)}, u32[]{:S(2)}) copy-start(f32[4096]{0:T(1024)} %param.8) | copy-start | bytes 49156
  48.6 3.8 %collective-permute-start.9 = (bf16[64,4352]{1,0:T(8,128)(2,1)S(1)}, bf16[64,4352]{1,0:T(8,128)(2,1)S(1)}, u32[]{:S(2)}, u32[]{:S(2)}) collective-permute-start(bf16[64,4352]{1,0:T(8,128)(2,1)S(1)} %get-tuple-element.56), channel_id=1, source_target_pairs={{16,17},{17,16},{18,19},{19,18},{20,21},{21,20},{22,23},{23,22},{2... | collective-permute-start | bytes 1671176 | tf_op jit(solution)/shard_map/ppermute | solution.py:567
  52.6 10.6 %collective-permute-start.10 = (bf16[32,4352]{1,0:T(8,128)(2,1)S(1)}, bf16[32,4352]{1,0:T(8,128)(2,1)S(1)}, u32[]{:S(2)}, u32[]{:S(2)}) collective-permute-start(bf16[32,4352]{1,0:T(8,128)(2,1)S(1)} %get-tuple-element.59), channel_id=1, source_target_pairs={{16,18},{17,19},{18,16},{19,17},{20,22},{21,23},{22,20},{23,21},{2... | collective-permute-start | bytes 835592 | tf_op jit(solution)/shard_map/ppermute | solution.py:567
  63.3 9.6 %collective-permute-start.12 = (bf16[32,4096]{1,0:T(8,128)(2,1)S(1)}, bf16[32,4096]{1,0:T(8,128)(2,1)S(1)}, u32[]{:S(2)}, u32[]{:S(2)}) collective-permute-start(bf16[32,4096]{1,0:T(8,128)(2,1)S(1)} %get-tuple-element.67.own_ref), channel_id=1, source_target_pairs={{16,20},{17,21},{18,22},{19,23}} | collective-permute-start | bytes 786440 | tf_op jit(solution)/shard_map/ppermute | solution.py:571
  66.7 6.2 %collective-permute-start.11 = (bf16[32,4096]{1,0:T(8,128)(2,1)S(1)}, bf16[32,4096]{1,0:T(8,128)(2,1)S(1)}, u32[]{:S(2)}, u32[]{:S(2)}) collective-permute-start(bf16[32,4096]{1,0:T(8,128)(2,1)S(1)} %get-tuple-element.67.own_ref), channel_id=1, source_target_pairs={{28,20},{29,21},{30,22},{31,23},{24,8},{25,9},{26,10},{27,11}} | collective-permute-start | bytes 786440 | tf_op jit(solution)/shard_map/ppermute | solution.py:571
  67.4 18.0 %all-to-all-start = ((bf16[4,128,1024]{2,1,0:T(8,128)(2,1)}), bf16[4,128,1024]{2,1,0:T(8,128)(2,1)S(1)}, u32[]{:S(2)}, u32[]{:S(2)}) async-start(bf16[4,128,1024]{2,1,0:T(8,128)(2,1)} %shard_map.124), calls=%async_computation | async-start | bytes 2097152 | tf_op jit(solution)/shard_map/all_to_all | solution.py:642
  71.0 5.6 %collective-permute-start.15 = (f32[32,128]{1,0:T(8,128)S(1)}, f32[32,128]{1,0:T(8,128)S(1)}, u32[]{:S(2)}, u32[]{:S(2)}) collective-permute-start(f32[32,128]{1,0:T(8,128)S(1)} %get-tuple-element.63.refs_1_.own_ref), channel_id=1, source_target_pairs={{16,20},{17,21},{18,22},{19,23},{20,16},{21,17},{22,18},{23,19},{2... | collective-permute-start | bytes 49160 | tf_op jit(solution)/shard_map/ppermute | solution.py:571
  73.0 13.4 %collective-permute-start.14 = (bf16[32,4096]{1,0:T(8,128)(2,1)S(1)}, bf16[32,4096]{1,0:T(8,128)(2,1)S(1)}, u32[]{:S(2)}, u32[]{:S(2)}) collective-permute-start(bf16[32,4096]{1,0:T(8,128)(2,1)S(1)} %get-tuple-element.68), channel_id=1, source_target_pairs={{8,12},{9,13},{10,14},{11,15}} | collective-permute-start | bytes 786440 | tf_op jit(solution)/shard_map/ppermute | solution.py:571
  73.7 12.7 %collective-permute-start.13 = (bf16[32,4096]{1,0:T(8,128)(2,1)S(1)}, bf16[32,4096]{1,0:T(8,128)(2,1)S(1)}, u32[]{:S(2)}, u32[]{:S(2)}) collective-permute-start(bf16[32,4096]{1,0:T(8,128)(2,1)S(1)} %get-tuple-element.68), channel_id=1, source_target_pairs={{20,12},{21,13},{22,14},{23,15}} | collective-permute-start | bytes 786440 | tf_op jit(solution)/shard_map/ppermute | solution.py:571
  76.6 9.8 %copy-start.2 = (bf16[1,32,4096]{2,1,0:T(8,128)(2,1)S(1)}, bf16[1,32,4096]{2,1,0:T(8,128)(2,1)}, u32[]{:S(2)}) copy-start(bf16[1,32,4096]{2,1,0:T(8,128)(2,1)} %enc_ref.3) | copy-start | bytes 786436
  76.6 10.9 %collective-permute-start.18 = (f32[32,128]{1,0:T(8,128)S(1)}, f32[32,128]{1,0:T(8,128)S(1)}, u32[]{:S(2)}, u32[]{:S(2)}) collective-permute-start(f32[32,128]{1,0:T(8,128)S(1)} %shard_map.128.own_ref), channel_id=1, source_target_pairs={{16,4},{17,5},{18,6},{19,7},{20,12},{21,13},{22,14},{23,15},{24,0}... | collective-permute-start | bytes 49160 | tf_op jit(solution)/shard_map/ppermute | solution.py:571
  78.0 9.5 %collective-permute-start.17 = (f32[32,128]{1,0:T(8,128)S(1)}, f32[32,128]{1,0:T(8,128)S(1)}, u32[]{:S(2)}, u32[]{:S(2)}) collective-permute-start(f32[32,128]{1,0:T(8,128)S(1)} %shard_map.128.own_ref), channel_id=1, source_target_pairs={{16,0},{17,1},{18,2},{19,3},{20,8},{21,9},{22,10},{23,11},{24,4},{... | collective-permute-start | bytes 49160 | tf_op jit(solution)/shard_map/ppermute | solution.py:571
  79.3 8.2 %collective-permute-start.16 = (f32[32,128]{1,0:T(8,128)S(1)}, f32[32,128]{1,0:T(8,128)S(1)}, u32[]{:S(2)}, u32[]{:S(2)}) collective-permute-start(f32[32,128]{1,0:T(8,128)S(1)} %shard_map.128.own_ref), channel_id=1, source_target_pairs={{16,24},{17,25},{18,26},{19,27},{20,28},{21,29},{22,30},{23,31},{2... | collective-permute-start | bytes 49160 | tf_op jit(solution)/shard_map/ppermute | solution.py:571
  (1 other events, 0.7 us)

commit v6 on v5

--- a/solution.py
+++ b/solution.py
@@ -203,30 +203,6 @@
         in_specs=[VMEM] * 2 + [ANY] * len(tokens),
         out_specs=VMEM,
     )(first, second, *tokens)
-
-
-def join_heads(shares):
-    replicas, rows, piece = shares.shape
-
-    def kernel(share_ref, out_ref, token_ref, sems):
-        copies = []
-        for k in range(replicas):
-            columns = pl.ds(k * piece, piece)
-            copy = pltpu.make_async_copy(share_ref.at[k], out_ref.at[0, :, columns], sems.at[k])
-            copy.start()
-            copies.append(copy)
-        mark(token_ref)
-        for copy in copies:
-            copy.wait()
-
-    return call(
-        kernel,
-        [shape((1, rows, replicas * piece)), TOKEN],
-        moved=4 * rows * replicas * piece,
-        in_specs=[VMEM],
-        out_specs=[ANY, VMEM],
-        scratch_shapes=[pltpu.SemaphoreType.DMA((replicas,))],
-    )(shares)
 
 
 def hold_weights(w_key, w_value, tokens):
@@ -485,16 +461,33 @@
     )(own, came, token)
 
 
-def add_gains(terms, token):
-    def kernel(own_ref, other_ref, first_ref, second_ref, _, out_ref):
-        out_ref[...] = (own_ref[...] + other_ref[...]) + (first_ref[...] + second_ref[...])
-
-    return call(
-        kernel,
-        shape(terms[0].shape, jnp.float32),
-        in_specs=[VMEM] * 4 + [ANY],
-        out_specs=VMEM,
-    )(*terms, token)
+def close(terms, shares, tokens):
+    replicas, rows, piece = shares.shape
+
+    def kernel(own_ref, other_ref, first_ref, second_ref, share_ref, *refs):
+        out_ref, query_ref, held, sems = refs[len(tokens) :]
+        held[...] = (own_ref[...] + other_ref[...]) + (first_ref[...] + second_ref[...])
+        copies = [pltpu.make_async_copy(held, out_ref, sems.at[replicas])]
+        for k in range(replicas):
+            columns = pl.ds(k * piece, piece)
+            place = query_ref.at[0, :, columns]
+            copies.append(pltpu.make_async_copy(share_ref.at[k], place, sems.at[k]))
+        for copy in copies:
+            copy.start()
+        for copy in copies:
+            copy.wait()
+
+    return call(
+        kernel,
+        [shape(terms[0].shape, jnp.float32), shape((1, rows, replicas * piece))],
+        moved=4 * shares.size,
+        in_specs=[VMEM] * 5 + [ANY] * len(tokens),
+        out_specs=[ANY, ANY],
+        scratch_shapes=[
+            pltpu.VMEM(terms[0].shape, jnp.float32),
+            pltpu.SemaphoreType.DMA((replicas + 1,)),
+        ],
+    )(*terms, shares, *tokens)
 
 
 def weight_grads(memory, width, first, last, dk, dv, before, tokens=()):
@@ -526,7 +519,7 @@
     return grads, token
 
 
-def finish(holder, enc_state, gain, terms, tokens):
+def finish(holder, enc_state, gain, terms):
     rows, width = enc_state.shape[1:]
 
     def kernel(enc_ref, gain_ref, *refs):
@@ -545,9 +538,9 @@
         kernel,
         [shape((1, rows, width)), TOKEN],
         moved=8 * rows * width,
-        in_specs=[VMEM] * (2 + len(terms)) + [ANY] * len(tokens),
+        in_specs=[VMEM] * (2 + len(terms)),
         out_specs=[VMEM] * 2,
-    )(enc_state, gain, *terms, *tokens)
+    )(enc_state, gain, *terms)
 
 
 def on_device(enc_state, final_gain, queries, w_key, w_value, ctx_grad, mem_len):
@@ -584,7 +577,7 @@
     holding = add_blocks(came, [held])
     near, split = split_heads(queries, ctx_grad, [*groups, [0]], replicas, [holding])
     for stage in rounds[1:]:
-        arrived += [over_section(holding, group) for group in split_pairs(stage)]
+        arrived += [over_section(holding, group) for group in reversed(split_pairs(stage))]
         length = mem_len if stage is rounds[-1] else None
         holding = add_blocks(arrived, [split], length)
     blocks, tokens = {replicas // 2: came_far}, []
@@ -622,7 +615,8 @@
     key_weight_grad, value_weight_grad = grads
     dq = follow(dq, [gain_part])
     for number, stage in reversed(list(enumerate(rounds))):
-        came = [over_section(sent, [(b, a) for a, b in group]) for group in split_pairs(stage)]
+        groups = reversed(split_pairs(stage))
+        came = [over_section(sent, [(b, a) for a, b in group]) for group in groups]
         if number:
             sent, token = add_sections(sent, came)
     step = 1
@@ -638,11 +632,10 @@
         over_section(gain_part, [(half + i, places[i ^ step]) for i in range(half)]),
     ]
 
-    query_grad, joined = join_heads(
-        lax.all_to_all(dq, "dp", split_axis=0, concat_axis=0, tiled=True)
-    )
-    state_grad, done = finish(half - 1, enc_state, gain, came, [joined])
-    gain_grad = add_gains(terms, done).reshape(width)
+    state_grad, done = finish(half - 1, enc_state, gain, came)
+    dq = lax.all_to_all(dq, "dp", split_axis=0, concat_axis=0, tiled=True)
+    gain_grad, query_grad = close(terms, dq, [done])
+    gain_grad = gain_grad.reshape(final_gain.shape)
     return (query_grad, key_weight_grad, value_weight_grad, state_grad, gain_grad)
 
 

time: 88.7 us -> 87.9 us (level)
  the two profiles are of different devices: /device:TPU:16 before, /device:TPU:12 now
where the time goes in v6:
time: 87.9 us; the launch traced here: 86.9 us
  waiting for transfers between devices  32.2 us (37%)
  Pallas kernels  27.7 us (32%)
  starting transfers between devices  24.6 us (28%)
  between operations  1.7 us (2%)
    ppermute x12, waiting for transfers between devices, over_section(): return lax.ppermute(block, BOTH, pairs)  32.2 us
    ppermute x12, starting transfers between devices, over_section(): return lax.ppermute(block, BOTH, pairs)  16.2 us
    pallas_call x1, Pallas kernels, weight_grads(): call(kernel, [shape((1, width, columns))] * 2 + [TOKEN], flops=4 * rows *...  6.88 us
    pallas_call x1, Pallas kernels, hold_weights(): call(kernel, [shape(w_key.shape)] * 2 + [TOKEN], flops=COST_HOLD, moved=4...  6.06 us
    ppermute x7, starting transfers between devices, over_dp(): return lax.ppermute(block, BOTH, pairs)  4.86 us
    pallas_call x1, Pallas kernels, memory_part(): call(kernel, [shape((keep, depth), jnp.float32), shape((keep, depth + 2 *...  4.66 us
    all_to_all x1, starting transfers between devices, on_device(): dq = lax.all_to_all(dq, 'dp', split_axis=0, concat_axis=0, tiled=True)  3.53 us
    pallas_call x1, Pallas kernels, project(): call(kernel, [shape((rows, width))] * 2, flops=4 * rows * depth * width,...  2.45 us
  transfers between devices with their start and end apart: 20, of which 1 were waited for; matrix products, arithmetic and copies ran while one was open for 0% of the time, Pallas kernels for 21%

profile of v6, /device:TPU:12, one launch (start us, length us, event | category | flops | bytes accessed | tf_op | source)
XLA Modules:
  0.0 86.9 jit_solution(3276663011660378720)
XLA Ops:
  0.6 2.4 %shard_map.110 = (bf16[32,4096]{1,0:T(8,128)(2,1)}, bf16[2,2,128,1024]{3,2,1,0:T(8,128)(2,1)}, f32[8,128]{1,0:T(8,128)}) custom-call(bf16[1,32,4096]{2,1,0:T(8,128)(2,1)} %enc_ref.3, f32[1,4096]{1,0:T(1,128)} %bitcast.2, bf16[1,128,4096]{2,1,0:T(8,128)(2,1)} %query_ref.3, bf16[1,128,4096]{2,1,0:T(8,128)(2,1)} %grad_ref.3), custom_call_target="tpu_custom_call" | custom-call | bytes 2621440 | tf_op jit(solution)/shard_map/pallas_call | solution.py:119
  3.0 0.7 collective-permute-start.7
  3.8 2.4 %collective-permute-start.1 = (bf16[32,4096]{1,0:T(8,128)(2,1)}, bf16[32,4096]{1,0:T(8,128)(2,1)S(1)}, u32[]{:S(2)}, u32[]{:S(2)}) collective-permute-start(bf16[32,4096]{1,0:T(8,128)(2,1)} %get-tuple-element.39), channel_id=1, source_target_pairs={{12,8},{13,9},{14,10},{15,11}} | collective-permute-start | bytes 786440 | tf_op jit(solution)/shard_map/ppermute | solution.py:564
  6.2 4.4 %collective-permute-start = (bf16[32,4096]{1,0:T(8,128)(2,1)}, bf16[32,4096]{1,0:T(8,128)(2,1)S(1)}, u32[]{:S(2)}, u32[]{:S(2)}) collective-permute-start(bf16[32,4096]{1,0:T(8,128)(2,1)} %get-tuple-element.39), channel_id=1, source_target_pairs={{12,20},{13,21},{14,22},{15,23}} | collective-permute-start | bytes 786440 | tf_op jit(solution)/shard_map/ppermute | solution.py:564
  11.3 6.1 %shard_map.111 = (bf16[1,4096,1024]{2,1,0:T(8,128)(2,1)S(1)}, bf16[1,4096,1024]{2,1,0:T(8,128)(2,1)S(1)}, f32[8,128]{1,0:T(8,128)S(1)}) custom-call(bf16[1,4096,1024]{2,1,0:T(8,128)(2,1)} %wk_ref.1, bf16[1,4096,1024]{2,1,0:T(8,128)(2,1)} %wv_ref.1, f32[8,128]{1,0:T(8,128)S(1)} %copy-done.4), custom_call_target="tpu_custom_call" | custom-call | flops 1073741824 | bytes 16777216 | tf_op jit(solution)/shard_map/pallas_call | solution.py:225
  19.0 0.7 collective-permute-start.5
  20.4 0.7 collective-permute-start.4
  21.1 0.7 collective-permute-start.6
  21.9 0.7 collective-permute-start.8
  22.7 2.5 %shard_map.117 = (bf16[128,1024]{1,0:T(8,128)(2,1)S(1)}, bf16[128,1024]{1,0:T(8,128)(2,1)S(1)}) custom-call(bf16[128,4224]{1,0:T(8,128)(2,1)S(1)} %shard_map.116.memory_ref, bf16[1,4096,1024]{2,1,0:T(8,128)(2,1)S(1)} %get-tuple-element.44.wk_ref, bf16[1,4096,1024]{2,1,0:T(8,128)(2,1)S(1)} %get-tuple-element.45.wv_ref), custom_call_target="tpu_custom_call" | custom-call | flops 2147483648 | bytes 16777216 | tf_op jit(solution)/shard_map/pallas_call | solution.py:246
  25.2 1.1 %shard_map.118 = (bf16[128,1024]{1,0:T(8,128)(2,1)S(1)}, bf16[128,1024]{1,0:T(8,128)(2,1)S(1)}, bf16[2,16,32,128]{3,2,1,0:T(8,128)(2,1)S(1)}) custom-call(bf16[128,4224]{1,0:T(8,128)(2,1)S(1)} %shard_map.116.memory_ref, bf16[128,1024]{1,0:T(8,128)(2,1)S(1)} %get-tuple-element.46.key_ref, bf16[128,1024]{1,0:T(8,128)(2,1)S(1)} %get-tuple-element.47.value_ref, ...), custom_call_target="tpu_custom_call" | custom-call | flops 134217728 | bytes 4194304 | tf_op jit(solution)/shard_map/pallas_call | solution.py:296
  26.3 4.7 %shard_map.119 = (f32[64,4096]{1,0:T(8,128)S(1)}, bf16[64,4352]{1,0:T(8,128)(2,1)S(1)}, f32[32,128]{1,0:T(8,128)S(1)}) custom-call(bf16[128,4224]{1,0:T(8,128)(2,1)S(1)} %shard_map.116.memory_ref, bf16[128,1024]{1,0:T(8,128)(2,1)S(1)} %get-tuple-element.50.dk_ref, bf16[128,1024]{1,0:T(8,128)(2,1)S(1)} %get-tuple-element.51.dv_ref, ...), custom_call_target="tpu_custom_call" | custom-call | flops 2147483648 | bytes 16777216 | tf_op jit(solution)/shard_map/pallas_call | solution.py:370
  31.0 0.7 collective-permute-start.9
  31.7 1.5 %shard_map.120 = (bf16[4,128,1024]{2,1,0:T(8,128)(2,1)}, f32[8,128]{1,0:T(8,128)S(1)}) custom-call(bf16[2,16,32,128]{3,2,1,0:T(8,128)(2,1)S(1)} %get-tuple-element.55.score_ref, bf16[128,1024]{1,0:T(8,128)(2,1)S(1)} %get-tuple-element.46.key_ref, f32[32,128]{1,0:T(8,128)S(1)} %get-tuple-element.54.refs_0_.gain_ref), custom_call_target="tpu_custom_call" | custom-call | flops 33554432 | bytes 2097152 | tf_op jit(solution)/shard_map/pallas_call | solution.py:326
  33.3 0.7 collective-permute-start.10
  34.0 6.9 %shard_map.122 = (bf16[1,4096,1024]{2,1,0:T(8,128)(2,1)}, bf16[1,4096,1024]{2,1,0:T(8,128)(2,1)}, f32[8,128]{1,0:T(8,128)S(1)}) custom-call(bf16[128,4224]{1,0:T(8,128)(2,1)S(1)} %shard_map.116.memory_ref, bf16[128,1024]{1,0:T(8,128)(2,1)S(1)} %get-tuple-element.50.dk_ref, bf16[128,1024]{1,0:T(8,128)(2,1)S(1)} %get-tuple-element.51.dv_ref, ...), custom_call_target="tpu_custom_call" | custom-call | flops 2147483648 | bytes 16777216 | tf_op jit(solution)/shard_map/pallas_call | solution.py:508
  42.3 3.5 %all-to-all-start = ((bf16[4,128,1024]{2,1,0:T(8,128)(2,1)}), bf16[4,128,1024]{2,1,0:T(8,128)(2,1)S(1)}, u32[]{:S(2)}, u32[]{:S(2)}) async-start(bf16[4,128,1024]{2,1,0:T(8,128)(2,1)} %shard_map.126), calls=%async_computation | async-start | bytes 2097152 | tf_op jit(solution)/shard_map/all_to_all | solution.py:636
  46.6 1.4 %collective-permute-start.18 = (bf16[32,4096]{1,0:T(8,128)(2,1)S(1)}, bf16[32,4096]{1,0:T(8,128)(2,1)S(1)}, u32[]{:S(2)}, u32[]{:S(2)}) collective-permute-start(bf16[32,4096]{1,0:T(8,128)(2,1)S(1)} %get-tuple-element.66), channel_id=1, source_target_pairs={{20,12},{21,13},{22,14},{23,15}} | collective-permute-start | bytes 786440 | tf_op jit(solution)/shard_map/ppermute | solution.py:564
  48.1 1.3 %collective-permute-start.17 = (bf16[32,4096]{1,0:T(8,128)(2,1)S(1)}, bf16[32,4096]{1,0:T(8,128)(2,1)S(1)}, u32[]{:S(2)}, u32[]{:S(2)}) collective-permute-start(bf16[32,4096]{1,0:T(8,128)(2,1)S(1)} %get-tuple-element.66), channel_id=1, source_target_pairs={{8,12},{9,13},{10,14},{11,15}} | collective-permute-start | bytes 786440 | tf_op jit(solution)/shard_map/ppermute | solution.py:564
  49.4 1.3 %collective-permute-start.16 = (f32[32,128]{1,0:T(8,128)S(1)}, f32[32,128]{1,0:T(8,128)S(1)}, u32[]{:S(2)}, u32[]{:S(2)}) collective-permute-start(f32[32,128]{1,0:T(8,128)S(1)} %shard_map.125.own_ref), channel_id=1, source_target_pairs={{16,4},{17,5},{18,6},{19,7},{20,12},{21,13},{22,14},{23,15},{24,0}... | collective-permute-start | bytes 49160 | tf_op jit(solution)/shard_map/ppermute | solution.py:564
  50.7 1.3 %collective-permute-start.15 = (f32[32,128]{1,0:T(8,128)S(1)}, f32[32,128]{1,0:T(8,128)S(1)}, u32[]{:S(2)}, u32[]{:S(2)}) collective-permute-start(f32[32,128]{1,0:T(8,128)S(1)} %shard_map.125.own_ref), channel_id=1, source_target_pairs={{16,0},{17,1},{18,2},{19,3},{20,8},{21,9},{22,10},{23,11},{24,4},{... | collective-permute-start | bytes 49160 | tf_op jit(solution)/shard_map/ppermute | solution.py:564
  52.7 32.2 %collective-permute-done.18.refs_1_ = bf16[32,4096]{1,0:T(8,128)(2,1)S(1)} collective-permute-done((bf16[32,4096]{1,0:T(8,128)(2,1)S(1)}, bf16[32,4096]{1,0:T(8,128)(2,1)S(1)}, u32[]{:S(2)}, u32[]{:S(2)}) %collective-permute-start.18) | collective-permute-done | bytes 262176 | tf_op jit(solution)/shard_map/ppermute | solution.py:564
  84.8 1.1 %shard_map.127 = (bf16[1,32,4096]{2,1,0:T(8,128)(2,1)}, f32[8,128]{1,0:T(8,128)S(1)}) custom-call(bf16[1,32,4096]{2,1,0:T(8,128)(2,1)S(1)} %copy-done.2, f32[1,4096]{1,0:T(1,128)S(1)} %bitcast.4, bf16[32,4096]{1,0:T(8,128)(2,1)S(1)} %collective-permute-done.17.refs_0_, bf16[32,4096]{1,0:T(8,128)(2,1)S(1)} %collective-permute-done.18.refs_1_), custom_call_target="tpu_custom_call" | custom-call | bytes 1048576 | tf_op jit(solution)/shard_map/pallas_call | solution.py:537
  85.9 1.0 %shard_map.128 = (f32[32,128]{1,0:T(8,128)}, bf16[1,128,4096]{2,1,0:T(8,128)(2,1)}) custom-call(f32[32,128]{1,0:T(8,128)S(1)} %shard_map.125.own_ref, f32[32,128]{1,0:T(8,128)S(1)} %collective-permute-done.14.other_ref, f32[32,128]{1,0:T(8,128)S(1)} %collective-permute-done.15.first_ref, f32[32,128]{1,0:T(8,128)S(1)} %collective-permute-done.16.second_ref, ...), custom_call_target="tpu_custom_call" | custom-call | bytes 2097152 | tf_op jit(solution)/shard_map/pallas_call | solution.py:480
  (46 shorter events, 5.4 us)
Async XLA Ops:
  3.0 18.8 %collective-permute-start.7 = (bf16[2,2,128,1024]{3,2,1,0:T(8,128)(2,1)}, bf16[2,2,128,1024]{3,2,1,0:T(8,128)(2,1)S(1)}, u32[]{:S(2)}, u32[]{:S(2)}) collective-permute-start(bf16[2,2,128,1024]{3,2,1,0:T(8,128)(2,1)} %get-tuple-element.49), channel_id=1, source_target_pairs={{16,18},{17,19},{18,16},{19,17},{20,22},{21,23},{22,20},{23,21},{2... | collective-permute-start | bytes 3145736 | tf_op jit(solution)/shard_map/ppermute | solution.py:560
  3.8 13.6 %collective-permute-start.1 = (bf16[32,4096]{1,0:T(8,128)(2,1)}, bf16[32,4096]{1,0:T(8,128)(2,1)S(1)}, u32[]{:S(2)}, u32[]{:S(2)}) collective-permute-start(bf16[32,4096]{1,0:T(8,128)(2,1)} %get-tuple-element.39), channel_id=1, source_target_pairs={{12,8},{13,9},{14,10},{15,11}} | collective-permute-start | bytes 786440 | tf_op jit(solution)/shard_map/ppermute | solution.py:564
  6.2 11.2 %collective-permute-start = (bf16[32,4096]{1,0:T(8,128)(2,1)}, bf16[32,4096]{1,0:T(8,128)(2,1)S(1)}, u32[]{:S(2)}, u32[]{:S(2)}) collective-permute-start(bf16[32,4096]{1,0:T(8,128)(2,1)} %get-tuple-element.39), channel_id=1, source_target_pairs={{12,20},{13,21},{14,22},{15,23}} | collective-permute-start | bytes 786440 | tf_op jit(solution)/shard_map/ppermute | solution.py:564
  11.3 7.5 %copy-start = (bf16[1,128,4096]{2,1,0:T(8,128)(2,1)S(1)}, bf16[1,128,4096]{2,1,0:T(8,128)(2,1)}, u32[]{:S(2)}) copy-start(bf16[1,128,4096]{2,1,0:T(8,128)(2,1)} %query_ref.3) | copy-start | bytes 3145732
  11.3 7.5 %copy-start.1 = (bf16[1,128,4096]{2,1,0:T(8,128)(2,1)S(1)}, bf16[1,128,4096]{2,1,0:T(8,128)(2,1)}, u32[]{:S(2)}) copy-start(bf16[1,128,4096]{2,1,0:T(8,128)(2,1)} %grad_ref.3) | copy-start | bytes 3145732
  17.4 2.9 %collective-permute-start.3 = (bf16[32,4096]{1,0:T(8,128)(2,1)S(1)}, bf16[32,4096]{1,0:T(8,128)(2,1)S(1)}, u32[]{:S(2)}, u32[]{:S(2)}) collective-permute-start(bf16[32,4096]{1,0:T(8,128)(2,1)S(1)} %shard_map.112.refs_0_), channel_id=1, source_target_pairs={{20,28},{21,29},{22,30},{23,31},{8,24},{9,25},{10,26},{11,27}} | collective-permute-start | bytes 786440 | tf_op jit(solution)/shard_map/ppermute | solution.py:564
  18.1 2.2 %collective-permute-start.2 = (bf16[32,4096]{1,0:T(8,128)(2,1)S(1)}, bf16[32,4096]{1,0:T(8,128)(2,1)S(1)}, u32[]{:S(2)}, u32[]{:S(2)}) collective-permute-start(bf16[32,4096]{1,0:T(8,128)(2,1)S(1)} %shard_map.112.refs_0_), channel_id=1, source_target_pairs={{20,16},{21,17},{22,18},{23,19}} | collective-permute-start | bytes 786440 | tf_op jit(solution)/shard_map/ppermute | solution.py:564
  19.0 2.1 %collective-permute-start.5 = (bf16[1,2,128,1024]{3,2,1,0:T(8,128)(2,1)S(1)}, bf16[1,2,128,1024]{3,2,1,0:T(8,128)(2,1)S(1)}, u32[]{:S(2)}, u32[]{:S(2)}) collective-permute-start(bf16[1,2,128,1024]{3,2,1,0:T(8,128)(2,1)S(1)} %get-tuple-element.43), channel_id=1, source_target_pairs={{16,17},{17,16},{18,19},{19,18},{20,21},{21,20},{22,23},{23,22},{2... | collective-permute-start | bytes 1572872 | tf_op jit(solution)/shard_map/ppermute | solution.py:560
  20.4 0.7 collective-permute-start.4
  21.1 1.5 %collective-permute-start.6 = (bf16[64,4224]{1,0:T(8,128)(2,1)S(1)}, bf16[64,4224]{1,0:T(8,128)(2,1)S(1)}, u32[]{:S(2)}, u32[]{:S(2)}) collective-permute-start(bf16[64,4224]{1,0:T(8,128)(2,1)S(1)} %shard_map.115.first_ref), channel_id=1, source_target_pairs={{16,17},{17,16},{18,19},{19,18},{20,21},{21,20},{22,23},{23,22},{2... | collective-permute-start | bytes 1622024 | tf_op jit(solution)/shard_map/ppermute | solution.py:560
  21.9 3.3 %collective-permute-start.8 = (bf16[1,2,128,1024]{3,2,1,0:T(8,128)(2,1)S(1)}, bf16[1,2,128,1024]{3,2,1,0:T(8,128)(2,1)S(1)}, u32[]{:S(2)}, u32[]{:S(2)}) collective-permute-start(bf16[1,2,128,1024]{3,2,1,0:T(8,128)(2,1)S(1)} %slice.4), channel_id=1, source_target_pairs={{16,17},{17,16},{18,19},{19,18},{20,21},{21,20},{22,23},{23,22},{2... | collective-permute-start | bytes 1572872 | tf_op jit(solution)/shard_map/ppermute | solution.py:560
  22.7 3.6 %copy-start.3 = (f32[4096]{0:T(1024)S(1)}, f32[4096]{0:T(1024)}, u32[]{:S(2)}) copy-start(f32[4096]{0:T(1024)} %param.8) | copy-start | bytes 49156
  31.0 2.2 %collective-permute-start.9 = (bf16[64,4352]{1,0:T(8,128)(2,1)S(1)}, bf16[64,4352]{1,0:T(8,128)(2,1)S(1)}, u32[]{:S(2)}, u32[]{:S(2)}) collective-permute-start(bf16[64,4352]{1,0:T(8,128)(2,1)S(1)} %get-tuple-element.53), channel_id=1, source_target_pairs={{16,17},{17,16},{18,19},{19,18},{20,21},{21,20},{22,23},{23,22},{2... | collective-permute-start | bytes 1671176 | tf_op jit(solution)/shard_map/ppermute | solution.py:560
  33.3 7.6 %collective-permute-start.10 = (bf16[32,4352]{1,0:T(8,128)(2,1)S(1)}, bf16[32,4352]{1,0:T(8,128)(2,1)S(1)}, u32[]{:S(2)}, u32[]{:S(2)}) collective-permute-start(bf16[32,4352]{1,0:T(8,128)(2,1)S(1)} %get-tuple-element.58), channel_id=1, source_target_pairs={{16,18},{17,19},{18,16},{19,17},{20,22},{21,23},{22,20},{23,21},{2... | collective-permute-start | bytes 835592 | tf_op jit(solution)/shard_map/ppermute | solution.py:560
  40.9 5.6 %collective-permute-start.13 = (bf16[32,4096]{1,0:T(8,128)(2,1)S(1)}, bf16[32,4096]{1,0:T(8,128)(2,1)S(1)}, u32[]{:S(2)}, u32[]{:S(2)}) collective-permute-start(bf16[32,4096]{1,0:T(8,128)(2,1)S(1)} %get-tuple-element.63.own_ref), channel_id=1, source_target_pairs={{28,20},{29,21},{30,22},{31,23},{24,8},{25,9},{26,10},{27,11}} | collective-permute-start | bytes 786440 | tf_op jit(solution)/shard_map/ppermute | solution.py:564
  41.6 4.9 %collective-permute-start.12 = (bf16[32,4096]{1,0:T(8,128)(2,1)S(1)}, bf16[32,4096]{1,0:T(8,128)(2,1)S(1)}, u32[]{:S(2)}, u32[]{:S(2)}) collective-permute-start(bf16[32,4096]{1,0:T(8,128)(2,1)S(1)} %get-tuple-element.63.own_ref), channel_id=1, source_target_pairs={{16,20},{17,21},{18,22},{19,23}} | collective-permute-start | bytes 786440 | tf_op jit(solution)/shard_map/ppermute | solution.py:564
  42.3 43.6 %all-to-all-start = ((bf16[4,128,1024]{2,1,0:T(8,128)(2,1)}), bf16[4,128,1024]{2,1,0:T(8,128)(2,1)S(1)}, u32[]{:S(2)}, u32[]{:S(2)}) async-start(bf16[4,128,1024]{2,1,0:T(8,128)(2,1)} %shard_map.126), calls=%async_computation | async-start | bytes 2097152 | tf_op jit(solution)/shard_map/all_to_all | solution.py:636
  45.8 3.5 %collective-permute-start.11 = (f32[32,128]{1,0:T(8,128)S(1)}, f32[32,128]{1,0:T(8,128)S(1)}, u32[]{:S(2)}, u32[]{:S(2)}) collective-permute-start(f32[32,128]{1,0:T(8,128)S(1)} %get-tuple-element.62.own_ref.refs_1_), channel_id=1, source_target_pairs={{16,20},{17,21},{18,22},{19,23},{20,16},{21,17},{22,18},{23,19},{2... | collective-permute-start | bytes 49160 | tf_op jit(solution)/shard_map/ppermute | solution.py:564
  46.6 38.2 %copy-start.2 = (bf16[1,32,4096]{2,1,0:T(8,128)(2,1)S(1)}, bf16[1,32,4096]{2,1,0:T(8,128)(2,1)}, u32[]{:S(2)}) copy-start(bf16[1,32,4096]{2,1,0:T(8,128)(2,1)} %enc_ref.3) | copy-start | bytes 786436
  46.6 38.2 %collective-permute-start.18 = (bf16[32,4096]{1,0:T(8,128)(2,1)S(1)}, bf16[32,4096]{1,0:T(8,128)(2,1)S(1)}, u32[]{:S(2)}, u32[]{:S(2)}) collective-permute-start(bf16[32,4096]{1,0:T(8,128)(2,1)S(1)} %get-tuple-element.66), channel_id=1, source_target_pairs={{20,12},{21,13},{22,14},{23,15}} | collective-permute-start | bytes 786440 | tf_op jit(solution)/shard_map/ppermute | solution.py:564
  48.1 36.7 %collective-permute-start.17 = (bf16[32,4096]{1,0:T(8,128)(2,1)S(1)}, bf16[32,4096]{1,0:T(8,128)(2,1)S(1)}, u32[]{:S(2)}, u32[]{:S(2)}) collective-permute-start(bf16[32,4096]{1,0:T(8,128)(2,1)S(1)} %get-tuple-element.66), channel_id=1, source_target_pairs={{8,12},{9,13},{10,14},{11,15}} | collective-permute-start | bytes 786440 | tf_op jit(solution)/shard_map/ppermute | solution.py:564
  49.4 36.5 %collective-permute-start.16 = (f32[32,128]{1,0:T(8,128)S(1)}, f32[32,128]{1,0:T(8,128)S(1)}, u32[]{:S(2)}, u32[]{:S(2)}) collective-permute-start(f32[32,128]{1,0:T(8,128)S(1)} %shard_map.125.own_ref), channel_id=1, source_target_pairs={{16,4},{17,5},{18,6},{19,7},{20,12},{21,13},{22,14},{23,15},{24,0}... | collective-permute-start | bytes 49160 | tf_op jit(solution)/shard_map/ppermute | solution.py:564
  50.7 35.2 %collective-permute-start.15 = (f32[32,128]{1,0:T(8,128)S(1)}, f32[32,128]{1,0:T(8,128)S(1)}, u32[]{:S(2)}, u32[]{:S(2)}) collective-permute-start(f32[32,128]{1,0:T(8,128)S(1)} %shard_map.125.own_ref), channel_id=1, source_target_pairs={{16,0},{17,1},{18,2},{19,3},{20,8},{21,9},{22,10},{23,11},{24,4},{... | collective-permute-start | bytes 49160 | tf_op jit(solution)/shard_map/ppermute | solution.py:564
  52.0 33.9 %collective-permute-start.14 = (f32[32,128]{1,0:T(8,128)S(1)}, f32[32,128]{1,0:T(8,128)S(1)}, u32[]{:S(2)}, u32[]{:S(2)}) collective-permute-start(f32[32,128]{1,0:T(8,128)S(1)} %shard_map.125.own_ref), channel_id=1, source_target_pairs={{16,24},{17,25},{18,26},{19,27},{20,28},{21,29},{22,30},{23,31},{2... | collective-permute-start | bytes 49160 | tf_op jit(solution)/shard_map/ppermute | solution.py:564
  (1 other events, 0.7 us)

commit v7 on v6

--- a/solution.py
+++ b/solution.py
@@ -188,21 +188,21 @@
     )(*blocks, *scalars, *tokens)
 
 
-def stack_rows(first, second, tokens):
-    rows, width = first.shape
-
-    def kernel(first_ref, second_ref, *refs):
-        out_ref = refs[-1]
-        out_ref[:rows] = first_ref[...]
-        out_ref[rows:] = second_ref[...]
-
-    return call(
-        kernel,
-        shape((2 * rows, width)),
-        moved=8 * first.size,
-        in_specs=[VMEM] * 2 + [ANY] * len(tokens),
+def stack_rows(blocks, places, tokens):
+    rows, width = blocks[0].shape
+    count = len(blocks)
+
+    def kernel(*refs):
+        for i, ref in zip(places, refs[len(tokens) :], strict=False):
+            refs[-1][i * rows : (i + 1) * rows] = ref[...]
+
+    return call(
+        kernel,
+        shape((count * rows, width)),
+        moved=4 * count * rows * width,
+        in_specs=[ANY] * len(tokens) + [VMEM] * count,
         out_specs=VMEM,
-    )(first, second, *tokens)
+    )(*tokens, *blocks)
 
 
 def hold_weights(w_key, w_value, tokens):
@@ -580,18 +580,23 @@
         arrived += [over_section(holding, group) for group in reversed(split_pairs(stage))]
         length = mem_len if stage is rounds[-1] else None
         holding = add_blocks(arrived, [split], length)
-    blocks, tokens = {replicas // 2: came_far}, []
+    blocks = {replicas // 2: came_far}
     for bit, share in zip(reversed(range(bits - 1)), near, strict=False):
         size = 1 << bit
         passed = {k ^ size: over_dp(b[size : 2 * size], size) for k, b in blocks.items()}
         blocks = blocks | passed | {size: over_dp(share, size)}
-        tokens.append(blocks[size])
+    pieces = {0: holding}
+    for k in range(1, replicas):
+        step = k & -k
+        block = pieces[k ^ step]
+        if k ^ step:
+            block = stack_rows([block], [0], [pieces[step], blocks[step]])
+        pieces[k] = over_dp(block, step)
+    places = [order.index(k) for k in range(replicas)]
+    passed = [blocks[k] for k in range(1, replicas)]
+    pieces = stack_rows([pieces[k] for k in range(replicas)], places, passed)
     blocks[0] = near[-1]
     shares = [blocks[k] for k in order]
-    for bit in reversed(range(bits)):
-        holding = stack_rows(holding, over_dp(holding, 1 << bit), tokens)
-        tokens = []
-    pieces = holding
     keys, values = project(pieces, *weights)
     dk, dv, scores = attend(pieces, keys, values, shares, half)
 

time: 87.9 us -> 87 us (0.990)
  waiting for transfers between devices: 32.2 us -> 30.6 us
    ppermute x12, waiting for transfers between devices: 32.2 us -> 30.5 us  [over_section(): return lax.ppermute(block, BOTH, pairs)]
    ppermute x7 -> x8, starting transfers between devices: 4.86 us -> 5.52 us  [over_dp(): return lax.ppermute(block, BOTH, pairs)]
  transfers between devices with their start and end apart: 20 -> 21, of which waited for: 1 -> 1; matrix products, arithmetic and copies ran while one was open for 0% -> 0% of each run, Pallas kernels for 21% -> 18%
where the time goes in v7:
time: 87 us; the launch traced here: 85.9 us
  waiting for transfers between devices  30.6 us (35%)
  Pallas kernels  27.7 us (32%)
  starting transfers between devices  25.2 us (29%)
  between operations  1.71 us (2%)
    ppermute x12, waiting for transfers between devices, over_section(): return lax.ppermute(block, BOTH, pairs)  30.5 us
    ppermute x12, starting transfers between devices, over_section(): return lax.ppermute(block, BOTH, pairs)  16.2 us
    pallas_call x1, Pallas kernels, weight_grads(): call(kernel, [shape((1, width, columns))] * 2 + [TOKEN], flops=4 * rows *...  6.88 us
    pallas_call x1, Pallas kernels, hold_weights(): call(kernel, [shape(w_key.shape)] * 2 + [TOKEN], flops=COST_HOLD, moved=4...  6.06 us
    ppermute x8, starting transfers between devices, over_dp(): return lax.ppermute(block, BOTH, pairs)  5.52 us
    pallas_call x1, Pallas kernels, memory_part(): call(kernel, [shape((keep, depth), jnp.float32), shape((keep, depth + 2 *...  4.66 us
    all_to_all x1, starting transfers between devices, on_device(): dq = lax.all_to_all(dq, 'dp', split_axis=0, concat_axis=0, tiled=True)  3.53 us
    pallas_call x1, Pallas kernels, project(): call(kernel, [shape((rows, width))] * 2, flops=4 * rows * depth * width,...  2.45 us
  transfers between devices with their start and end apart: 21, of which 1 were waited for; matrix products, arithmetic and copies ran while one was open for 0% of the time, Pallas kernels for 18%

profile of v7, /device:TPU:12, one launch (start us, length us, event | category | flops | bytes accessed | tf_op | source)
XLA Modules:
  0.0 85.9 jit_solution(10268103133795415287)
XLA Ops:
  0.6 2.4 %shard_map.110 = (bf16[32,4096]{1,0:T(8,128)(2,1)}, bf16[2,2,128,1024]{3,2,1,0:T(8,128)(2,1)}, f32[8,128]{1,0:T(8,128)}) custom-call(bf16[1,32,4096]{2,1,0:T(8,128)(2,1)} %enc_ref.3, f32[1,4096]{1,0:T(1,128)} %bitcast.2, bf16[1,128,4096]{2,1,0:T(8,128)(2,1)} %query_ref.3, bf16[1,128,4096]{2,1,0:T(8,128)(2,1)} %grad_ref.3), custom_call_target="tpu_custom_call" | custom-call | bytes 2621440 | tf_op jit(solution)/shard_map/pallas_call | solution.py:119
  3.0 0.7 collective-permute-start.3
  3.8 2.4 %collective-permute-start.1 = (bf16[32,4096]{1,0:T(8,128)(2,1)}, bf16[32,4096]{1,0:T(8,128)(2,1)S(1)}, u32[]{:S(2)}, u32[]{:S(2)}) collective-permute-start(bf16[32,4096]{1,0:T(8,128)(2,1)} %get-tuple-element.39), channel_id=1, source_target_pairs={{12,8},{13,9},{14,10},{15,11}} | collective-permute-start | bytes 786440 | tf_op jit(solution)/shard_map/ppermute | solution.py:564
  6.2 4.4 %collective-permute-start = (bf16[32,4096]{1,0:T(8,128)(2,1)}, bf16[32,4096]{1,0:T(8,128)(2,1)S(1)}, u32[]{:S(2)}, u32[]{:S(2)}) collective-permute-start(bf16[32,4096]{1,0:T(8,128)(2,1)} %get-tuple-element.39), channel_id=1, source_target_pairs={{12,20},{13,21},{14,22},{15,23}} | collective-permute-start | bytes 786440 | tf_op jit(solution)/shard_map/ppermute | solution.py:564
  11.3 6.1 %shard_map.111 = (bf16[1,4096,1024]{2,1,0:T(8,128)(2,1)S(1)}, bf16[1,4096,1024]{2,1,0:T(8,128)(2,1)S(1)}, f32[8,128]{1,0:T(8,128)S(1)}) custom-call(bf16[1,4096,1024]{2,1,0:T(8,128)(2,1)} %wk_ref.1, bf16[1,4096,1024]{2,1,0:T(8,128)(2,1)} %wv_ref.1, f32[8,128]{1,0:T(8,128)S(1)} %copy-done.4), custom_call_target="tpu_custom_call" | custom-call | flops 1073741824 | bytes 16777216 | tf_op jit(solution)/shard_map/pallas_call | solution.py:225
  19.0 0.7 collective-permute-start.2
  21.1 0.7 collective-permute-start.7
  21.8 0.7 collective-permute-start.4
  22.6 0.7 collective-permute-start.9
  23.4 2.5 %shard_map.117 = (bf16[128,1024]{1,0:T(8,128)(2,1)S(1)}, bf16[128,1024]{1,0:T(8,128)(2,1)S(1)}) custom-call(bf16[128,4224]{1,0:T(8,128)(2,1)S(1)} %shard_map.116.memory_ref, bf16[1,4096,1024]{2,1,0:T(8,128)(2,1)S(1)} %get-tuple-element.45.wk_ref, bf16[1,4096,1024]{2,1,0:T(8,128)(2,1)S(1)} %get-tuple-element.46.wv_ref), custom_call_target="tpu_custom_call" | custom-call | flops 2147483648 | bytes 16777216 | tf_op jit(solution)/shard_map/pallas_call | solution.py:246
  25.8 1.1 %shard_map.118 = (bf16[128,1024]{1,0:T(8,128)(2,1)S(1)}, bf16[128,1024]{1,0:T(8,128)(2,1)S(1)}, bf16[2,16,32,128]{3,2,1,0:T(8,128)(2,1)S(1)}) custom-call(bf16[128,4224]{1,0:T(8,128)(2,1)S(1)} %shard_map.116.memory_ref, bf16[128,1024]{1,0:T(8,128)(2,1)S(1)} %get-tuple-element.47.key_ref, bf16[128,1024]{1,0:T(8,128)(2,1)S(1)} %get-tuple-element.48.value_ref, ...), custom_call_target="tpu_custom_call" | custom-call | flops 134217728 | bytes 4194304 | tf_op jit(solution)/shard_map/pallas_call | solution.py:296
  27.0 4.7 %shard_map.119 = (f32[64,4096]{1,0:T(8,128)S(1)}, bf16[64,4352]{1,0:T(8,128)(2,1)S(1)}, f32[32,128]{1,0:T(8,128)S(1)}) custom-call(bf16[128,4224]{1,0:T(8,128)(2,1)S(1)} %shard_map.116.memory_ref, bf16[128,1024]{1,0:T(8,128)(2,1)S(1)} %get-tuple-element.50.dk_ref, bf16[128,1024]{1,0:T(8,128)(2,1)S(1)} %get-tuple-element.51.dv_ref, ...), custom_call_target="tpu_custom_call" | custom-call | flops 2147483648 | bytes 16777216 | tf_op jit(solution)/shard_map/pallas_call | solution.py:370
  31.6 0.7 collective-permute-start.10
  32.3 1.5 %shard_map.120 = (bf16[4,128,1024]{2,1,0:T(8,128)(2,1)}, f32[8,128]{1,0:T(8,128)S(1)}) custom-call(bf16[2,16,32,128]{3,2,1,0:T(8,128)(2,1)S(1)} %get-tuple-element.55.score_ref, bf16[128,1024]{1,0:T(8,128)(2,1)S(1)} %get-tuple-element.47.key_ref, f32[32,128]{1,0:T(8,128)S(1)} %get-tuple-element.54.refs_0_.gain_ref), custom_call_target="tpu_custom_call" | custom-call | flops 33554432 | bytes 2097152 | tf_op jit(solution)/shard_map/pallas_call | solution.py:326
  33.9 0.7 collective-permute-start.11
  34.6 6.9 %shard_map.122 = (bf16[1,4096,1024]{2,1,0:T(8,128)(2,1)}, bf16[1,4096,1024]{2,1,0:T(8,128)(2,1)}, f32[8,128]{1,0:T(8,128)S(1)}) custom-call(bf16[128,4224]{1,0:T(8,128)(2,1)S(1)} %shard_map.116.memory_ref, bf16[128,1024]{1,0:T(8,128)(2,1)S(1)} %get-tuple-element.50.dk_ref, bf16[128,1024]{1,0:T(8,128)(2,1)S(1)} %get-tuple-element.51.dv_ref, ...), custom_call_target="tpu_custom_call" | custom-call | flops 2147483648 | bytes 16777216 | tf_op jit(solution)/shard_map/pallas_call | solution.py:508
  42.9 3.5 %all-to-all-start = ((bf16[4,128,1024]{2,1,0:T(8,128)(2,1)}), bf16[4,128,1024]{2,1,0:T(8,128)(2,1)S(1)}, u32[]{:S(2)}, u32[]{:S(2)}) async-start(bf16[4,128,1024]{2,1,0:T(8,128)(2,1)} %shard_map.126), calls=%async_computation | async-start | bytes 2097152 | tf_op jit(solution)/shard_map/all_to_all | solution.py:641
  47.3 1.4 %collective-permute-start.19 = (bf16[32,4096]{1,0:T(8,128)(2,1)S(1)}, bf16[32,4096]{1,0:T(8,128)(2,1)S(1)}, u32[]{:S(2)}, u32[]{:S(2)}) collective-permute-start(bf16[32,4096]{1,0:T(8,128)(2,1)S(1)} %get-tuple-element.66), channel_id=1, source_target_pairs={{20,12},{21,13},{22,14},{23,15}} | collective-permute-start | bytes 786440 | tf_op jit(solution)/shard_map/ppermute | solution.py:564
  48.7 1.3 %collective-permute-start.18 = (bf16[32,4096]{1,0:T(8,128)(2,1)S(1)}, bf16[32,4096]{1,0:T(8,128)(2,1)S(1)}, u32[]{:S(2)}, u32[]{:S(2)}) collective-permute-start(bf16[32,4096]{1,0:T(8,128)(2,1)S(1)} %get-tuple-element.66), channel_id=1, source_target_pairs={{8,12},{9,13},{10,14},{11,15}} | collective-permute-start | bytes 786440 | tf_op jit(solution)/shard_map/ppermute | solution.py:564
  50.0 1.3 %collective-permute-start.17 = (f32[32,128]{1,0:T(8,128)S(1)}, f32[32,128]{1,0:T(8,128)S(1)}, u32[]{:S(2)}, u32[]{:S(2)}) collective-permute-start(f32[32,128]{1,0:T(8,128)S(1)} %shard_map.125.own_ref), channel_id=1, source_target_pairs={{16,4},{17,5},{18,6},{19,7},{20,12},{21,13},{22,14},{23,15},{24,0}... | collective-permute-start | bytes 49160 | tf_op jit(solution)/shard_map/ppermute | solution.py:564
  51.3 1.3 %collective-permute-start.16 = (f32[32,128]{1,0:T(8,128)S(1)}, f32[32,128]{1,0:T(8,128)S(1)}, u32[]{:S(2)}, u32[]{:S(2)}) collective-permute-start(f32[32,128]{1,0:T(8,128)S(1)} %shard_map.125.own_ref), channel_id=1, source_target_pairs={{16,0},{17,1},{18,2},{19,3},{20,8},{21,9},{22,10},{23,11},{24,4},{... | collective-permute-start | bytes 49160 | tf_op jit(solution)/shard_map/ppermute | solution.py:564
  53.3 30.5 %collective-permute-done.19.refs_1_ = bf16[32,4096]{1,0:T(8,128)(2,1)S(1)} collective-permute-done((bf16[32,4096]{1,0:T(8,128)(2,1)S(1)}, bf16[32,4096]{1,0:T(8,128)(2,1)S(1)}, u32[]{:S(2)}, u32[]{:S(2)}) %collective-permute-start.19) | collective-permute-done | bytes 262176 | tf_op jit(solution)/shard_map/ppermute | solution.py:564
  83.8 1.1 %shard_map.127 = (bf16[1,32,4096]{2,1,0:T(8,128)(2,1)}, f32[8,128]{1,0:T(8,128)S(1)}) custom-call(bf16[1,32,4096]{2,1,0:T(8,128)(2,1)S(1)} %copy-done.2, f32[1,4096]{1,0:T(1,128)S(1)} %bitcast.4, bf16[32,4096]{1,0:T(8,128)(2,1)S(1)} %collective-permute-done.18.refs_0_, bf16[32,4096]{1,0:T(8,128)(2,1)S(1)} %collective-permute-done.19.refs_1_), custom_call_target="tpu_custom_call" | custom-call | bytes 1048576 | tf_op jit(solution)/shard_map/pallas_call | solution.py:537
  84.9 1.0 %shard_map.128 = (f32[32,128]{1,0:T(8,128)}, bf16[1,128,4096]{2,1,0:T(8,128)(2,1)}) custom-call(f32[32,128]{1,0:T(8,128)S(1)} %shard_map.125.own_ref, f32[32,128]{1,0:T(8,128)S(1)} %collective-permute-done.15.other_ref, f32[32,128]{1,0:T(8,128)S(1)} %collective-permute-done.16.first_ref, f32[32,128]{1,0:T(8,128)S(1)} %collective-permute-done.17.second_ref, ...), custom_call_target="tpu_custom_call" | custom-call | bytes 2097152 | tf_op jit(solution)/shard_map/pallas_call | solution.py:480
  (48 shorter events, 6.1 us)
Async XLA Ops:
  3.0 18.7 %collective-permute-start.3 = (bf16[2,2,128,1024]{3,2,1,0:T(8,128)(2,1)}, bf16[2,2,128,1024]{3,2,1,0:T(8,128)(2,1)S(1)}, u32[]{:S(2)}, u32[]{:S(2)}) collective-permute-start(bf16[2,2,128,1024]{3,2,1,0:T(8,128)(2,1)} %get-tuple-element.43), channel_id=1, source_target_pairs={{16,18},{17,19},{18,16},{19,17},{20,22},{21,23},{22,20},{23,21},{2... | collective-permute-start | bytes 3145736 | tf_op jit(solution)/shard_map/ppermute | solution.py:560
  3.8 13.6 %collective-permute-start.1 = (bf16[32,4096]{1,0:T(8,128)(2,1)}, bf16[32,4096]{1,0:T(8,128)(2,1)S(1)}, u32[]{:S(2)}, u32[]{:S(2)}) collective-permute-start(bf16[32,4096]{1,0:T(8,128)(2,1)} %get-tuple-element.39), channel_id=1, source_target_pairs={{12,8},{13,9},{14,10},{15,11}} | collective-permute-start | bytes 786440 | tf_op jit(solution)/shard_map/ppermute | solution.py:564
  6.2 11.2 %collective-permute-start = (bf16[32,4096]{1,0:T(8,128)(2,1)}, bf16[32,4096]{1,0:T(8,128)(2,1)S(1)}, u32[]{:S(2)}, u32[]{:S(2)}) collective-permute-start(bf16[32,4096]{1,0:T(8,128)(2,1)} %get-tuple-element.39), channel_id=1, source_target_pairs={{12,20},{13,21},{14,22},{15,23}} | collective-permute-start | bytes 786440 | tf_op jit(solution)/shard_map/ppermute | solution.py:564
  11.3 7.5 %copy-start = (bf16[1,128,4096]{2,1,0:T(8,128)(2,1)S(1)}, bf16[1,128,4096]{2,1,0:T(8,128)(2,1)}, u32[]{:S(2)}) copy-start(bf16[1,128,4096]{2,1,0:T(8,128)(2,1)} %query_ref.3) | copy-start | bytes 3145732
  11.3 7.5 %copy-start.1 = (bf16[1,128,4096]{2,1,0:T(8,128)(2,1)S(1)}, bf16[1,128,4096]{2,1,0:T(8,128)(2,1)}, u32[]{:S(2)}) copy-start(bf16[1,128,4096]{2,1,0:T(8,128)(2,1)} %grad_ref.3) | copy-start | bytes 3145732
  17.4 2.9 %collective-permute-start.6 = (bf16[32,4096]{1,0:T(8,128)(2,1)S(1)}, bf16[32,4096]{1,0:T(8,128)(2,1)S(1)}, u32[]{:S(2)}, u32[]{:S(2)}) collective-permute-start(bf16[32,4096]{1,0:T(8,128)(2,1)S(1)} %shard_map.112.refs_0_), channel_id=1, source_target_pairs={{20,28},{21,29},{22,30},{23,31},{8,24},{9,25},{10,26},{11,27}} | collective-permute-start | bytes 786440 | tf_op jit(solution)/shard_map/ppermute | solution.py:564
  18.1 2.2 %collective-permute-start.5 = (bf16[32,4096]{1,0:T(8,128)(2,1)S(1)}, bf16[32,4096]{1,0:T(8,128)(2,1)S(1)}, u32[]{:S(2)}, u32[]{:S(2)}) collective-permute-start(bf16[32,4096]{1,0:T(8,128)(2,1)S(1)} %shard_map.112.refs_0_), channel_id=1, source_target_pairs={{20,16},{21,17},{22,18},{23,19}} | collective-permute-start | bytes 786440 | tf_op jit(solution)/shard_map/ppermute | solution.py:564
  19.0 3.6 %collective-permute-start.2 = (bf16[1,2,128,1024]{3,2,1,0:T(8,128)(2,1)S(1)}, bf16[1,2,128,1024]{3,2,1,0:T(8,128)(2,1)S(1)}, u32[]{:S(2)}, u32[]{:S(2)}) collective-permute-start(bf16[1,2,128,1024]{3,2,1,0:T(8,128)(2,1)S(1)} %get-tuple-element.42), channel_id=1, source_target_pairs={{16,17},{17,16},{18,19},{19,18},{20,21},{21,20},{22,23},{23,22},{2... | collective-permute-start | bytes 1572872 | tf_op jit(solution)/shard_map/ppermute | solution.py:560
  20.4 2.1 %collective-permute-start.8 = (bf16[32,4224]{1,0:T(8,128)(2,1)S(1)}, bf16[32,4224]{1,0:T(8,128)(2,1)S(1)}, u32[]{:S(2)}, u32[]{:S(2)}) collective-permute-start(bf16[32,4224]{1,0:T(8,128)(2,1)S(1)} %shard_map.114.refs_3_), channel_id=1, source_target_pairs={{16,18},{17,19},{18,16},{19,17},{20,22},{21,23},{22,20},{23,21},{2... | collective-permute-start | bytes 811016 | tf_op jit(solution)/shard_map/ppermute | solution.py:560
  21.1 1.5 %collective-permute-start.7 = (bf16[32,4224]{1,0:T(8,128)(2,1)S(1)}, bf16[32,4224]{1,0:T(8,128)(2,1)S(1)}, u32[]{:S(2)}, u32[]{:S(2)}) collective-permute-start(bf16[32,4224]{1,0:T(8,128)(2,1)S(1)} %shard_map.114.refs_3_), channel_id=1, source_target_pairs={{16,17},{17,16},{18,19},{19,18},{20,21},{21,20},{22,23},{23,22},{2... | collective-permute-start | bytes 811016 | tf_op jit(solution)/shard_map/ppermute | solution.py:560
  21.8 1.5 %collective-permute-start.4 = (bf16[1,2,128,1024]{3,2,1,0:T(8,128)(2,1)S(1)}, bf16[1,2,128,1024]{3,2,1,0:T(8,128)(2,1)S(1)}, u32[]{:S(2)}, u32[]{:S(2)}) collective-permute-start(bf16[1,2,128,1024]{3,2,1,0:T(8,128)(2,1)S(1)} %slice.4), channel_id=1, source_target_pairs={{16,17},{17,16},{18,19},{19,18},{20,21},{21,20},{22,23},{23,22},{2... | collective-permute-start | bytes 1572872 | tf_op jit(solution)/shard_map/ppermute | solution.py:560
  22.6 0.7 collective-permute-start.9
  31.6 2.2 %collective-permute-start.10 = (bf16[64,4352]{1,0:T(8,128)(2,1)S(1)}, bf16[64,4352]{1,0:T(8,128)(2,1)S(1)}, u32[]{:S(2)}, u32[]{:S(2)}) collective-permute-start(bf16[64,4352]{1,0:T(8,128)(2,1)S(1)} %get-tuple-element.53), channel_id=1, source_target_pairs={{16,17},{17,16},{18,19},{19,18},{20,21},{21,20},{22,23},{23,22},{2... | collective-permute-start | bytes 1671176 | tf_op jit(solution)/shard_map/ppermute | solution.py:560
  33.9 7.6 %collective-permute-start.11 = (bf16[32,4352]{1,0:T(8,128)(2,1)S(1)}, bf16[32,4352]{1,0:T(8,128)(2,1)S(1)}, u32[]{:S(2)}, u32[]{:S(2)}) collective-permute-start(bf16[32,4352]{1,0:T(8,128)(2,1)S(1)} %get-tuple-element.58), channel_id=1, source_target_pairs={{16,18},{17,19},{18,16},{19,17},{20,22},{21,23},{22,20},{23,21},{2... | collective-permute-start | bytes 835592 | tf_op jit(solution)/shard_map/ppermute | solution.py:560
  41.6 5.6 %collective-permute-start.14 = (bf16[32,4096]{1,0:T(8,128)(2,1)S(1)}, bf16[32,4096]{1,0:T(8,128)(2,1)S(1)}, u32[]{:S(2)}, u32[]{:S(2)}) collective-permute-start(bf16[32,4096]{1,0:T(8,128)(2,1)S(1)} %get-tuple-element.63.own_ref), channel_id=1, source_target_pairs={{28,20},{29,21},{30,22},{31,23},{24,8},{25,9},{26,10},{27,11}} | collective-permute-start | bytes 786440 | tf_op jit(solution)/shard_map/ppermute | solution.py:564
  42.2 4.9 %collective-permute-start.13 = (bf16[32,4096]{1,0:T(8,128)(2,1)S(1)}, bf16[32,4096]{1,0:T(8,128)(2,1)S(1)}, u32[]{:S(2)}, u32[]{:S(2)}) collective-permute-start(bf16[32,4096]{1,0:T(8,128)(2,1)S(1)} %get-tuple-element.63.own_ref), channel_id=1, source_target_pairs={{16,20},{17,21},{18,22},{19,23}} | collective-permute-start | bytes 786440 | tf_op jit(solution)/shard_map/ppermute | solution.py:564
  42.9 42.0 %all-to-all-start = ((bf16[4,128,1024]{2,1,0:T(8,128)(2,1)}), bf16[4,128,1024]{2,1,0:T(8,128)(2,1)S(1)}, u32[]{:S(2)}, u32[]{:S(2)}) async-start(bf16[4,128,1024]{2,1,0:T(8,128)(2,1)} %shard_map.126), calls=%async_computation | async-start | bytes 2097152 | tf_op jit(solution)/shard_map/all_to_all | solution.py:641
  46.5 3.5 %collective-permute-start.12 = (f32[32,128]{1,0:T(8,128)S(1)}, f32[32,128]{1,0:T(8,128)S(1)}, u32[]{:S(2)}, u32[]{:S(2)}) collective-permute-start(f32[32,128]{1,0:T(8,128)S(1)} %get-tuple-element.62.own_ref.refs_1_), channel_id=1, source_target_pairs={{16,20},{17,21},{18,22},{19,23},{20,16},{21,17},{22,18},{23,19},{2... | collective-permute-start | bytes 49160 | tf_op jit(solution)/shard_map/ppermute | solution.py:564
  47.3 36.5 %copy-start.2 = (bf16[1,32,4096]{2,1,0:T(8,128)(2,1)S(1)}, bf16[1,32,4096]{2,1,0:T(8,128)(2,1)}, u32[]{:S(2)}) copy-start(bf16[1,32,4096]{2,1,0:T(8,128)(2,1)} %enc_ref.3) | copy-start | bytes 786436
  47.3 36.5 %collective-permute-start.19 = (bf16[32,4096]{1,0:T(8,128)(2,1)S(1)}, bf16[32,4096]{1,0:T(8,128)(2,1)S(1)}, u32[]{:S(2)}, u32[]{:S(2)}) collective-permute-start(bf16[32,4096]{1,0:T(8,128)(2,1)S(1)} %get-tuple-element.66), channel_id=1, source_target_pairs={{20,12},{21,13},{22,14},{23,15}} | collective-permute-start | bytes 786440 | tf_op jit(solution)/shard_map/ppermute | solution.py:564
  48.7 35.1 %collective-permute-start.18 = (bf16[32,4096]{1,0:T(8,128)(2,1)S(1)}, bf16[32,4096]{1,0:T(8,128)(2,1)S(1)}, u32[]{:S(2)}, u32[]{:S(2)}) collective-permute-start(bf16[32,4096]{1,0:T(8,128)(2,1)S(1)} %get-tuple-element.66), channel_id=1, source_target_pairs={{8,12},{9,13},{10,14},{11,15}} | collective-permute-start | bytes 786440 | tf_op jit(solution)/shard_map/ppermute | solution.py:564
  50.0 34.8 %collective-permute-start.17 = (f32[32,128]{1,0:T(8,128)S(1)}, f32[32,128]{1,0:T(8,128)S(1)}, u32[]{:S(2)}, u32[]{:S(2)}) collective-permute-start(f32[32,128]{1,0:T(8,128)S(1)} %shard_map.125.own_ref), channel_id=1, source_target_pairs={{16,4},{17,5},{18,6},{19,7},{20,12},{21,13},{22,14},{23,15},{24,0}... | collective-permute-start | bytes 49160 | tf_op jit(solution)/shard_map/ppermute | solution.py:564
  51.3 33.5 %collective-permute-start.16 = (f32[32,128]{1,0:T(8,128)S(1)}, f32[32,128]{1,0:T(8,128)S(1)}, u32[]{:S(2)}, u32[]{:S(2)}) collective-permute-start(f32[32,128]{1,0:T(8,128)S(1)} %shard_map.125.own_ref), channel_id=1, source_target_pairs={{16,0},{17,1},{18,2},{19,3},{20,8},{21,9},{22,10},{23,11},{24,4},{... | collective-permute-start | bytes 49160 | tf_op jit(solution)/shard_map/ppermute | solution.py:564
  52.6 32.2 %collective-permute-start.15 = (f32[32,128]{1,0:T(8,128)S(1)}, f32[32,128]{1,0:T(8,128)S(1)}, u32[]{:S(2)}, u32[]{:S(2)}) collective-permute-start(f32[32,128]{1,0:T(8,128)S(1)} %shard_map.125.own_ref), channel_id=1, source_target_pairs={{16,24},{17,25},{18,26},{19,27},{20,28},{21,29},{22,30},{23,31},{2... | collective-permute-start | bytes 49160 | tf_op jit(solution)/shard_map/ppermute | solution.py:564
  (2 other events, 4.3 us)

commit v8 on v7

--- a/solution.py
+++ b/solution.py
@@ -571,8 +571,8 @@
     memory, far, begun = begin(enc_state, gain, queries, ctx_grad, replicas)
     came_far = over_dp(far, replicas // 2)
     groups = [[k for k in range(1 << bit, 2 << bit)] for bit in reversed(range(bits - 1))]
-    came = [over_section(memory, group) for group in split_pairs(rounds[0])]
-    arrived = [came[0]]
+    came = [over_section(memory, group) for group in reversed(split_pairs(rounds[0]))]
+    arrived = [came[-1]]
     weights, held = hold_weights(w_key, w_value, [begun])
     holding = add_blocks(came, [held])
     near, split = split_heads(queries, ctx_grad, [*groups, [0]], replicas, [holding])

time: 87 us -> 87 us (level)
  no operation moved by 1% of the time
where the time goes in v8:
time: 87 us; the launch traced here: 85.9 us
  waiting for transfers between devices  29.9 us (34%)
  Pallas kernels  27.7 us (32%)
  starting transfers between devices  25.9 us (30%)
  between operations  1.71 us (2%)
    ppermute x12, waiting for transfers between devices, over_section(): return lax.ppermute(block, BOTH, pairs)  29.9 us
    ppermute x12, starting transfers between devices, over_section(): return lax.ppermute(block, BOTH, pairs)  16.8 us
    pallas_call x1, Pallas kernels, weight_grads(): call(kernel, [shape((1, width, columns))] * 2 + [TOKEN], flops=4 * rows *...  6.88 us
    pallas_call x1, Pallas kernels, hold_weights(): call(kernel, [shape(w_key.shape)] * 2 + [TOKEN], flops=COST_HOLD, moved=4...  6.06 us
    ppermute x8, starting transfers between devices, over_dp(): return lax.ppermute(block, BOTH, pairs)  5.52 us
    pallas_call x1, Pallas kernels, memory_part(): call(kernel, [shape((keep, depth), jnp.float32), shape((keep, depth + 2 *...  4.66 us
    all_to_all x1, starting transfers between devices, on_device(): dq = lax.all_to_all(dq, 'dp', split_axis=0, concat_axis=0, tiled=True)  3.53 us
    pallas_call x1, Pallas kernels, project(): call(kernel, [shape((rows, width))] * 2, flops=4 * rows * depth * width,...  2.47 us
  transfers between devices with their start and end apart: 21, of which 1 were waited for; matrix products, arithmetic and copies ran while one was open for 0% of the time, Pallas kernels for 18%

profile of v8, /device:TPU:12, one launch (start us, length us, event | category | flops | bytes accessed | tf_op | source)
XLA Modules:
  0.0 85.9 jit_solution(15776628808836267914)
XLA Ops:
  0.6 2.4 %shard_map.110 = (bf16[32,4096]{1,0:T(8,128)(2,1)}, bf16[2,2,128,1024]{3,2,1,0:T(8,128)(2,1)}, f32[8,128]{1,0:T(8,128)}) custom-call(bf16[1,32,4096]{2,1,0:T(8,128)(2,1)} %enc_ref.3, f32[1,4096]{1,0:T(1,128)} %bitcast.2, bf16[1,128,4096]{2,1,0:T(8,128)(2,1)} %query_ref.3, bf16[1,128,4096]{2,1,0:T(8,128)(2,1)} %grad_ref.3), custom_call_target="tpu_custom_call" | custom-call | bytes 2621440 | tf_op jit(solution)/shard_map/pallas_call | solution.py:119
  3.0 0.7 collective-permute-start.3
  3.8 6.2 %collective-permute-start.1 = (bf16[32,4096]{1,0:T(8,128)(2,1)}, bf16[32,4096]{1,0:T(8,128)(2,1)S(1)}, u32[]{:S(2)}, u32[]{:S(2)}) collective-permute-start(bf16[32,4096]{1,0:T(8,128)(2,1)} %get-tuple-element.39), channel_id=1, source_target_pairs={{12,20},{13,21},{14,22},{15,23}} | collective-permute-start | bytes 786440 | tf_op jit(solution)/shard_map/ppermute | solution.py:564
  9.9 1.3 %collective-permute-start = (bf16[32,4096]{1,0:T(8,128)(2,1)}, bf16[32,4096]{1,0:T(8,128)(2,1)S(1)}, u32[]{:S(2)}, u32[]{:S(2)}) collective-permute-start(bf16[32,4096]{1,0:T(8,128)(2,1)} %get-tuple-element.39), channel_id=1, source_target_pairs={{12,8},{13,9},{14,10},{15,11}} | collective-permute-start | bytes 786440 | tf_op jit(solution)/shard_map/ppermute | solution.py:564
  11.3 0.7 copy-done.4
  11.9 6.1 %shard_map.111 = (bf16[1,4096,1024]{2,1,0:T(8,128)(2,1)S(1)}, bf16[1,4096,1024]{2,1,0:T(8,128)(2,1)S(1)}, f32[8,128]{1,0:T(8,128)S(1)}) custom-call(bf16[1,4096,1024]{2,1,0:T(8,128)(2,1)} %wk_ref.1, bf16[1,4096,1024]{2,1,0:T(8,128)(2,1)} %wv_ref.1, f32[8,128]{1,0:T(8,128)S(1)} %copy-done.4), custom_call_target="tpu_custom_call" | custom-call | flops 1073741824 | bytes 16777216 | tf_op jit(solution)/shard_map/pallas_call | solution.py:225
  19.6 0.7 collective-permute-start.2
  21.0 0.7 collective-permute-start.8
  22.5 0.7 collective-permute-start.4
  24.0 2.5 %shard_map.117 = (bf16[128,1024]{1,0:T(8,128)(2,1)S(1)}, bf16[128,1024]{1,0:T(8,128)(2,1)S(1)}) custom-call(bf16[128,4224]{1,0:T(8,128)(2,1)S(1)} %shard_map.116.memory_ref, bf16[1,4096,1024]{2,1,0:T(8,128)(2,1)S(1)} %get-tuple-element.45.wk_ref, bf16[1,4096,1024]{2,1,0:T(8,128)(2,1)S(1)} %get-tuple-element.46.wv_ref), custom_call_target="tpu_custom_call" | custom-call | flops 2147483648 | bytes 16777216 | tf_op jit(solution)/shard_map/pallas_call | solution.py:246
  26.5 1.1 %shard_map.118 = (bf16[128,1024]{1,0:T(8,128)(2,1)S(1)}, bf16[128,1024]{1,0:T(8,128)(2,1)S(1)}, bf16[2,16,32,128]{3,2,1,0:T(8,128)(2,1)S(1)}) custom-call(bf16[128,4224]{1,0:T(8,128)(2,1)S(1)} %shard_map.116.memory_ref, bf16[128,1024]{1,0:T(8,128)(2,1)S(1)} %get-tuple-element.47.key_ref, bf16[128,1024]{1,0:T(8,128)(2,1)S(1)} %get-tuple-element.48.value_ref, ...), custom_call_target="tpu_custom_call" | custom-call | flops 134217728 | bytes 4194304 | tf_op jit(solution)/shard_map/pallas_call | solution.py:296
  27.6 4.7 %shard_map.119 = (f32[64,4096]{1,0:T(8,128)S(1)}, bf16[64,4352]{1,0:T(8,128)(2,1)S(1)}, f32[32,128]{1,0:T(8,128)S(1)}) custom-call(bf16[128,4224]{1,0:T(8,128)(2,1)S(1)} %shard_map.116.memory_ref, bf16[128,1024]{1,0:T(8,128)(2,1)S(1)} %get-tuple-element.50.dk_ref, bf16[128,1024]{1,0:T(8,128)(2,1)S(1)} %get-tuple-element.51.dv_ref, ...), custom_call_target="tpu_custom_call" | custom-call | flops 2147483648 | bytes 16777216 | tf_op jit(solution)/shard_map/pallas_call | solution.py:370
  32.3 0.7 collective-permute-start.10
  33.0 1.5 %shard_map.120 = (bf16[4,128,1024]{2,1,0:T(8,128)(2,1)}, f32[8,128]{1,0:T(8,128)S(1)}) custom-call(bf16[2,16,32,128]{3,2,1,0:T(8,128)(2,1)S(1)} %get-tuple-element.55.score_ref, bf16[128,1024]{1,0:T(8,128)(2,1)S(1)} %get-tuple-element.47.key_ref, f32[32,128]{1,0:T(8,128)S(1)} %get-tuple-element.54.refs_0_.gain_ref), custom_call_target="tpu_custom_call" | custom-call | flops 33554432 | bytes 2097152 | tf_op jit(solution)/shard_map/pallas_call | solution.py:326
  34.6 0.7 collective-permute-start.11
  35.3 6.9 %shard_map.122 = (bf16[1,4096,1024]{2,1,0:T(8,128)(2,1)}, bf16[1,4096,1024]{2,1,0:T(8,128)(2,1)}, f32[8,128]{1,0:T(8,128)S(1)}) custom-call(bf16[128,4224]{1,0:T(8,128)(2,1)S(1)} %shard_map.116.memory_ref, bf16[128,1024]{1,0:T(8,128)(2,1)S(1)} %get-tuple-element.50.dk_ref, bf16[128,1024]{1,0:T(8,128)(2,1)S(1)} %get-tuple-element.51.dv_ref, ...), custom_call_target="tpu_custom_call" | custom-call | flops 2147483648 | bytes 16777216 | tf_op jit(solution)/shard_map/pallas_call | solution.py:508
  43.6 3.5 %all-to-all-start = ((bf16[4,128,1024]{2,1,0:T(8,128)(2,1)}), bf16[4,128,1024]{2,1,0:T(8,128)(2,1)S(1)}, u32[]{:S(2)}, u32[]{:S(2)}) async-start(bf16[4,128,1024]{2,1,0:T(8,128)(2,1)} %shard_map.126), calls=%async_computation | async-start | bytes 2097152 | tf_op jit(solution)/shard_map/all_to_all | solution.py:641
  47.9 1.4 %collective-permute-start.19 = (bf16[32,4096]{1,0:T(8,128)(2,1)S(1)}, bf16[32,4096]{1,0:T(8,128)(2,1)S(1)}, u32[]{:S(2)}, u32[]{:S(2)}) collective-permute-start(bf16[32,4096]{1,0:T(8,128)(2,1)S(1)} %get-tuple-element.66), channel_id=1, source_target_pairs={{20,12},{21,13},{22,14},{23,15}} | collective-permute-start | bytes 786440 | tf_op jit(solution)/shard_map/ppermute | solution.py:564
  49.4 1.3 %collective-permute-start.18 = (bf16[32,4096]{1,0:T(8,128)(2,1)S(1)}, bf16[32,4096]{1,0:T(8,128)(2,1)S(1)}, u32[]{:S(2)}, u32[]{:S(2)}) collective-permute-start(bf16[32,4096]{1,0:T(8,128)(2,1)S(1)} %get-tuple-element.66), channel_id=1, source_target_pairs={{8,12},{9,13},{10,14},{11,15}} | collective-permute-start | bytes 786440 | tf_op jit(solution)/shard_map/ppermute | solution.py:564
  50.7 1.3 %collective-permute-start.17 = (f32[32,128]{1,0:T(8,128)S(1)}, f32[32,128]{1,0:T(8,128)S(1)}, u32[]{:S(2)}, u32[]{:S(2)}) collective-permute-start(f32[32,128]{1,0:T(8,128)S(1)} %shard_map.125.own_ref), channel_id=1, source_target_pairs={{16,4},{17,5},{18,6},{19,7},{20,12},{21,13},{22,14},{23,15},{24,0}... | collective-permute-start | bytes 49160 | tf_op jit(solution)/shard_map/ppermute | solution.py:564
  52.0 1.3 %collective-permute-start.16 = (f32[32,128]{1,0:T(8,128)S(1)}, f32[32,128]{1,0:T(8,128)S(1)}, u32[]{:S(2)}, u32[]{:S(2)}) collective-permute-start(f32[32,128]{1,0:T(8,128)S(1)} %shard_map.125.own_ref), channel_id=1, source_target_pairs={{16,0},{17,1},{18,2},{19,3},{20,8},{21,9},{22,10},{23,11},{24,4},{... | collective-permute-start | bytes 49160 | tf_op jit(solution)/shard_map/ppermute | solution.py:564
  54.0 29.9 %collective-permute-done.19.refs_1_ = bf16[32,4096]{1,0:T(8,128)(2,1)S(1)} collective-permute-done((bf16[32,4096]{1,0:T(8,128)(2,1)S(1)}, bf16[32,4096]{1,0:T(8,128)(2,1)S(1)}, u32[]{:S(2)}, u32[]{:S(2)}) %collective-permute-start.19) | collective-permute-done | bytes 262176 | tf_op jit(solution)/shard_map/ppermute | solution.py:564
  83.8 1.1 %shard_map.127 = (bf16[1,32,4096]{2,1,0:T(8,128)(2,1)}, f32[8,128]{1,0:T(8,128)S(1)}) custom-call(bf16[1,32,4096]{2,1,0:T(8,128)(2,1)S(1)} %copy-done.2, f32[1,4096]{1,0:T(1,128)S(1)} %bitcast.4, bf16[32,4096]{1,0:T(8,128)(2,1)S(1)} %collective-permute-done.18.refs_0_, bf16[32,4096]{1,0:T(8,128)(2,1)S(1)} %collective-permute-done.19.refs_1_), custom_call_target="tpu_custom_call" | custom-call | bytes 1048576 | tf_op jit(solution)/shard_map/pallas_call | solution.py:537
  84.9 1.0 %shard_map.128 = (f32[32,128]{1,0:T(8,128)}, bf16[1,128,4096]{2,1,0:T(8,128)(2,1)}) custom-call(f32[32,128]{1,0:T(8,128)S(1)} %shard_map.125.own_ref, f32[32,128]{1,0:T(8,128)S(1)} %collective-permute-done.15.other_ref, f32[32,128]{1,0:T(8,128)S(1)} %collective-permute-done.16.first_ref, f32[32,128]{1,0:T(8,128)S(1)} %collective-permute-done.17.second_ref, ...), custom_call_target="tpu_custom_call" | custom-call | bytes 2097152 | tf_op jit(solution)/shard_map/pallas_call | solution.py:480
  (48 shorter events, 6.1 us)
Async XLA Ops:
  3.0 19.4 %collective-permute-start.3 = (bf16[2,2,128,1024]{3,2,1,0:T(8,128)(2,1)}, bf16[2,2,128,1024]{3,2,1,0:T(8,128)(2,1)S(1)}, u32[]{:S(2)}, u32[]{:S(2)}) collective-permute-start(bf16[2,2,128,1024]{3,2,1,0:T(8,128)(2,1)} %get-tuple-element.43), channel_id=1, source_target_pairs={{16,18},{17,19},{18,16},{19,17},{20,22},{21,23},{22,20},{23,21},{2... | collective-permute-start | bytes 3145736 | tf_op jit(solution)/shard_map/ppermute | solution.py:560
  3.8 14.3 %collective-permute-start.1 = (bf16[32,4096]{1,0:T(8,128)(2,1)}, bf16[32,4096]{1,0:T(8,128)(2,1)S(1)}, u32[]{:S(2)}, u32[]{:S(2)}) collective-permute-start(bf16[32,4096]{1,0:T(8,128)(2,1)} %get-tuple-element.39), channel_id=1, source_target_pairs={{12,20},{13,21},{14,22},{15,23}} | collective-permute-start | bytes 786440 | tf_op jit(solution)/shard_map/ppermute | solution.py:564
  9.9 8.1 %collective-permute-start = (bf16[32,4096]{1,0:T(8,128)(2,1)}, bf16[32,4096]{1,0:T(8,128)(2,1)S(1)}, u32[]{:S(2)}, u32[]{:S(2)}) collective-permute-start(bf16[32,4096]{1,0:T(8,128)(2,1)} %get-tuple-element.39), channel_id=1, source_target_pairs={{12,8},{13,9},{14,10},{15,11}} | collective-permute-start | bytes 786440 | tf_op jit(solution)/shard_map/ppermute | solution.py:564
  11.9 7.5 %copy-start = (bf16[1,128,4096]{2,1,0:T(8,128)(2,1)S(1)}, bf16[1,128,4096]{2,1,0:T(8,128)(2,1)}, u32[]{:S(2)}) copy-start(bf16[1,128,4096]{2,1,0:T(8,128)(2,1)} %query_ref.3) | copy-start | bytes 3145732
  11.9 7.5 %copy-start.1 = (bf16[1,128,4096]{2,1,0:T(8,128)(2,1)S(1)}, bf16[1,128,4096]{2,1,0:T(8,128)(2,1)}, u32[]{:S(2)}) copy-start(bf16[1,128,4096]{2,1,0:T(8,128)(2,1)} %grad_ref.3) | copy-start | bytes 3145732
  18.1 2.9 %collective-permute-start.6 = (bf16[32,4096]{1,0:T(8,128)(2,1)S(1)}, bf16[32,4096]{1,0:T(8,128)(2,1)S(1)}, u32[]{:S(2)}, u32[]{:S(2)}) collective-permute-start(bf16[32,4096]{1,0:T(8,128)(2,1)S(1)} %shard_map.112.refs_0_), channel_id=1, source_target_pairs={{20,28},{21,29},{22,30},{23,31},{8,24},{9,25},{10,26},{11,27}} | collective-permute-start | bytes 786440 | tf_op jit(solution)/shard_map/ppermute | solution.py:564
  18.8 2.2 %collective-permute-start.5 = (bf16[32,4096]{1,0:T(8,128)(2,1)S(1)}, bf16[32,4096]{1,0:T(8,128)(2,1)S(1)}, u32[]{:S(2)}, u32[]{:S(2)}) collective-permute-start(bf16[32,4096]{1,0:T(8,128)(2,1)S(1)} %shard_map.112.refs_0_), channel_id=1, source_target_pairs={{20,16},{21,17},{22,18},{23,19}} | collective-permute-start | bytes 786440 | tf_op jit(solution)/shard_map/ppermute | solution.py:564
  19.6 3.6 %collective-permute-start.2 = (bf16[1,2,128,1024]{3,2,1,0:T(8,128)(2,1)S(1)}, bf16[1,2,128,1024]{3,2,1,0:T(8,128)(2,1)S(1)}, u32[]{:S(2)}, u32[]{:S(2)}) collective-permute-start(bf16[1,2,128,1024]{3,2,1,0:T(8,128)(2,1)S(1)} %get-tuple-element.42), channel_id=1, source_target_pairs={{16,17},{17,16},{18,19},{19,18},{20,21},{21,20},{22,23},{23,22},{2... | collective-permute-start | bytes 1572872 | tf_op jit(solution)/shard_map/ppermute | solution.py:560
  21.0 2.1 %collective-permute-start.8 = (bf16[32,4224]{1,0:T(8,128)(2,1)S(1)}, bf16[32,4224]{1,0:T(8,128)(2,1)S(1)}, u32[]{:S(2)}, u32[]{:S(2)}) collective-permute-start(bf16[32,4224]{1,0:T(8,128)(2,1)S(1)} %shard_map.114.refs_3_), channel_id=1, source_target_pairs={{16,18},{17,19},{18,16},{19,17},{20,22},{21,23},{22,20},{23,21},{2... | collective-permute-start | bytes 811016 | tf_op jit(solution)/shard_map/ppermute | solution.py:560
  21.7 1.5 %collective-permute-start.7 = (bf16[32,4224]{1,0:T(8,128)(2,1)S(1)}, bf16[32,4224]{1,0:T(8,128)(2,1)S(1)}, u32[]{:S(2)}, u32[]{:S(2)}) collective-permute-start(bf16[32,4224]{1,0:T(8,128)(2,1)S(1)} %shard_map.114.refs_3_), channel_id=1, source_target_pairs={{16,17},{17,16},{18,19},{19,18},{20,21},{21,20},{22,23},{23,22},{2... | collective-permute-start | bytes 811016 | tf_op jit(solution)/shard_map/ppermute | solution.py:560
  22.5 1.5 %collective-permute-start.4 = (bf16[1,2,128,1024]{3,2,1,0:T(8,128)(2,1)S(1)}, bf16[1,2,128,1024]{3,2,1,0:T(8,128)(2,1)S(1)}, u32[]{:S(2)}, u32[]{:S(2)}) collective-permute-start(bf16[1,2,128,1024]{3,2,1,0:T(8,128)(2,1)S(1)} %slice.4), channel_id=1, source_target_pairs={{16,17},{17,16},{18,19},{19,18},{20,21},{21,20},{22,23},{23,22},{2... | collective-permute-start | bytes 1572872 | tf_op jit(solution)/shard_map/ppermute | solution.py:560
  23.2 0.7 collective-permute-start.9
  32.3 2.2 %collective-permute-start.10 = (bf16[64,4352]{1,0:T(8,128)(2,1)S(1)}, bf16[64,4352]{1,0:T(8,128)(2,1)S(1)}, u32[]{:S(2)}, u32[]{:S(2)}) collective-permute-start(bf16[64,4352]{1,0:T(8,128)(2,1)S(1)} %get-tuple-element.53), channel_id=1, source_target_pairs={{16,17},{17,16},{18,19},{19,18},{20,21},{21,20},{22,23},{23,22},{2... | collective-permute-start | bytes 1671176 | tf_op jit(solution)/shard_map/ppermute | solution.py:560
  34.6 7.6 %collective-permute-start.11 = (bf16[32,4352]{1,0:T(8,128)(2,1)S(1)}, bf16[32,4352]{1,0:T(8,128)(2,1)S(1)}, u32[]{:S(2)}, u32[]{:S(2)}) collective-permute-start(bf16[32,4352]{1,0:T(8,128)(2,1)S(1)} %get-tuple-element.58), channel_id=1, source_target_pairs={{16,18},{17,19},{18,16},{19,17},{20,22},{21,23},{22,20},{23,21},{2... | collective-permute-start | bytes 835592 | tf_op jit(solution)/shard_map/ppermute | solution.py:560
  42.2 5.6 %collective-permute-start.14 = (bf16[32,4096]{1,0:T(8,128)(2,1)S(1)}, bf16[32,4096]{1,0:T(8,128)(2,1)S(1)}, u32[]{:S(2)}, u32[]{:S(2)}) collective-permute-start(bf16[32,4096]{1,0:T(8,128)(2,1)S(1)} %get-tuple-element.63.own_ref), channel_id=1, source_target_pairs={{28,20},{29,21},{30,22},{31,23},{24,8},{25,9},{26,10},{27,11}} | collective-permute-start | bytes 786440 | tf_op jit(solution)/shard_map/ppermute | solution.py:564
  42.9 4.9 %collective-permute-start.13 = (bf16[32,4096]{1,0:T(8,128)(2,1)S(1)}, bf16[32,4096]{1,0:T(8,128)(2,1)S(1)}, u32[]{:S(2)}, u32[]{:S(2)}) collective-permute-start(bf16[32,4096]{1,0:T(8,128)(2,1)S(1)} %get-tuple-element.63.own_ref), channel_id=1, source_target_pairs={{16,20},{17,21},{18,22},{19,23}} | collective-permute-start | bytes 786440 | tf_op jit(solution)/shard_map/ppermute | solution.py:564
  43.6 41.3 %all-to-all-start = ((bf16[4,128,1024]{2,1,0:T(8,128)(2,1)}), bf16[4,128,1024]{2,1,0:T(8,128)(2,1)S(1)}, u32[]{:S(2)}, u32[]{:S(2)}) async-start(bf16[4,128,1024]{2,1,0:T(8,128)(2,1)} %shard_map.126), calls=%async_computation | async-start | bytes 2097152 | tf_op jit(solution)/shard_map/all_to_all | solution.py:641
  47.1 3.5 %collective-permute-start.12 = (f32[32,128]{1,0:T(8,128)S(1)}, f32[32,128]{1,0:T(8,128)S(1)}, u32[]{:S(2)}, u32[]{:S(2)}) collective-permute-start(f32[32,128]{1,0:T(8,128)S(1)} %get-tuple-element.62.own_ref.refs_1_), channel_id=1, source_target_pairs={{16,20},{17,21},{18,22},{19,23},{20,16},{21,17},{22,18},{23,19},{2... | collective-permute-start | bytes 49160 | tf_op jit(solution)/shard_map/ppermute | solution.py:564
  47.9 35.9 %copy-start.2 = (bf16[1,32,4096]{2,1,0:T(8,128)(2,1)S(1)}, bf16[1,32,4096]{2,1,0:T(8,128)(2,1)}, u32[]{:S(2)}) copy-start(bf16[1,32,4096]{2,1,0:T(8,128)(2,1)} %enc_ref.3) | copy-start | bytes 786436
  47.9 35.9 %collective-permute-start.19 = (bf16[32,4096]{1,0:T(8,128)(2,1)S(1)}, bf16[32,4096]{1,0:T(8,128)(2,1)S(1)}, u32[]{:S(2)}, u32[]{:S(2)}) collective-permute-start(bf16[32,4096]{1,0:T(8,128)(2,1)S(1)} %get-tuple-element.66), channel_id=1, source_target_pairs={{20,12},{21,13},{22,14},{23,15}} | collective-permute-start | bytes 786440 | tf_op jit(solution)/shard_map/ppermute | solution.py:564
  49.4 34.5 %collective-permute-start.18 = (bf16[32,4096]{1,0:T(8,128)(2,1)S(1)}, bf16[32,4096]{1,0:T(8,128)(2,1)S(1)}, u32[]{:S(2)}, u32[]{:S(2)}) collective-permute-start(bf16[32,4096]{1,0:T(8,128)(2,1)S(1)} %get-tuple-element.66), channel_id=1, source_target_pairs={{8,12},{9,13},{10,14},{11,15}} | collective-permute-start | bytes 786440 | tf_op jit(solution)/shard_map/ppermute | solution.py:564
  50.7 34.2 %collective-permute-start.17 = (f32[32,128]{1,0:T(8,128)S(1)}, f32[32,128]{1,0:T(8,128)S(1)}, u32[]{:S(2)}, u32[]{:S(2)}) collective-permute-start(f32[32,128]{1,0:T(8,128)S(1)} %shard_map.125.own_ref), channel_id=1, source_target_pairs={{16,4},{17,5},{18,6},{19,7},{20,12},{21,13},{22,14},{23,15},{24,0}... | collective-permute-start | bytes 49160 | tf_op jit(solution)/shard_map/ppermute | solution.py:564
  52.0 32.9 %collective-permute-start.16 = (f32[32,128]{1,0:T(8,128)S(1)}, f32[32,128]{1,0:T(8,128)S(1)}, u32[]{:S(2)}, u32[]{:S(2)}) collective-permute-start(f32[32,128]{1,0:T(8,128)S(1)} %shard_map.125.own_ref), channel_id=1, source_target_pairs={{16,0},{17,1},{18,2},{19,3},{20,8},{21,9},{22,10},{23,11},{24,4},{... | collective-permute-start | bytes 49160 | tf_op jit(solution)/shard_map/ppermute | solution.py:564
  53.3 31.6 %collective-permute-start.15 = (f32[32,128]{1,0:T(8,128)S(1)}, f32[32,128]{1,0:T(8,128)S(1)}, u32[]{:S(2)}, u32[]{:S(2)}) collective-permute-start(f32[32,128]{1,0:T(8,128)S(1)} %shard_map.125.own_ref), channel_id=1, source_target_pairs={{16,24},{17,25},{18,26},{19,27},{20,28},{21,29},{22,30},{23,31},{2... | collective-permute-start | bytes 49160 | tf_op jit(solution)/shard_map/ppermute | solution.py:564
  (2 other events, 4.3 us)
